TPU v7x, 128 devices: a whole 4x4x4 slice. The times are simulated.
128 devices in a mesh: dp: 8 (over y, z_hi), ctx: 16 (over x, z_lo, core).
Axes of the slice: x: 4, y: 4, z: 4 (z_hi: 2, z_lo: 2; z = z_hi * 2 + z_lo), core: 2. Of those that a mesh axis runs over, the one named last changes fastest.
Arguments:
- query_rows: bfloat16 [65536, 2048], P(('dp', 'ctx')), may hold values from -6 to 6
- key_rows: bfloat16 [65536, 2048], P(('dp', 'ctx')), may hold values from -6 to 6
- value_rows: bfloat16 [65536, 2048], P(('dp', 'ctx')), may hold values from -6 to 6
- pyramid_start: int32 [65536], P(('dp', 'ctx')), may hold values from 0 to 8191, as said below
- scale_end: int32 [65536], P(('dp', 'ctx')), may hold values from 1 to 8192, as said below
- out_weight: bfloat16 [2048, 2048], P('dp'), may hold values from -0.125 to 0.125
- cotangent: bfloat16 [65536, 2048], P(('dp', 'ctx')), may hold values from -6 to 6
Outputs:
- layer_out: bfloat16 [65536, 2048], P(('dp', 'ctx'))
- query_grad: bfloat16 [65536, 2048], P(('dp', 'ctx'))
- key_grad: bfloat16 [65536, 2048], P(('dp', 'ctx'))
- value_grad: bfloat16 [65536, 2048], P(('dp', 'ctx'))
- weight_grad: float32 [2048, 2048], P('dp')
Inputs may be any that keep to these rules, and one draw needn't show every extreme that they name: `pyramid_start`: each group's packed sequence of 8192 tokens is cut into pyramids laid end to end; a pyramid is the first 4 to 9 scales of lengths 1, 1, 4, 9, 16, 25, 36, 64, 100 (at most 256 tokens), a pyramid may be cut off at the group's end, the first pyramid of every group has 4 scales and the next 2 pyramids have all 9, and the group's last token always starts a pyramid of its own. Each token holds its pyramid's first position counted within its group. `scale_end`: each token holds one past the last position of its scale within its group, cut at 8191 for every token but the group's last; it is above the token's own position and at most 256 above its pyramid_start.
All inputs are finite; a program needn't handle non-finite values.
Results may differ from a plain program's by a relative error of at most 0.0072.
Values may be sent and summed in bfloat16 or wider, within the bound.
No kernel may reach another device: no remote copies, remote signals or barrier semaphores. Data moves between devices by JAX's collectives and lax.ppermute only.
A program may use at most 192 MiB of HBM per device.

v0:
```python
import jax
import jax.numpy as jnp
from jax import lax
from jax.sharding import PartitionSpec as P

HEADS = 16
HEAD_DIM = 128
PYR = 256


def with_halo(cells, sides, width):
    for axis, dim in sides:
        count = lax.axis_size(axis)
        ends = count - 1
        head = lax.slice_in_dim(cells, 0, width, axis=dim)
        tail = lax.slice_in_dim(cells, cells.shape[dim] - width, cells.shape[dim], axis=dim)
        cells = jnp.concatenate(
            [
                lax.ppermute(tail, axis, [(i, (i + 1) % count) for i in range(ends)]),
                cells,
                lax.ppermute(head, axis, [((i + 1) % count, i) for i in range(ends)]),
            ],
            axis=dim,
        )
    return cells


def passed_along(shard, axis, by):
    devices = lax.axis_size(axis)
    pairs = [(i, i + by) for i in range(devices) if 0 <= i + by < devices]
    return lax.ppermute(shard, axis, pairs)


def contract_rows(left, right):
    return lax.dot_general(
        left, right, (((0,), (0,)), ((), ())), preferred_element_type=jnp.float32
    )


def contract_cols(left, right):
    return lax.dot_general(
        left, right, (((1,), (1,)), ((), ())), preferred_element_type=jnp.float32
    )


def attend_heads(query_rows, key_wide, value_wide, grad_attn, allowed):
    factor = HEAD_DIM ** (-0.5)

    def one_head(head_index):
        start = head_index * HEAD_DIM
        query_head = lax.dynamic_slice_in_dim(query_rows, start, HEAD_DIM, 1)
        key_head = lax.dynamic_slice_in_dim(key_wide, start, HEAD_DIM, 1)
        value_head = lax.dynamic_slice_in_dim(value_wide, start, HEAD_DIM, 1)
        grad_head = lax.dynamic_slice_in_dim(grad_attn, start, HEAD_DIM, 1)
        scores = contract_cols(query_head, key_head) * factor
        scores = jnp.where(allowed, scores, -jnp.inf)
        top = jnp.max(scores, axis=1, keepdims=True)
        weights = jnp.exp(scores - top)
        probs = weights / jnp.sum(weights, axis=1, keepdims=True)
        probs_low = probs.astype(jnp.bfloat16)
        mixed = jnp.dot(probs_low, value_head, preferred_element_type=jnp.float32).astype(
            jnp.bfloat16
        )
        grad_values = contract_rows(probs_low, grad_head)
        grad_probs = contract_cols(grad_head, value_head)
        inner = jnp.sum(probs * grad_probs, axis=1, keepdims=True)
        grad_scores = (probs * (grad_probs - inner)).astype(jnp.bfloat16)
        grad_query = (
            jnp.dot(grad_scores, key_head, preferred_element_type=jnp.float32) * factor
        ).astype(jnp.bfloat16)
        grad_keys = contract_rows(grad_scores, query_head) * factor
        return (mixed, grad_query, jnp.concatenate([grad_keys, grad_values], axis=1))

    return lax.map(one_head, jnp.arange(HEADS, dtype=jnp.int32))


def heads_to_rows(stacked):
    return jnp.transpose(stacked, (1, 0, 2)).reshape(
        stacked.shape[1], stacked.shape[0] * stacked.shape[2]
    )


def on_device(query_rows, key_rows, value_rows, pyramid_start, scale_end, out_weight, cotangent):
    tok_rows = query_rows.shape[0]
    width = query_rows.shape[1]
    first_row = lax.axis_index("ctx") * tok_rows
    full_weight = lax.all_gather(out_weight, "dp", axis=0, tiled=True)
    grad_attn = contract_cols(cotangent, full_weight).astype(jnp.bfloat16)
    joined = jnp.concatenate([key_rows, value_rows], axis=1)
    wide = with_halo(joined, (("ctx", 0),), PYR)
    key_wide = wide[:, :width]
    value_wide = wide[:, width:]
    key_pos = first_row - PYR + jnp.arange(tok_rows + 2 * PYR, dtype=jnp.int32)
    allowed = (key_pos[None, :] >= pyramid_start[:, None]) & (key_pos[None, :] < scale_end[:, None])
    mixed, grad_query, grad_pairs = attend_heads(
        query_rows, key_wide, value_wide, grad_attn, allowed
    )
    attn = heads_to_rows(mixed)
    query_grad = heads_to_rows(grad_query)
    from_before = passed_along(
        grad_pairs[:, PYR + tok_rows :].astype(jnp.bfloat16), "ctx", 1
    ).astype(jnp.float32)
    from_after = passed_along(grad_pairs[:, :PYR], "ctx", -1)
    own_pairs = grad_pairs[:, PYR : PYR + tok_rows]
    own_pairs = own_pairs + jnp.pad(from_before, ((0, 0), (0, tok_rows - PYR), (0, 0)))
    own_pairs = own_pairs + jnp.pad(from_after, ((0, 0), (tok_rows - PYR, 0), (0, 0)))
    key_grad = heads_to_rows(own_pairs[:, :, :HEAD_DIM]).astype(jnp.bfloat16)
    value_grad = heads_to_rows(own_pairs[:, :, HEAD_DIM:]).astype(jnp.bfloat16)
    layer_out = jnp.dot(attn, full_weight, preferred_element_type=jnp.float32).astype(jnp.bfloat16)
    scaling = float(tok_rows * lax.axis_size("ctx") * lax.axis_size("dp")) ** (-0.5)
    full_term = contract_rows(attn, cotangent)
    partial_sum = lax.psum_scatter(full_term, "ctx", scatter_dimension=1, tiled=True)
    partial_sum = lax.psum_scatter(partial_sum, "dp", scatter_dimension=0, tiled=True)
    weight_grad = lax.all_gather(partial_sum, "ctx", axis=1, tiled=True) * scaling
    return (layer_out, query_grad, key_grad, value_grad, weight_grad)


def solution(mesh):
    placed = (
        P(("dp", "ctx"), None),
        P(("dp", "ctx"), None),
        P(("dp", "ctx"), None),
        P(("dp", "ctx")),
        P(("dp", "ctx")),
        P("dp", None),
        P(("dp", "ctx"), None),
    )
    return jax.shard_map(
        on_device,
        mesh=mesh,
        in_specs=placed,
        out_specs=(
            P(("dp", "ctx"), None),
            P(("dp", "ctx"), None),
            P(("dp", "ctx"), None),
            P(("dp", "ctx"), None),
            P("dp", None),
        ),
        check_vma=False,
    )
```

profile of v0, /device:TPU:1, one launch (start us, length us, event | category | flops | bytes accessed | tf_op | source)
XLA Modules:
  0.0 746.2 jit_solution(2221483677594102731)
XLA Ops:
  10.3 2.7 fusion.31
  13.6 4.9 collective-permute-start
  20.6 55.0 %collective-permute-done = bf16[256,4096]{1,0:T(8,128)(2,1)} collective-permute-done((bf16[256,4096]{1,0:T(8,128)(2,1)}, bf16[256,4096]{1,0:T(8,128)(2,1)}, u32[]{:S(2)}, u32[]{:S(2)}) %collective-permute-start) | collective-permute-done | bytes 2097184 | tf_op jit(solution)/shard_map/ppermute | solution.py:19
  75.6 4.3 pad_maximum_fusion
  79.8 4.1 fusion.29
  83.9 64.9 %all-gather.3.cloned.1.call-done = bf16[2048,2048]{1,0:T(8,128)(2,1)} async-done(((bf16[256,2048]{1,0:T(8,128)(2,1)}), bf16[2048,2048]{1,0:T(8,128)(2,1)}) %all-gather.3.cloned.1.call-update) | async-done | bytes 8388624 | tf_op jit(solution)/shard_map/all_gather | solution.py:87
  148.8 9.1 %convolution_convert_fusion.2 = bf16[512,2048]{1,0:T(8,128)(2,1)} fusion(bf16[512,2048]{1,0:T(8,128)(2,1)S(1)} %copy-done, bf16[2048,2048]{1,0:T(8,128)(2,1)} %all-gather.3.cloned.1.call-done), kind=kOutput, calls=%fused_computation.39 | convolution fusion | flops 4296015872 | bytes 12582912 | tf_op jit(solution)/shard_map/dot_general | solution.py:41
  157.9 225.9 %while.15 = (s32[]{:T(128)}, bf16[16,512,128]{1,2,0:T(8,128)(2,1)}, bf16[16,512,128]{2,1,0:T(8,128)(2,1)}, f32[16,1024,256]{1,2,0:T(8,128)}, s32[16]{0:T(128)S(1...) while((s32[]{:T(128)}, bf16[16,512,128]{1,2,0:T(8,128)(2,1)}, ...), condition=%wide.region_4.5_spmd.clone, body=%wide.region_0.4_spmd.clone.sunk | while | flops 814807552 | bytes 29647120 | solution.py:74
  207.1 2.1 fusion.68
  306.0 2.1 fusion.68
  383.8 9.8 %fusion.32 = f32[2048,2048]{1,0:T(8,128)} fusion(bf16[512,2048]{0,1:T(8,128)(2,1)} %bitcast.50, bf16[512,2048]{1,0:T(8,128)(2,1)S(1)} %copy-done), kind=kOutput, calls=%fused_computation.49 | convolution fusion | flops 4294967296 | bytes 20971520 | tf_op jit(solution)/shard_map/dot_general | solution.py:35
  393.7 179.1 %reduce-scatter.3.cloned.1.call-done = f32[2048,128]{1,0:T(8,128)} async-done(((f32[2048,2048]{1,0:T(8,128)}), f32[2048,128]{1,0:T(8,128)}) %reduce-scatter.3.cloned.1.call-update) | async-done | bytes 1048592 | tf_op jit(solution)/shard_map/reduce_scatter | solution.py:112
  572.8 4.6 slice.36
  579.3 103.3 %reduce-scatter.5.cloned.1.call-done = f32[256,128]{1,0:T(8,128)} async-done(((f32[2048,128]{1,0:T(8,128)}), f32[256,128]{1,0:T(8,128)}) %reduce-scatter.5.cloned.1.call-update) | async-done | bytes 131088 | tf_op jit(solution)/shard_map/reduce_scatter | solution.py:113
  682.7 2.6 slice.48
  685.3 5.1 collective-permute-start.2
  690.4 3.4 copy_bitcast_fusion
  693.8 9.3 %convolution_convert_fusion.1 = bf16[512,2048]{1,0:T(8,128)(2,1)} fusion(bf16[512,2048]{0,1:T(8,128)(2,1)S(1)} %bitcast.51, bf16[2048,2048]{1,0:T(8,128)(2,1)} %all-gather.3.cloned.1.call-done), kind=kOutput, calls=%fused_computation.38 | convolution fusion | flops 4296015872 | bytes 12582912 | tf_op jit(solution)/shard_map/dot_general | solution.py:109
  703.1 19.9 %collective-permute-done.2 = bf16[16,256,256]{1,2,0:T(8,128)(2,1)S(1)} collective-permute-done((bf16[16,256,256]{1,2,0:T(8,128)(2,1)S(1)}, bf16[16,256,256]{1,2,0:T(8,128)(2,1)S(1)}, u32[]{:S(2)}, u32[]{:S(2)}) %collective-permute-start.2) | collective-permute-done | bytes 2097184 | tf_op jit(solution)/shard_map/ppermute | solution.py:31
  723.1 3.3 add_convert_fusion
  726.4 2.3 fusion.30
  728.7 3.9 copy.20
  732.6 3.9 copy.19
  736.5 3.1 broadcast_multiply_fusion
  (263 shorter events, 218.3 us)
Async XLA Ops:
  7.2 141.7 %copy-start = (bf16[512,2048]{1,0:T(8,128)(2,1)S(1)}, bf16[512,2048]{1,0:T(8,128)(2,1)}, u32[]{:S(2)}) copy-start(bf16[512,2048]{1,0:T(8,128)(2,1)} %param.15) | copy-start | bytes 6291460
  7.2 141.6 %all-gather.3.cloned.1.call-start = ((), (), s32[]{:S(2)}) async-start(), calls=%async_computation.2 | async-start | bytes 9437184 | tf_op jit(solution)/shard_map/all_gather | solution.py:87
  7.9 564.8 %reduce-scatter.3.cloned.1.call-start = ((), (), s32[]{:S(2)}) async-start(), calls=%async_computation.3 | async-start | bytes 17825792 | tf_op jit(solution)/shard_map/reduce_scatter | solution.py:112
  13.6 61.9 %collective-permute-start = (bf16[256,4096]{1,0:T(8,128)(2,1)}, bf16[256,4096]{1,0:T(8,128)(2,1)}, u32[]{:S(2)}, u32[]{:S(2)}) collective-permute-start(bf16[256,4096]{1,0:T(8,128)(2,1)} %get-tuple-element.124), channel_id=1, source_target_pairs={{0,1},{1,2},{2,3},{3,4},{4,5},{5,6},{6,7},{7,8},{8,9},{9,10},{10,1... | collective-permute-start | bytes 6291464 | tf_op jit(solution)/shard_map/ppermute | solution.py:19
  18.6 57.0 %collective-permute-start.1 = (bf16[256,4096]{1,0:T(8,128)(2,1)}, bf16[256,4096]{1,0:T(8,128)(2,1)}, u32[]{:S(2)}, u32[]{:S(2)}) collective-permute-start(bf16[256,4096]{1,0:T(8,128)(2,1)} %get-tuple-element.125), channel_id=1, source_target_pairs={{1,0},{2,1},{3,2},{4,3},{5,4},{6,5},{7,6},{8,7},{9,8},{10,9},{11,1... | collective-permute-start | bytes 6291464 | tf_op jit(solution)/shard_map/ppermute | solution.py:21
  83.9 74.0 %copy-start.5 = (s32[512]{0:T(512)S(1)}, s32[512]{0:T(512)}, u32[]{:S(2)}) copy-start(s32[512]{0:T(512)} %param.12) | copy-start | bytes 6148
  83.9 74.0 %copy-start.6 = (s32[512]{0:T(512)S(1)}, s32[512]{0:T(512)}, u32[]{:S(2)}) copy-start(s32[512]{0:T(512)} %param.13) | copy-start | bytes 6148
  209.3 4.1 copy-start.1
  237.5 4.1 copy-start.1
  251.6 4.1 copy-start.1
  265.7 4.1 copy-start.1
  294.0 4.1 copy-start.1
  308.2 4.1 copy-start.1
  322.3 4.1 copy-start.1
  336.4 4.1 copy-start.1
  393.6 289.0 %reduce-scatter.5.cloned.1.call-start = ((), (), s32[]{:S(2)}) async-start(), calls=%async_computation.4 | async-start | bytes 1179648 | tf_op jit(solution)/shard_map/reduce_scatter | solution.py:113
  572.8 163.7 %all-gather.5.cloned.1.call-start = ((), (), s32[]{:S(2)}) async-start(), calls=%async_computation.5 | async-start | bytes 2228224 | tf_op jit(solution)/shard_map/all_gather | solution.py:114
  577.4 145.6 %collective-permute-start.3 = (f32[16,256,256]{1,2,0:T(8,128)}, f32[16,256,256]{1,2,0:T(8,128)}, u32[]{:S(2)}, u32[]{:S(2)}) collective-permute-start(f32[16,256,256]{1,2,0:T(8,128)} %slice.36), channel_id=1, source_target_pairs={{1,0},{2,1},{3,2},{4,3},{5,4},{6,5},{7,6},{8,7},{9,8},{10,9},{11,1... | collective-permute-start | bytes 12582920 | tf_op jit(solution)/shard_map/ppermute | solution.py:31
  682.7 11.1 %copy-start.4 = (bf16[16,512,128]{1,2,0:T(8,128)(2,1)S(1)}, bf16[16,512,128]{1,2,0:T(8,128)(2,1)}, u32[]{:S(2)}) copy-start(bf16[16,512,128]{1,2,0:T(8,128)(2,1)} %get-tuple-element.59) | copy-start | bytes 6291460
  682.7 40.3 %slice-start = ((s8[16777216]{0:T(1024)(128)(4,1)}), s8[4194304]{0:T(1024)(128)(4,1)S(1)}, s32[]{:S(2)}) async-start(s8[16777216]{0:T(1024)(128)(4,1)} %bitcast.46), calls=%async_computation.6 | async-start | bytes 8388608
  685.3 37.7 %collective-permute-start.2 = (bf16[16,256,256]{1,2,0:T(8,128)(2,1)S(1)}, bf16[16,256,256]{1,2,0:T(8,128)(2,1)S(1)}, u32[]{:S(2)}, u32[]{:S(2)}) collective-permute-start(bf16[16,256,256]{1,2,0:T(8,128)(2,1)S(1)} %slice.48), channel_id=1, source_target_pairs={{0,1},{1,2},{2,3},{3,4},{4,5},{5,6},{6,7},{7,8},{8,9},{9,10},{10,1... | collective-permute-start | bytes 6291464 | tf_op jit(solution)/shard_map/ppermute | solution.py:31
  690.4 32.6 %slice-start.1 = ((s8[16777216]{0:T(1024)(128)(4,1)}), s8[4194304]{0:T(1024)(128)(4,1)S(1)}, s32[]{:S(2)}) async-start(s8[16777216]{0:T(1024)(128)(4,1)} %bitcast.46), calls=%async_computation.7 | async-start | bytes 8388608
  693.8 29.2 %slice-start.2 = ((s8[16777216]{0:T(1024)(128)(4,1)}), s8[4194304]{0:T(1024)(128)(4,1)S(1)}, s32[]{:S(2)}) async-start(s8[16777216]{0:T(1024)(128)(4,1)} %bitcast.46), calls=%async_computation.8 | async-start | bytes 8388608
  693.8 29.2 %slice-start.3 = ((s8[16777216]{0:T(1024)(128)(4,1)}), s8[4194304]{0:T(1024)(128)(4,1)S(1)}, s32[]{:S(2)}) async-start(s8[16777216]{0:T(1024)(128)(4,1)} %bitcast.46), calls=%async_computation.9 | async-start | bytes 8388608
  (10 other events, 38.0 us)
Sparse Core Ops, SparseCore 0:
  10.4 138.4 all-gather.2
  393.8 178.9 reduce-scatter.2
  576.4 106.2 reduce-scatter.4
  684.2 40.7 all-gather.4
where the time goes:
time: 751 us; the launch traced here: 746 us
  waiting for transfers between devices  423 us (56%)
  matrix products  192 us (26%)
  local copies, waits for them, and re-layouts  52.3 us (7%)
  other arithmetic  40.1 us (5%)
  starting transfers between devices  14 us (2%)
  between operations  14 us (2%)
  loops' own time  11.2 us (1%)
    reduce_scatter x1, waiting for transfers between devices, on_device(): lax.psum_scatter(full_term, 'ctx', scatter_dimension=1, tiled=True)  179 us
    reduce_scatter x1, waiting for transfers between devices, on_device(): lax.psum_scatter(partial_sum, 'dp', scatter_dimension=0, tiled=True)  103 us
    all_gather x1, waiting for transfers between devices, on_device(): full_weight = lax.all_gather(out_weight, 'dp', axis=0, tiled=True)  64.9 us
    dot_general x33, matrix products, contract_rows(): lax.dot_general(left, right, (((0,), (0,)), ((), ())), preferred_element_...  63.9 us
    dot_general x33, matrix products, contract_cols(): lax.dot_general(left, right, (((1,), (1,)), ((), ())), preferred_element_...  63.3 us
    ppermute x1, waiting for transfers between devices, with_halo(): lax.ppermute(tail, axis, [(i, (i + 1) % count) for i in range(ends)])  55 us
    dot_general x16, matrix products, one_head(): jnp.dot(grad_scores, key_head, preferred_element_type=jnp.float32) * factor  32.9 us
    dot_general x16, matrix products, one_head(): jnp.dot(probs_low, value_head, preferred_element_type=jnp.float32)  22.4 us
  transfers between devices with their start and end apart: 8, of which 5 were waited for; matrix products, arithmetic and copies ran while one was open for 6% of the time, Pallas kernels for 0%

commit v1 on v0

v1 whole, which is shorter than its diff:
```python
import functools

import jax
import jax.numpy as jnp
from jax import lax
from jax.experimental import pallas as pl
from jax.experimental.pallas import tpu as pltpu
from jax.sharding import Mesh, PartitionSpec as P

HEADS = 16
HEAD_DIM = 128
WIDTH = HEADS * HEAD_DIM
TOK = 512
BLOCK = 256
BEFORE = 256
AFTER = 128
SPAN = BEFORE + BLOCK + AFTER
FACTOR = HEAD_DIM ** -0.5
TOKENS = 65536

AXES = ("y", "zh", "x", "zl", "core")
SIZES = (4, 2, 4, 2, 2)
GROUP_AXES = ("x", "zl", "core")
CHIPS = ("y", "zh", "x", "zl")
SHARDS = 8
MB = 1024 * 1024
PER_STEP = 4
STEPS = HEADS // PER_STEP
COLS = PER_STEP * HEAD_DIM


def dot_nt(left, right):
    return lax.dot_general(left, right, (((1,), (1,)), ((), ())), preferred_element_type=jnp.float32)


def dot_nn(left, right):
    return lax.dot_general(left, right, (((1,), (0,)), ((), ())), preferred_element_type=jnp.float32)


def dot_tn(left, right):
    return lax.dot_general(left, right, (((0,), (0,)), ((), ())), preferred_element_type=jnp.float32)


def fixed(shape):
    return pl.BlockSpec(shape, lambda i, *_: (0,) * len(shape))


def columns(rows, shift=0, row_block=0):
    return pl.BlockSpec((rows, COLS), lambda i, *_: (row_block, i + shift))


def cost(flops, micros=0.0):
    return pl.CostEstimate(flops=int(flops), bytes_accessed=int(micros * 3.0e6), transcendentals=0)


def params(mib):
    return pltpu.CompilerParams(vmem_limit_bytes=mib * MB)


def fill_bias(late, start_ref, end_ref, bias_ref):
    first = 0 if late else -BEFORE
    pos = lax.broadcasted_iota(jnp.int32, (SPAN, BLOCK), 0) + first
    ok = (pos >= start_ref[...]) & (pos < end_ref[...])
    bias_ref[...] = jnp.where(ok, 0.0, -jnp.inf).astype(jnp.float32)


def gather_keys(late, own, halo):
    if late:
        return jnp.concatenate([own, halo], axis=0)
    return jnp.concatenate([halo, own[: SPAN - BEFORE]], axis=0)


def forward_kernel(core_ref, start_ref, end_ref, q_ref, ko_ref, kh_ref, vo_ref, vh_ref,
                   out_ref, theirs_ref, lse_ref, bias_ref, *, late):
    @pl.when(pl.program_id(0) == 0)
    def _():
        fill_bias(late, start_ref, end_ref, bias_ref)

    even = core_ref[0] == 0
    for pair in range(PER_STEP // 2):
        outs = []
        for h in (2 * pair, 2 * pair + 1):
            cols = slice(h * HEAD_DIM, (h + 1) * HEAD_DIM)
            k = gather_keys(late, ko_ref[:, cols], kh_ref[:, cols])
            v = gather_keys(late, vo_ref[:, cols], vh_ref[:, cols])
            s = dot_nt(k, q_ref[:, cols]) + bias_ref[...]
            top = jnp.max(s, axis=0, keepdims=True)
            e = jnp.exp((s - top) * FACTOR)
            total = jnp.sum(e, axis=0, keepdims=True)
            o_t = dot_nn(v.T, e.astype(jnp.bfloat16)) * (1.0 / total)
            out = o_t.T.astype(jnp.bfloat16)
            out_ref[:, cols] = out
            outs.append(out)
            lse_ref[h] = top * FACTOR + jnp.log(total)
        theirs_ref[:, pair * HEAD_DIM:(pair + 1) * HEAD_DIM] = jnp.where(even, outs[1], outs[0])


def forward(late, core, start, end, q, k, v, halo):
    row_block = 1 if late else 0
    halo_rows = AFTER if late else BEFORE
    bounds = pl.BlockSpec((1, BLOCK), lambda i, *_: (0, row_block))
    return pl.pallas_call(
        functools.partial(forward_kernel, late=late),
        grid_spec=pltpu.PrefetchScalarGridSpec(
            num_scalar_prefetch=1,
            grid=(STEPS,),
            in_specs=[bounds, bounds, columns(BLOCK, row_block=row_block),
                      columns(TOK), columns(halo_rows), columns(TOK), columns(halo_rows, STEPS)],
            out_specs=[columns(BLOCK),
                       pl.BlockSpec((BLOCK, COLS // 2), lambda i, *_: (0, i)),
                       pl.BlockSpec((PER_STEP, 1, BLOCK), lambda i, *_: (i, 0, 0))],
            scratch_shapes=[pltpu.VMEM((SPAN, BLOCK), jnp.float32)],
        ),
        out_shape=[jax.ShapeDtypeStruct((BLOCK, WIDTH), jnp.bfloat16),
                   jax.ShapeDtypeStruct((BLOCK, WIDTH // 2), jnp.bfloat16),
                   jax.ShapeDtypeStruct((HEADS, 1, BLOCK), jnp.float32)],
        compiler_params=params(32),
        cost_estimate=cost(10e9),
        name="attend_late" if late else "attend_early",
    )(core, start, end, q, k, halo, v, halo)


def backward_kernel(start_ref, end_ref, lse_ref, q_ref, g_ref, ko_ref, kh_ref, vo_ref, vh_ref, *refs, late):
    if late:
        dki_ref, dvi_ref, dq_ref, dk_ref, dv_ref, halo_k_ref, halo_v_ref, bias_ref = refs
    else:
        dq_ref, dk_ref, dv_ref, halo_k_ref, halo_v_ref, bias_ref = refs

    @pl.when(pl.program_id(0) == 0)
    def _():
        fill_bias(late, start_ref, end_ref, bias_ref)

    for h in range(PER_STEP):
        cols = slice(h * HEAD_DIM, (h + 1) * HEAD_DIM)
        k = gather_keys(late, ko_ref[:, cols], kh_ref[:, cols])
        v = gather_keys(late, vo_ref[:, cols], vh_ref[:, cols])
        q = q_ref[:, cols]
        g = g_ref[:, cols]
        s = dot_nt(k, q) + bias_ref[...]
        p = jnp.exp(s * FACTOR - lse_ref[h])
        dp = dot_nt(v, g)
        inner = jnp.sum(p * dp, axis=0, keepdims=True)
        ds = (p * (dp - inner)).astype(jnp.bfloat16)
        dv = dot_nn(p.astype(jnp.bfloat16), g)
        dk = dot_nn(ds, q) * FACTOR
        dq_ref[:, cols] = (dot_nn(k.T, ds) * FACTOR).T.astype(jnp.bfloat16)
        if late:
            keep = SPAN - BEFORE
            dk_ref[:keep, cols] = (dk[:keep] + dki_ref[:, cols].astype(jnp.float32)).astype(jnp.bfloat16)
            dv_ref[:keep, cols] = (dv[:keep] + dvi_ref[:, cols].astype(jnp.float32)).astype(jnp.bfloat16)
            dk_ref[keep:, cols] = dk[keep:TOK].astype(jnp.bfloat16)
            dv_ref[keep:, cols] = dv[keep:TOK].astype(jnp.bfloat16)
            halo_k_ref[:, cols] = dk[TOK:].astype(jnp.bfloat16)
            halo_v_ref[:, cols] = dv[TOK:].astype(jnp.bfloat16)
        else:
            dk_ref[:, cols] = dk[BEFORE:].astype(dk_ref.dtype)
            dv_ref[:, cols] = dv[BEFORE:].astype(dv_ref.dtype)
            halo_k_ref[:, cols] = dk[:BEFORE].astype(jnp.bfloat16)
            halo_v_ref[:, cols] = dv[:BEFORE].astype(jnp.bfloat16)


def backward(late, start, end, lse, q, g, k, v, halo, *earlier):
    row_block = 1 if late else 0
    halo_rows = AFTER if late else BEFORE
    own_rows = TOK if late else SPAN - BEFORE
    own_type = jnp.bfloat16 if late else jnp.float32
    bounds = pl.BlockSpec((1, BLOCK), lambda i, *_: (0, row_block))
    shape = jax.ShapeDtypeStruct
    return pl.pallas_call(
        functools.partial(backward_kernel, late=late),
        grid=(STEPS,),
        in_specs=[bounds, bounds, pl.BlockSpec((PER_STEP, 1, BLOCK), lambda i: (i, 0, 0)),
                  columns(BLOCK, row_block=row_block), columns(BLOCK, row_block=row_block),
                  columns(TOK), columns(halo_rows), columns(TOK), columns(halo_rows, STEPS)]
        + [columns(SPAN - BEFORE)] * len(earlier),
        out_specs=[columns(BLOCK), columns(own_rows), columns(own_rows), columns(halo_rows), columns(halo_rows)],
        out_shape=[shape((BLOCK, WIDTH), jnp.bfloat16),
                   shape((own_rows, WIDTH), own_type), shape((own_rows, WIDTH), own_type),
                   shape((halo_rows, WIDTH), jnp.bfloat16), shape((halo_rows, WIDTH), jnp.bfloat16)],
        scratch_shapes=[pltpu.VMEM((SPAN, BLOCK), jnp.float32)],
        compiler_params=params(40),
        cost_estimate=cost(13e9),
        name="grads_late" if late else "grads_early",
    )(start, end, lse, q, g, k, halo, v, halo, *earlier)


def finish_kernel(dq0_ref, dq1_ref, dk_ref, dv_ref, kn_ref, vn_ref, kp_ref, vp_ref, dq_ref, dko_ref, dvo_ref):
    dq_ref[:BLOCK] = dq0_ref[...]
    dq_ref[BLOCK:] = dq1_ref[...]
    for own_ref, next_ref, prev_ref, out_ref in ((dk_ref, kn_ref, kp_ref, dko_ref), (dv_ref, vn_ref, vp_ref, dvo_ref)):
        f32 = jnp.float32
        out_ref[:AFTER] = (own_ref[:AFTER].astype(f32) + prev_ref[...].astype(f32)).astype(jnp.bfloat16)
        out_ref[AFTER:TOK - BEFORE] = own_ref[AFTER:TOK - BEFORE]
        out_ref[TOK - BEFORE:] = (own_ref[TOK - BEFORE:].astype(f32) + next_ref[...].astype(f32)).astype(jnp.bfloat16)


def finish(dq0, dq1, dk, dv, k_next, v_next, k_prev, v_prev):
    return pl.pallas_call(
        finish_kernel,
        grid=(STEPS,),
        in_specs=[columns(BLOCK), columns(BLOCK), columns(TOK), columns(TOK),
                  columns(BEFORE), columns(BEFORE), columns(AFTER), columns(AFTER)],
        out_specs=[columns(TOK)] * 3,
        out_shape=[jax.ShapeDtypeStruct((TOK, WIDTH), jnp.bfloat16)] * 3,
        compiler_params=params(24),
        cost_estimate=cost(4e9),
        name="finish_grads",
    )(dq0, dq1, dk, dv, k_next, v_next, k_prev, v_prev)


def weight_sums_kernel(core_ref, early_ref, late_ref, peer_early_ref, peer_late_ref, cot_ref, cot_peer_ref, out_ref):
    own = jnp.concatenate([early_ref[...], late_ref[...]], axis=0)
    peer = jnp.concatenate([peer_early_ref[...], peer_late_ref[...]], axis=0)
    core = core_ref[0]
    parts = [jnp.where(core == 0, own[:, 2 * j * HEAD_DIM:(2 * j + 1) * HEAD_DIM],
                       own[:, (2 * j + 1) * HEAD_DIM:(2 * j + 2) * HEAD_DIM]) for j in range(2)]
    own = jnp.concatenate(parts, axis=1)
    both = dot_tn(own, cot_ref[...]) + dot_tn(peer, cot_peer_ref[...])
    out_ref[...] = both.astype(jnp.bfloat16)


def weight_sums(core, early, late, peer_early, peer_late, cot, cot_peer):
    own_spec = pl.BlockSpec((BLOCK, 4 * HEAD_DIM), lambda i, *_: (0, i))
    peer_spec = pl.BlockSpec((BLOCK, 2 * HEAD_DIM), lambda i, *_: (0, i))
    return pl.pallas_call(
        weight_sums_kernel,
        grid_spec=pltpu.PrefetchScalarGridSpec(
            num_scalar_prefetch=1,
            grid=(4,),
            in_specs=[own_spec, own_spec, peer_spec, peer_spec, fixed((TOK, WIDTH)), fixed((TOK, WIDTH))],
            out_specs=pl.BlockSpec((2 * HEAD_DIM, WIDTH), lambda i, *_: (i, 0)),
        ),
        out_shape=jax.ShapeDtypeStruct((WIDTH // 2, WIDTH), jnp.bfloat16),
        compiler_params=params(40),
        cost_estimate=cost(7e9),
        name="weight_sums",
    )(core, early, late, peer_early, peer_late, cot, cot_peer)


def grad_attn_kernel(core_ref, cot_ref, mine_ref, other_ref, out_ref, rows_ref):
    core = core_ref[0]
    rows_ref[core] = mine_ref[0]
    rows_ref[1 - core] = other_ref[0]
    out_ref[...] = dot_nt(cot_ref[...], rows_ref[...].reshape(2 * HEAD_DIM, WIDTH)).astype(jnp.bfloat16)


def grad_attention(core, cot, mine, other):
    piece = pl.BlockSpec((1, HEAD_DIM, WIDTH), lambda i, *_: (i, 0, 0))
    return pl.pallas_call(
        grad_attn_kernel,
        grid_spec=pltpu.PrefetchScalarGridSpec(
            num_scalar_prefetch=1,
            grid=(SHARDS,),
            in_specs=[fixed((TOK, WIDTH)), piece, piece],
            out_specs=pl.BlockSpec((TOK, 2 * HEAD_DIM), lambda i, *_: (0, i)),
            scratch_shapes=[pltpu.VMEM((2, HEAD_DIM, WIDTH), jnp.bfloat16)],
        ),
        out_shape=jax.ShapeDtypeStruct((TOK, WIDTH), jnp.bfloat16),
        compiler_params=params(32),
        cost_estimate=cost(7e9),
        name="grad_attention",
    )(core, cot, mine, other)


def project_kernel(core_ref, early_ref, late_ref, mine_ref, other_ref, out_ref, rows_ref):
    core = core_ref[0]
    tile = out_ref.shape[1]
    rows_ref[:, core] = mine_ref[...]
    rows_ref[:, 1 - core] = other_ref[...]
    weight = rows_ref[...].reshape(WIDTH, tile)
    out_ref[:BLOCK] = dot_nn(early_ref[...], weight).astype(jnp.bfloat16)
    out_ref[BLOCK:] = dot_nn(late_ref[...], weight).astype(jnp.bfloat16)


def project(core, early, late, mine, other):
    tile = 512
    piece = pl.BlockSpec((SHARDS, HEAD_DIM, tile), lambda i, *_: (0, 0, i))
    return pl.pallas_call(
        project_kernel,
        grid_spec=pltpu.PrefetchScalarGridSpec(
            num_scalar_prefetch=1,
            grid=(WIDTH // tile,),
            in_specs=[fixed((BLOCK, WIDTH)), fixed((BLOCK, WIDTH)), piece, piece],
            out_specs=pl.BlockSpec((TOK, tile), lambda i, *_: (0, i)),
            scratch_shapes=[pltpu.VMEM((SHARDS, 2, HEAD_DIM, tile), jnp.bfloat16)],
        ),
        out_shape=jax.ShapeDtypeStruct((TOK, WIDTH), jnp.bfloat16),
        compiler_params=params(32),
        cost_estimate=cost(7e9),
        name="project",
    )(core, early, late, mine, other)


def sum_pieces_kernel(pieces_ref, out_ref):
    total = pieces_ref[0].astype(jnp.float32)
    for i in range(1, pieces_ref.shape[0]):
        total += pieces_ref[i].astype(jnp.float32)
    for i in range(out_ref.shape[0]):
        out_ref[i] = total.astype(jnp.bfloat16)


def sum_pieces(pieces, copies):
    count, rows, width = pieces.shape
    tile = 512
    return pl.pallas_call(
        sum_pieces_kernel,
        grid=(width // tile,),
        in_specs=[pl.BlockSpec((count, rows, tile), lambda i: (0, 0, i))],
        out_specs=pl.BlockSpec((copies, rows, tile), lambda i: (0, 0, i)),
        out_shape=jax.ShapeDtypeStruct((copies, rows, width), jnp.bfloat16),
        compiler_params=params(24),
        cost_estimate=cost(2e9),
        name="sum_pieces",
    )(pieces)


def swapped(array):
    return lax.ppermute(array, "core", [(0, 1), (1, 0)])


def passed_along(array, by):
    devices = 16
    pairs = [(i, i + by) for i in range(devices) if 0 <= i + by < devices]
    return lax.ppermute(array, GROUP_AXES, pairs)


def on_device(query_rows, key_rows, value_rows, pyramid_start, scale_end, out_weight, cotangent):
    core = lax.axis_index("core").astype(jnp.int32)
    group_index = lax.axis_index(GROUP_AXES).astype(jnp.int32)
    core_arg = core.reshape(1)
    start = (pyramid_start - group_index * TOK).reshape(1, TOK)
    end = (scale_end - group_index * TOK).reshape(1, TOK)

    after = passed_along(jnp.concatenate([key_rows[:AFTER], value_rows[:AFTER]], axis=1), -1)
    before = passed_along(jnp.concatenate([key_rows[TOK - BEFORE:], value_rows[TOK - BEFORE:]], axis=1), 1)
    half = lax.dynamic_slice_in_dim(out_weight, core * HEAD_DIM, HEAD_DIM, 0)
    mine = lax.all_to_all(jnp.broadcast_to(half, (SHARDS, HEAD_DIM, WIDTH)), ("y", "zh"), 0, 0, tiled=True)
    other = swapped(mine)
    cot_peer = swapped(cotangent)

    late, late_theirs, late_lse = forward(True, core_arg, start, end, query_rows, key_rows, value_rows, after)
    peer_late = swapped(late_theirs)
    early, early_theirs, early_lse = forward(False, core_arg, start, end, query_rows, key_rows, value_rows, before)
    peer_early = swapped(early_theirs)

    sums = weight_sums(core_arg, early, late, peer_early, peer_late, cotangent, cot_peer)
    pieces = lax.all_to_all(sums.reshape(64, 16, WIDTH), CHIPS, 0, 0, tiled=True)

    grad_attn = grad_attention(core_arg, cotangent, mine, other)
    dq0, dk0, dv0, k_before, v_before = backward(
        False, start, end, early_lse, query_rows, grad_attn, key_rows, value_rows, before)
    k_next = passed_along(k_before, -1)
    v_next = passed_along(v_before, -1)
    dq1, dk1, dv1, k_after, v_after = backward(
        True, start, end, late_lse, query_rows, grad_attn, key_rows, value_rows, after, dk0, dv0)
    k_prev = passed_along(k_after, 1)
    v_prev = passed_along(v_after, 1)

    layer_out = project(core_arg, early, late, mine, other)

    summed = sum_pieces(pieces, 16)
    rows = lax.all_to_all(summed, ("core", "x", "zl"), 0, 0, tiled=True)
    weight_grad = rows.reshape(2 * HEAD_DIM, WIDTH).astype(jnp.float32) * (float(TOKENS) ** -0.5)

    query_grad, key_grad, value_grad = finish(dq0, dq1, dk1, dv1, k_next, v_next, k_prev, v_prev)
    return (layer_out, query_grad, key_grad, value_grad, weight_grad)


def solution(mesh):
    inner = Mesh(mesh.devices.reshape(SIZES), AXES)
    rows = P(AXES, None)
    shard = P(("y", "zh"), None)
    return jax.shard_map(
        on_device,
        mesh=inner,
        in_specs=(rows, rows, rows, P(AXES), P(AXES), shard, rows),
        out_specs=(rows, rows, rows, rows, shard),
        check_vma=False,
    )
```

time: 751 us -> 278 us (0.37)
  waiting for transfers between devices: 423 us -> 109 us
  matrix products: 192 us -> 0 us
  Pallas kernels: 0 us -> 77.6 us
  local copies, waits for them, and re-layouts: 52.3 us -> 10.5 us
  starting transfers between devices: 14 us -> 52.2 us
  other arithmetic: 40.1 us -> 4.13 us
  blocking collectives: 0 us -> 20.8 us
  between operations: 14 us -> 0.98 us
  loops' own time: 11.2 us -> 0 us
    reduce_scatter x2 -> x0, waiting for transfers between devices: 282 us -> none  [the longest x1 179 us: on_device(): lax.psum_scatter(full_term, 'ctx', scatter_dimension=1, tiled=True)]
    dot_general x99 -> x0, matrix products: 192 us -> none  [the longest x33 63.9 us: contract_rows(): lax.dot_general(left, right, (((0,), (0,)), ((), ())), preferred_element_...]
    pallas_call x0 -> x9, Pallas kernels: none -> 77.6 us  [the longest x2 24.8 us: backward(): pl.pallas_call(functools.partial(backward_kernel, late=late), grid=(STEPS...]
    all_gather x2 -> x0, waiting for transfers between devices: 64.9 us -> none  [the longest x1 64.9 us: on_device(): full_weight = lax.all_gather(out_weight, 'dp', axis=0, tiled=True)]
    all_to_all x0 -> x2, waiting for transfers between devices: none -> 53.5 us  [the longest x1 53.5 us: on_device(): lax.all_to_all(sums.reshape(64, 16, WIDTH), CHIPS, 0, 0, tiled=True)]
    all_to_all x0 -> x2, starting transfers between devices: none -> 34 us  [the longest x1 26.7 us: on_device(): lax.all_to_all(sums.reshape(64, 16, WIDTH), CHIPS, 0, 0, tiled=True)]
    all_to_all x0 -> x1, blocking collectives: none -> 20.8 us  [on_device(): rows = lax.all_to_all(summed, ('core', 'x', 'zl'), 0, 0, tiled=True)]
    ppermute x4 -> x10, waiting for transfers between devices: 74.9 us -> 55.8 us  [the longest x6 53.9 us: passed_along(): return lax.ppermute(array, GROUP_AXES, pairs)]
  transfers between devices with their start and end apart: 8 -> 12, of which waited for: 5 -> 6; matrix products, arithmetic and copies ran while one was open for 6% -> 2% of each run, Pallas kernels for 0% -> 19%
where the time goes in v1:
time: 278 us; the launch traced here: 275 us
  waiting for transfers between devices  109 us (39%)
  Pallas kernels  77.6 us (28%)
  starting transfers between devices  52.2 us (19%)
  blocking collectives  20.8 us (7%)
  local copies, waits for them, and re-layouts  10.5 us (4%)
  other arithmetic  4.13 us (1%)
    ppermute x6, waiting for transfers between devices, passed_along(): return lax.ppermute(array, GROUP_AXES, pairs)  53.9 us
    all_to_all x1, waiting for transfers between devices, on_device(): lax.all_to_all(sums.reshape(64, 16, WIDTH), CHIPS, 0, 0, tiled=True)  53.5 us
    all_to_all x1, starting transfers between devices, on_device(): lax.all_to_all(sums.reshape(64, 16, WIDTH), CHIPS, 0, 0, tiled=True)  26.7 us
    pallas_call x2, Pallas kernels, backward(): pl.pallas_call(functools.partial(backward_kernel, late=late), grid=(STEPS...  24.8 us
    pallas_call x2, Pallas kernels, forward(): pl.pallas_call(functools.partial(forward_kernel, late=late), grid_spec=pl...  21 us
    all_to_all x1, blocking collectives, on_device(): rows = lax.all_to_all(summed, ('core', 'x', 'zl'), 0, 0, tiled=True)  20.8 us
    ppermute x6, starting transfers between devices, passed_along(): return lax.ppermute(array, GROUP_AXES, pairs)  17.5 us
    pallas_call x1, Pallas kernels, grad_attention(): pl.pallas_call(grad_attn_kernel, grid_spec=pltpu.PrefetchScalarGridSpec(n...  9.56 us
  transfers between devices with their start and end apart: 12, of which 6 were waited for; matrix products, arithmetic and copies ran while one was open for 2% of the time, Pallas kernels for 19%

profile of v1, /device:TPU:1, one launch (start us, length us, event | category | flops | bytes accessed | tf_op | source)
XLA Modules:
  0.0 275.4 jit_solution(11957838230002629641)
XLA Ops:
  4.0 5.1 %collective-permute-start = (bf16[256,4096]{1,0:T(8,128)(2,1)}, bf16[256,4096]{1,0:T(8,128)(2,1)}, u32[]{:S(2)}, u32[]{:S(2)}) collective-permute-start(bf16[256,4096]{1,0:T(8,128)(2,1)} %pad_maximum_fusion), channel_id=1, source_target_pairs={{0,1},{1,2},{2,3},{3,4},{4,5},{5,6},{6,7},{7,8},{8,9},{9,10},{10,1... | collective-permute-start | bytes 6291464 | tf_op jit(solution)/shard_map/ppermute | solution.py:324
  10.1 1.9 collective-permute-start.1
  12.1 2.6 broadcast_in_dim.3
  14.7 7.3 %all-to-all-start = ((bf16[8,128,2048]{2,1,0:T(8,128)(2,1)}), bf16[8,128,2048]{2,1,0:T(8,128)(2,1)}, u32[]{:S(2)}, u32[]{:S(2)}) async-start(bf16[8,128,2048]{2,1,0:T(8,128)(2,1)} %broadcast_in_dim.3), calls=%async_computation | async-start | bytes 8388608 | tf_op jit(solution)/shard_map/all_to_all | solution.py:337
  22.1 30.0 %collective-permute-done.1.kh_ref.vh_ref = bf16[128,4096]{1,0:T(8,128)(2,1)} collective-permute-done((bf16[128,4096]{1,0:T(8,128)(2,1)}, bf16[128,4096]{1,0:T(8,128)(2,1)}, u32[]{:S(2)}, u32[]{:S(2)}) %collective-permute-start.1) | collective-permute-done | bytes 1048608 | tf_op jit(solution)/shard_map/ppermute | solution.py:324
  55.3 10.5 %attend_late.1 = (bf16[256,2048]{1,0:T(8,128)(2,1)S(1)}, bf16[256,1024]{1,0:T(8,128)(2,1)S(1)}, f32[16,1,256]{2,1,0:T(1,128)S(1)}) custom-call(s32[1]{0:T(128)} %bitcast.core_ref, s32[1,512]{1,0:T(1,128)S(1)} %bitcast.10, s32[1,512]{1,0:T(1,128)S(1)} %bitcast.6, bf16[512,2048]{1,0:T(8,128)(2,1)S(1)} %copy-done.8, bf16[512,2048]{1,0:T(8,128)(2,1)S(1)} %copy-done.3, ...), custom_call_target="tpu_custom_call" | custom-call | flops 10000000000 | tf_op jit(solution)/shard_map/attend_late/pallas_call | solution.py:102
  65.9 17.0 %collective-permute-done.kh_ref.vh_ref = bf16[256,4096]{1,0:T(8,128)(2,1)} collective-permute-done((bf16[256,4096]{1,0:T(8,128)(2,1)}, bf16[256,4096]{1,0:T(8,128)(2,1)}, u32[]{:S(2)}, u32[]{:S(2)}) %collective-permute-start) | collective-permute-done | bytes 2097184 | tf_op jit(solution)/shard_map/ppermute | solution.py:324
  82.9 10.5 %attend_early.1 = (bf16[256,2048]{1,0:T(8,128)(2,1)S(1)}, bf16[256,1024]{1,0:T(8,128)(2,1)S(1)}, f32[16,1,256]{2,1,0:T(1,128)S(1)}) custom-call(s32[1]{0:T(128)} %bitcast.core_ref, s32[1,512]{1,0:T(1,128)S(1)} %bitcast.11, s32[1,512]{1,0:T(1,128)S(1)} %bitcast.7, bf16[512,2048]{1,0:T(8,128)(2,1)S(1)} %copy-done.8, bf16[512,2048]{1,0:T(8,128)(2,1)S(1)} %copy-done.3, ...), custom_call_target="tpu_custom_call" | custom-call | flops 10000000000 | tf_op jit(solution)/shard_map/attend_early/pallas_call | solution.py:102
  95.5 7.0 %weight_sums.1 = bf16[1024,2048]{1,0:T(8,128)(2,1)S(1)} custom-call(s32[1]{0:T(128)} %bitcast.core_ref, bf16[256,2048]{1,0:T(8,128)(2,1)S(1)} %get-tuple-element.24.early_ref, bf16[256,2048]{1,0:T(8,128)(2,1)S(1)} %get-tuple-element.25.late_ref, bf16[256,1024]{1,0:T(8,128)(2,1)S(1)} %collective-permute-done.7.peer_early_ref, ...), custom_call_target="tpu_custom_call" | custom-call | flops 7000000000 | tf_op jit(solution)/shard_map/weight_sums/pallas_call | solution.py:225
  102.5 2.0 copy-done.2
  104.5 26.7 %all-to-all-start.1 = ((bf16[64,16,2048]{2,1,0:T(8,128)(2,1)}), bf16[64,16,2048]{2,1,0:T(8,128)(2,1)}, u32[]{:S(2)}, u32[]{:S(2)}) async-start(bf16[64,16,2048]{2,1,0:T(8,128)(2,1)} %bitcast.5), calls=%async_computation.1 | async-start | bytes 8388608 | tf_op jit(solution)/shard_map/all_to_all | solution.py:347
  131.7 53.5 %all-to-all-done.1.pieces_ref = bf16[64,16,2048]{2,1,0:T(8,128)(2,1)} async-done(((bf16[64,16,2048]{2,1,0:T(8,128)(2,1)}), bf16[64,16,2048]{2,1,0:T(8,128)(2,1)}, u32[]{:S(2)}, u32[]{:S(2)}) %all-to-all-start.1) | async-done | bytes 4194336 | tf_op jit(solution)/shard_map/all_to_all | solution.py:347
  185.2 3.2 %sum_pieces.1 = bf16[16,16,2048]{2,1,0:T(8,128)(2,1)S(1)} custom-call(bf16[64,16,2048]{2,1,0:T(8,128)(2,1)} %all-to-all-done.1.pieces_ref), custom_call_target="tpu_custom_call" | custom-call | flops 2000000000 | tf_op jit(solution)/shard_map/sum_pieces/pallas_call | solution.py:305
  188.4 20.8 %all_to_all.15 = bf16[16,16,2048]{2,1,0:T(8,128)(2,1)S(1)} all-to-all(bf16[16,16,2048]{2,1,0:T(8,128)(2,1)S(1)} %sum_pieces.1), channel_id=1, replica_groups=mesh['y'=4,'zh'=2,'x'=4,'zl'=2,'core'=2] {'core','x','zl'}, dimensions={0} | all-to-all | bytes 2097152 | tf_op jit(solution)/shard_map/all_to_all | solution.py:362
  211.5 9.6 %grad_attention.1.g_ref = bf16[512,2048]{1,0:T(8,128)(2,1)S(1)} custom-call(s32[1]{0:T(128)} %bitcast.core_ref, bf16[512,2048]{1,0:T(8,128)(2,1)S(1)} %copy-done.7, bf16[8,128,2048]{2,1,0:T(8,128)(2,1)} %all-to-all-done.mine_ref, bf16[8,128,2048]{2,1,0:T(8,128)(2,1)} %collective-permute-done.2.other_ref), custom_call_target="tpu_custom_call" | custom-call | flops 7000000000 | tf_op jit(solution)/shard_map/grad_attention/pallas_call | solution.py:249
  221.1 12.4 %grads_early.1 = (bf16[256,2048]{1,0:T(8,128)(2,1)S(1)}, f32[384,2048]{1,0:T(8,128)}, f32[384,2048]{1,0:T(8,128)}, bf16[256,2048]{1,0:T(8,128)(2,1)S(1)}, bf16[256,2048]{1,0:T(8,128)(2,1)S(1)}) custom-call(s32[1,512]{1,0:T(1,128)S(1)} %bitcast.12, s32[1,512]{1,0:T(1,128)S(1)} %bitcast.8, f32[16,1,256]{2,1,0:T(1,128)S(1)} %get-tuple-element.26.lse_ref, ...), custom_call_target="tpu_custom_call" | custom-call | flops 12999999488 | tf_op jit(solution)/shard_map/grads_early/pallas_call | solution.py:169
  233.6 3.0 %collective-permute-start.3 = (bf16[256,2048]{1,0:T(8,128)(2,1)S(1)}, bf16[256,2048]{1,0:T(8,128)(2,1)S(1)}, u32[]{:S(2)}, u32[]{:S(2)}) collective-permute-start(bf16[256,2048]{1,0:T(8,128)(2,1)S(1)} %get-tuple-element.34), channel_id=1, source_target_pairs={{1,0},{2,1},{3,2},{4,3},{5,4},{6,5},{7,6},{8,7},{9,8},{10,9},{11,1... | collective-permute-start | bytes 3145736 | tf_op jit(solution)/shard_map/ppermute | solution.py:324
  236.6 1.9 collective-permute-start.4
  238.6 12.4 %grads_late.1 = (bf16[256,2048]{1,0:T(8,128)(2,1)S(1)}, bf16[512,2048]{1,0:T(8,128)(2,1)S(1)}, bf16[512,2048]{1,0:T(8,128)(2,1)S(1)}, bf16[128,2048]{1,0:T(8,128)(2,1)S(1)}, bf16[128,2048]{1,0:T(8,128)(2,1)S(1)}) custom-call(s32[1,512]{1,0:T(1,128)S(1)} %bitcast.13, s32[1,512]{1,0:T(1,128)S(1)} %bitcast.9, f32[16,1,256]{2,1,0:T(1,128)S(1)} %get-tuple-element.28.lse_ref, ...), custom_call_target="tpu_custom_call" | custom-call | flops 12999999488 | tf_op jit(solution)/shard_map/grads_late/pallas_call | solution.py:169
  250.9 3.6 %collective-permute-start.5 = (bf16[128,2048]{1,0:T(8,128)(2,1)S(1)}, bf16[128,2048]{1,0:T(8,128)(2,1)S(1)}, u32[]{:S(2)}, u32[]{:S(2)}) collective-permute-start(bf16[128,2048]{1,0:T(8,128)(2,1)S(1)} %get-tuple-element.36), channel_id=1, source_target_pairs={{0,1},{1,2},{2,3},{3,4},{4,5},{5,6},{6,7},{7,8},{8,9},{9,10},{10,1... | collective-permute-start | bytes 1572872 | tf_op jit(solution)/shard_map/ppermute | solution.py:324
  254.6 1.9 collective-permute-start.6
  256.5 8.4 %project.1 = bf16[512,2048]{1,0:T(8,128)(2,1)} custom-call(s32[1]{0:T(128)} %bitcast.core_ref, bf16[256,2048]{1,0:T(8,128)(2,1)S(1)} %copy-done.13, bf16[256,2048]{1,0:T(8,128)(2,1)S(1)} %copy-done.11, bf16[8,128,2048]{2,1,0:T(8,128)(2,1)} %all-to-all-done.mine_ref, bf16[8,128,2048]{2,1,0:T(8,128)(2,1)} %collective-permute-done.2.other_ref), custom_call_target="tpu_custom_call" | custom-call | flops 7000000000 | tf_op jit(solution)/shard_map/project/pallas_call | solution.py:278
  266.2 5.6 %collective-permute-done.6.vp_ref = bf16[128,2048]{1,0:T(8,128)(2,1)S(1)} collective-permute-done((bf16[128,2048]{1,0:T(8,128)(2,1)S(1)}, bf16[128,2048]{1,0:T(8,128)(2,1)S(1)}, u32[]{:S(2)}, u32[]{:S(2)}) %collective-permute-start.6) | collective-permute-done | bytes 524320 | tf_op jit(solution)/shard_map/ppermute | solution.py:324
  271.8 3.6 %finish_grads.1 = (bf16[512,2048]{1,0:T(8,128)(2,1)}, bf16[512,2048]{1,0:T(8,128)(2,1)}, bf16[512,2048]{1,0:T(8,128)(2,1)}) custom-call(bf16[256,2048]{1,0:T(8,128)(2,1)S(1)} %get-tuple-element.27.dq0_ref, bf16[256,2048]{1,0:T(8,128)(2,1)S(1)} %get-tuple-element.31.dq1_ref, bf16[512,2048]{1,0:T(8,128)(2,1)S(1)} %get-tuple-element.32.dk_ref, ...), custom_call_target="tpu_custom_call" | custom-call | flops 4000000000 | tf_op jit(solution)/shard_map/finish_grads/pallas_call | solution.py:198
  (56 shorter events, 13.9 us)
Async XLA Ops:
  0.6 11.4 %copy-start = (bf16[256,2048]{1,0:T(8,128)(2,1)S(1)}, bf16[256,2048]{1,0:T(8,128)(2,1)}, u32[]{:S(2)}) copy-start(bf16[256,2048]{1,0:T(8,128)(2,1)} %param.12) | copy-start | bytes 3145732
  4.0 5.1 %slice-start.3 = ((bf16[512,2048]{1,0:T(8,128)(2,1)}), bf16[128,2048]{1,0:T(8,128)(2,1)S(1)}, s32[]{:S(2)}) async-start(bf16[512,2048]{1,0:T(8,128)(2,1)} %vo_ref.7), calls=%async_computation.6 | async-start | bytes 1048576 | tf_op jit(solution)/shard_map/slice | solution.py:334
  4.0 78.9 %collective-permute-start = (bf16[256,4096]{1,0:T(8,128)(2,1)}, bf16[256,4096]{1,0:T(8,128)(2,1)}, u32[]{:S(2)}, u32[]{:S(2)}) collective-permute-start(bf16[256,4096]{1,0:T(8,128)(2,1)} %pad_maximum_fusion), channel_id=1, source_target_pairs={{0,1},{1,2},{2,3},{3,4},{4,5},{5,6},{6,7},{7,8},{8,9},{9,10},{10,1... | collective-permute-start | bytes 6291464 | tf_op jit(solution)/shard_map/ppermute | solution.py:324
  10.1 41.9 %collective-permute-start.1 = (bf16[128,4096]{1,0:T(8,128)(2,1)}, bf16[128,4096]{1,0:T(8,128)(2,1)}, u32[]{:S(2)}, u32[]{:S(2)}) collective-permute-start(bf16[128,4096]{1,0:T(8,128)(2,1)} %pad_maximum_fusion.1), channel_id=1, source_target_pairs={{1,0},{2,1},{3,2},{4,3},{5,4},{6,5},{7,6},{8,7},{9,8},{10,9},{11,1... | collective-permute-start | bytes 3145736 | tf_op jit(solution)/shard_map/ppermute | solution.py:324
  14.7 7.4 %copy-start.14 = (s32[512]{0:T(512)S(1)}, s32[512]{0:T(512)}, u32[]{:S(2)}) copy-start(s32[512]{0:T(512)} %param.11) | copy-start | bytes 6148
  14.7 7.4 %copy-start.15 = (s32[512]{0:T(512)S(1)}, s32[512]{0:T(512)}, u32[]{:S(2)}) copy-start(s32[512]{0:T(512)} %param.10) | copy-start | bytes 6148
  14.7 37.4 %copy-start.3 = (bf16[512,2048]{1,0:T(8,128)(2,1)S(1)}, bf16[512,2048]{1,0:T(8,128)(2,1)}, u32[]{:S(2)}) copy-start(bf16[512,2048]{1,0:T(8,128)(2,1)} %ko_ref.7) | copy-start | bytes 6291460
  14.7 89.8 %all-to-all-start = ((bf16[8,128,2048]{2,1,0:T(8,128)(2,1)}), bf16[8,128,2048]{2,1,0:T(8,128)(2,1)}, u32[]{:S(2)}, u32[]{:S(2)}) async-start(bf16[8,128,2048]{2,1,0:T(8,128)(2,1)} %broadcast_in_dim.3), calls=%async_computation | async-start | bytes 8388608 | tf_op jit(solution)/shard_map/all_to_all | solution.py:337
  22.0 71.5 %collective-permute-start.9 = (bf16[512,2048]{1,0:T(8,128)(2,1)}, bf16[512,2048]{1,0:T(8,128)(2,1)}, u32[]{:S(2)}, u32[]{:S(2)}) collective-permute-start(bf16[512,2048]{1,0:T(8,128)(2,1)} %cot_ref.3), channel_id=1, source_target_pairs={{0,1},{1,0},{2,3},{3,2},{4,5},{5,4},{6,7},{7,6},{8,9},{9,8},{10,11... | collective-permute-start | bytes 6291464 | tf_op jit(solution)/shard_map/ppermute | solution.py:318
  65.7 29.7 %copy-start.10 = (bf16[256,2048]{1,0:T(8,128)(2,1)}, bf16[256,2048]{1,0:T(8,128)(2,1)S(1)}, u32[]{:S(2)}) copy-start(bf16[256,2048]{1,0:T(8,128)(2,1)S(1)} %get-tuple-element.25.late_ref) | copy-start | bytes 3145732
  65.8 29.7 %copy-start.6 = (bf16[512,2048]{1,0:T(8,128)(2,1)S(1)}, bf16[512,2048]{1,0:T(8,128)(2,1)}, u32[]{:S(2)}) copy-start(bf16[512,2048]{1,0:T(8,128)(2,1)} %cot_ref.3) | copy-start | bytes 6291460
  65.8 27.8 %collective-permute-start.8 = (bf16[256,1024]{1,0:T(8,128)(2,1)S(1)}, bf16[256,1024]{1,0:T(8,128)(2,1)S(1)}, u32[]{:S(2)}, u32[]{:S(2)}) collective-permute-start(bf16[256,1024]{1,0:T(8,128)(2,1)S(1)} %get-tuple-element.42), channel_id=1, source_target_pairs={{0,1},{1,0},{2,3},{3,2},{4,5},{5,4},{6,7},{7,6},{8,9},{9,8},{10,11... | collective-permute-start | bytes 1572872 | tf_op jit(solution)/shard_map/ppermute | solution.py:318
  93.5 9.0 %copy-start.12 = (bf16[256,2048]{1,0:T(8,128)(2,1)}, bf16[256,2048]{1,0:T(8,128)(2,1)S(1)}, u32[]{:S(2)}) copy-start(bf16[256,2048]{1,0:T(8,128)(2,1)S(1)} %get-tuple-element.24.early_ref) | copy-start | bytes 3145732
  93.5 2.0 collective-permute-start.7
  104.5 80.7 %all-to-all-start.1 = ((bf16[64,16,2048]{2,1,0:T(8,128)(2,1)}), bf16[64,16,2048]{2,1,0:T(8,128)(2,1)}, u32[]{:S(2)}, u32[]{:S(2)}) async-start(bf16[64,16,2048]{2,1,0:T(8,128)(2,1)} %bitcast.5), calls=%async_computation.1 | async-start | bytes 8388608 | tf_op jit(solution)/shard_map/all_to_all | solution.py:347
  131.2 79.6 %collective-permute-start.2 = (bf16[8,128,2048]{2,1,0:T(8,128)(2,1)}, bf16[8,128,2048]{2,1,0:T(8,128)(2,1)}, u32[]{:S(2)}, u32[]{:S(2)}) collective-permute-start(bf16[8,128,2048]{2,1,0:T(8,128)(2,1)} %all-to-all-done.mine_ref), channel_id=1, source_target_pairs={{0,1},{1,0},{2,3},{3,2},{4,5},{5,4},{6,7},{7,6},{8,9},{9,8},{10,11... | collective-permute-start | bytes 12582920 | tf_op jit(solution)/shard_map/ppermute | solution.py:318
  210.8 10.3 %copy-start.5 = (bf16[512,2048]{1,0:T(8,128)(2,1)S(1)}, bf16[512,2048]{1,0:T(8,128)(2,1)}, u32[]{:S(2)}) copy-start(bf16[512,2048]{1,0:T(8,128)(2,1)} %vo_ref.7) | copy-start | bytes 6291460
  210.8 10.4 %copy-start.9 = (bf16[512,2048]{1,0:T(8,128)(2,1)S(1)}, bf16[512,2048]{1,0:T(8,128)(2,1)}, u32[]{:S(2)}) copy-start(bf16[512,2048]{1,0:T(8,128)(2,1)} %q_ref.7) | copy-start | bytes 6291460
  233.6 38.2 %collective-permute-start.3 = (bf16[256,2048]{1,0:T(8,128)(2,1)S(1)}, bf16[256,2048]{1,0:T(8,128)(2,1)S(1)}, u32[]{:S(2)}, u32[]{:S(2)}) collective-permute-start(bf16[256,2048]{1,0:T(8,128)(2,1)S(1)} %get-tuple-element.34), channel_id=1, source_target_pairs={{1,0},{2,1},{3,2},{4,3},{5,4},{6,5},{7,6},{8,7},{9,8},{10,9},{11,1... | collective-permute-start | bytes 3145736 | tf_op jit(solution)/shard_map/ppermute | solution.py:324
  236.6 35.2 %collective-permute-start.4 = (bf16[256,2048]{1,0:T(8,128)(2,1)S(1)}, bf16[256,2048]{1,0:T(8,128)(2,1)S(1)}, u32[]{:S(2)}, u32[]{:S(2)}) collective-permute-start(bf16[256,2048]{1,0:T(8,128)(2,1)S(1)} %get-tuple-element.35), channel_id=1, source_target_pairs={{1,0},{2,1},{3,2},{4,3},{5,4},{6,5},{7,6},{8,7},{9,8},{10,9},{11,1... | collective-permute-start | bytes 3145736 | tf_op jit(solution)/shard_map/ppermute | solution.py:324
  238.5 18.0 %copy-start.11 = (bf16[256,2048]{1,0:T(8,128)(2,1)S(1)}, bf16[256,2048]{1,0:T(8,128)(2,1)}, u32[]{:S(2)}) copy-start(bf16[256,2048]{1,0:T(8,128)(2,1)} %copy-done.10) | copy-start | bytes 3145732
  238.6 18.0 %copy-start.13 = (bf16[256,2048]{1,0:T(8,128)(2,1)S(1)}, bf16[256,2048]{1,0:T(8,128)(2,1)}, u32[]{:S(2)}) copy-start(bf16[256,2048]{1,0:T(8,128)(2,1)} %copy-done.12) | copy-start | bytes 3145732
  250.9 15.2 %collective-permute-start.5 = (bf16[128,2048]{1,0:T(8,128)(2,1)S(1)}, bf16[128,2048]{1,0:T(8,128)(2,1)S(1)}, u32[]{:S(2)}, u32[]{:S(2)}) collective-permute-start(bf16[128,2048]{1,0:T(8,128)(2,1)S(1)} %get-tuple-element.36), channel_id=1, source_target_pairs={{0,1},{1,2},{2,3},{3,4},{4,5},{5,6},{6,7},{7,8},{8,9},{9,10},{10,1... | collective-permute-start | bytes 1572872 | tf_op jit(solution)/shard_map/ppermute | solution.py:324
  254.6 17.2 %collective-permute-start.6 = (bf16[128,2048]{1,0:T(8,128)(2,1)S(1)}, bf16[128,2048]{1,0:T(8,128)(2,1)S(1)}, u32[]{:S(2)}, u32[]{:S(2)}) collective-permute-start(bf16[128,2048]{1,0:T(8,128)(2,1)S(1)} %get-tuple-element.37), channel_id=1, source_target_pairs={{0,1},{1,2},{2,3},{3,4},{4,5},{5,6},{6,7},{7,8},{8,9},{9,10},{10,1... | collective-permute-start | bytes 1572872 | tf_op jit(solution)/shard_map/ppermute | solution.py:324
  (8 other events, 19.6 us)

commit v2 on v1

v2 whole, which is shorter than its diff:
```python
import functools

import jax
import jax.numpy as jnp
from jax import lax
from jax.experimental import pallas as pl
from jax.experimental.pallas import tpu as pltpu
from jax.sharding import Mesh, PartitionSpec as P

HEADS = 16
HEAD_DIM = 128
WIDTH = HEADS * HEAD_DIM
TOK = 512
BLOCK = 256
BEFORE = 256
AFTER = 128
SPAN = BEFORE + BLOCK + AFTER
FACTOR = HEAD_DIM ** -0.5
TOKENS = 65536

AXES = ("y", "zh", "x", "zl", "core")
SIZES = (4, 2, 4, 2, 2)
GROUP_AXES = ("x", "zl", "core")
MB = 1024 * 1024
PER_STEP = 4
STEPS = HEADS // PER_STEP
COLS = PER_STEP * HEAD_DIM


def dot_nt(left, right):
    return lax.dot_general(left, right, (((1,), (1,)), ((), ())), preferred_element_type=jnp.float32)


def dot_nn(left, right):
    return lax.dot_general(left, right, (((1,), (0,)), ((), ())), preferred_element_type=jnp.float32)


def dot_tn(left, right):
    return lax.dot_general(left, right, (((0,), (0,)), ((), ())), preferred_element_type=jnp.float32)


def fixed(shape):
    return pl.BlockSpec(shape, lambda i, *_: (0,) * len(shape))


def columns(rows, shift=0, row_block=0):
    return pl.BlockSpec((rows, COLS), lambda i, *_: (row_block, i + shift))


def halo_columns(rows):
    return pl.BlockSpec((2, rows, COLS), lambda i, *_: (0, 0, i))


def cost(flops):
    return pl.CostEstimate(flops=int(flops * 1e-3), bytes_accessed=0, transcendentals=0)


def params():
    return pltpu.CompilerParams(vmem_limit_bytes=56 * MB)


def fill_bias(late, start_ref, end_ref, bias_ref):
    first = 0 if late else -BEFORE
    pos = lax.broadcasted_iota(jnp.int32, (SPAN, BLOCK), 0) + first
    ok = (pos >= start_ref[...]) & (pos < end_ref[...])
    bias_ref[...] = jnp.where(ok, 0.0, -jnp.inf).astype(jnp.float32)


def gather_keys(late, own, halo):
    if late:
        return jnp.concatenate([own, halo], axis=0)
    return jnp.concatenate([halo, own[: SPAN - BEFORE]], axis=0)


HALVES = ((slice(0, 128), slice(0, 512)), (slice(128, 256), slice(128, 640)))


def assemble(first, second):
    none = jnp.zeros((SPAN - 512, 128), first.dtype)
    return jnp.concatenate([jnp.concatenate([first, none], axis=0), jnp.concatenate([none, second], axis=0)], axis=1)


def forward_kernel(core_ref, start_ref, end_ref, q_ref, ko_ref, kh_ref, vo_ref, vh_ref,
                   out_ref, theirs_ref, lse_ref, bias_ref, *, late):
    @pl.when(pl.program_id(0) == 0)
    def _():
        fill_bias(late, start_ref, end_ref, bias_ref)

    even = core_ref[0] == 0
    outs = []

    def head(h):
        return slice(h * HEAD_DIM, (h + 1) * HEAD_DIM)

    def scores(h):
        return dot_nt(gather_keys(late, ko_ref[:, head(h)], kh_ref[:, head(h)]), q_ref[:, head(h)])

    def weigh(s):
        parts = []
        for queries, keys in HALVES:
            part = s[keys, queries] + bias_ref[keys, queries]
            top = jnp.max(part, axis=0, keepdims=True)
            e = jnp.exp((part - top) * FACTOR)
            total = jnp.sum(e, axis=0, keepdims=True)
            parts.append((e.astype(jnp.bfloat16), top, total))
        first, second = parts
        return (assemble(first[0], second[0]), jnp.concatenate([first[1], second[1]], axis=1),
                jnp.concatenate([first[2], second[2]], axis=1))

    def mix(h, e, top, total):
        v = gather_keys(late, vo_ref[:, head(h)], vh_ref[:, head(h)])
        out = (dot_nn(v.T, e) * (1.0 / total)).T.astype(jnp.bfloat16)
        out_ref[:, head(h)] = out
        lse_ref[h] = top * FACTOR + jnp.log(total)
        outs.append(out)
        if h % 2:
            theirs_ref[:, head(h // 2)] = jnp.where(even, outs[h], outs[h - 1])

    ahead = scores(0)
    behind = None
    for h in range(PER_STEP):
        now, ahead = ahead, scores(h + 1) if h + 1 < PER_STEP else None
        weighed = weigh(now)
        if behind is not None:
            mix(h - 1, *behind)
        behind = weighed
    mix(PER_STEP - 1, *behind)


def forward(late, core, start, end, q, k, v, halo):
    row_block = 1 if late else 0
    halo_rows = AFTER if late else BEFORE
    bounds = pl.BlockSpec((1, BLOCK), lambda i, *_: (0, row_block))
    return pl.pallas_call(
        functools.partial(forward_kernel, late=late),
        grid_spec=pltpu.PrefetchScalarGridSpec(
            num_scalar_prefetch=1,
            grid=(STEPS,),
            in_specs=[bounds, bounds, columns(BLOCK, row_block=row_block),
                      columns(TOK), columns(halo_rows), columns(TOK), columns(halo_rows, STEPS)],
            out_specs=[columns(BLOCK),
                       pl.BlockSpec((BLOCK, COLS // 2), lambda i, *_: (0, i)),
                       pl.BlockSpec((PER_STEP, 1, BLOCK), lambda i, *_: (i, 0, 0))],
            scratch_shapes=[pltpu.VMEM((SPAN, BLOCK), jnp.float32)],
        ),
        out_shape=[jax.ShapeDtypeStruct((BLOCK, WIDTH), jnp.bfloat16),
                   jax.ShapeDtypeStruct((BLOCK, WIDTH // 2), jnp.bfloat16),
                   jax.ShapeDtypeStruct((HEADS, 1, BLOCK), jnp.float32)],
        compiler_params=params(),
        cost_estimate=cost(8e9),
        name="attend_late" if late else "attend_early",
    )(core, start, end, q, k, halo, v, halo)


def backward_kernel(place_ref, start_ref, end_ref, lse_ref, q_ref, near_ref, far_ref, ko_ref, kh_ref, vo_ref, vh_ref,
                    *refs, late):
    if late:
        dki_ref, dvi_ref, _, dq_ref, dk_ref, dv_ref, halo_ref, bias_ref, g_ref = refs
    else:
        dq_ref, dk_ref, dv_ref, halo_ref, bias_ref, g_ref = refs
    first = place_ref[1] == 0
    g_ref[:, :2 * HEAD_DIM] = jnp.where(first, near_ref[...], far_ref[...])
    g_ref[:, 2 * HEAD_DIM:] = jnp.where(first, far_ref[...], near_ref[...])

    @pl.when(pl.program_id(0) == 0)
    def _():
        fill_bias(late, start_ref, end_ref, bias_ref)

    def head(h):
        return slice(h * HEAD_DIM, (h + 1) * HEAD_DIM)

    def products(h):
        k = gather_keys(late, ko_ref[:, head(h)], kh_ref[:, head(h)])
        v = gather_keys(late, vo_ref[:, head(h)], vh_ref[:, head(h)])
        return k, [(dot_nt(k[keys], q_ref[queries, head(h)]), dot_nt(v[keys], g_ref[queries, head(h)]))
                   for queries, keys in HALVES]

    def differentiate(h, k, pairs):
        probs = []
        grads = []
        for (queries, keys), (s, dp) in zip(HALVES, pairs):
            p = jnp.exp((s + bias_ref[keys, queries]) * FACTOR - lse_ref[h, :, queries])
            inner = jnp.sum(p * dp, axis=0, keepdims=True)
            probs.append(p.astype(jnp.bfloat16))
            grads.append((p * (dp - inner)).astype(jnp.bfloat16))
        return k, assemble(*probs), assemble(*grads)

    def collect(h, k, p, ds):
        cols = head(h)
        dv = dot_nn(p, g_ref[:, cols])
        dk = dot_nn(ds, q_ref[:, cols]) * FACTOR
        dq_ref[:, cols] = (dot_nn(k.T, ds) * FACTOR).T.astype(jnp.bfloat16)
        if late:
            keep = SPAN - BEFORE
            dk_ref[:keep, cols] = (dk[:keep] + dki_ref[:, cols].astype(jnp.float32)).astype(jnp.bfloat16)
            dv_ref[:keep, cols] = (dv[:keep] + dvi_ref[:, cols].astype(jnp.float32)).astype(jnp.bfloat16)
            dk_ref[keep:, cols] = dk[keep:TOK].astype(jnp.bfloat16)
            dv_ref[keep:, cols] = dv[keep:TOK].astype(jnp.bfloat16)
            halo_ref[0, :, cols] = dk[TOK:].astype(jnp.bfloat16)
            halo_ref[1, :, cols] = dv[TOK:].astype(jnp.bfloat16)
        else:
            dk_ref[:, cols] = dk[BEFORE:].astype(dk_ref.dtype)
            dv_ref[:, cols] = dv[BEFORE:].astype(dv_ref.dtype)
            halo_ref[0, :, cols] = dk[:BEFORE].astype(jnp.bfloat16)
            halo_ref[1, :, cols] = dv[:BEFORE].astype(jnp.bfloat16)

    ahead = products(0)
    behind = None
    for h in range(PER_STEP):
        now, ahead = ahead, products(h + 1) if h + 1 < PER_STEP else None
        done = differentiate(h, *now)
        if behind is not None:
            collect(h - 1, *behind)
        behind = done
    collect(PER_STEP - 1, *behind)


def backward(late, place, start, end, lse, q, near, far, k, v, halo, *earlier):
    row_block = 1 if late else 0
    halo_rows = AFTER if late else BEFORE
    own_rows = TOK if late else SPAN - BEFORE
    own_type = jnp.bfloat16 if late else jnp.float32
    bounds = pl.BlockSpec((1, BLOCK), lambda i, *_: (0, row_block))
    half = pl.BlockSpec((BLOCK, COLS // 2), lambda i, *_: (row_block, i))
    shape = jax.ShapeDtypeStruct
    return pl.pallas_call(
        functools.partial(backward_kernel, late=late),
        grid_spec=pltpu.PrefetchScalarGridSpec(
            num_scalar_prefetch=1,
            grid=(STEPS,),
            in_specs=[bounds, bounds, pl.BlockSpec((PER_STEP, 1, BLOCK), lambda i, *_: (i, 0, 0)),
                      columns(BLOCK, row_block=row_block), half, half,
                      columns(TOK), columns(halo_rows), columns(TOK), columns(halo_rows, STEPS)]
            + ([columns(SPAN - BEFORE)] * 2 + [pl.BlockSpec(memory_space=pl.ANY)] if late else []),
            out_specs=[columns(BLOCK, row_block=row_block), columns(own_rows), columns(own_rows), halo_columns(halo_rows)],
            scratch_shapes=[pltpu.VMEM((SPAN, BLOCK), jnp.float32), pltpu.VMEM((BLOCK, COLS), jnp.bfloat16)],
        ),
        out_shape=[shape((TOK, WIDTH), jnp.bfloat16),
                   shape((own_rows, WIDTH), own_type), shape((own_rows, WIDTH), own_type),
                   shape((2, halo_rows, WIDTH), jnp.bfloat16)],
        input_output_aliases={13: 0} if late else {},
        compiler_params=params(),
        cost_estimate=cost(10e9),
        name="grads_late" if late else "grads_early",
    )(place, start, end, lse, q, near, far, k, halo, v, halo, *earlier)


def finish_kernel(dk_ref, dv_ref, next_ref, prev_ref, dko_ref, dvo_ref):
    f32 = jnp.float32
    for i, own_ref, out_ref in ((0, dk_ref, dko_ref), (1, dv_ref, dvo_ref)):
        out_ref[:AFTER] = (own_ref[:AFTER].astype(f32) + prev_ref[i].astype(f32)).astype(jnp.bfloat16)
        out_ref[AFTER:TOK - BEFORE] = own_ref[AFTER:TOK - BEFORE]
        out_ref[TOK - BEFORE:] = (own_ref[TOK - BEFORE:].astype(f32) + next_ref[i].astype(f32)).astype(jnp.bfloat16)


def finish(dk, dv, from_next, from_prev):
    return pl.pallas_call(
        finish_kernel,
        grid=(STEPS,),
        in_specs=[columns(TOK), columns(TOK), halo_columns(BEFORE), halo_columns(AFTER)],
        out_specs=[columns(TOK)] * 2,
        out_shape=[jax.ShapeDtypeStruct((TOK, WIDTH), jnp.bfloat16)] * 2,
        compiler_params=params(),
        cost_estimate=cost(4e9),
        name="finish_grads",
    )(dk, dv, from_next, from_prev)


def weight_sums_kernel(core_ref, early_ref, late_ref, peer_early_ref, peer_late_ref, cot_ref, cot_peer_ref, out_ref):
    own = jnp.concatenate([early_ref[...], late_ref[...]], axis=0)
    peer = jnp.concatenate([peer_early_ref[...], peer_late_ref[...]], axis=0)
    core = core_ref[0]
    parts = [jnp.where(core == 0, own[:, 2 * j * HEAD_DIM:(2 * j + 1) * HEAD_DIM],
                       own[:, (2 * j + 1) * HEAD_DIM:(2 * j + 2) * HEAD_DIM]) for j in range(2)]
    own = jnp.concatenate(parts, axis=1)
    out_ref[...] = (dot_tn(own, cot_ref[...]) + dot_tn(peer, cot_peer_ref[...])).astype(jnp.bfloat16)


def weight_sums(core, early, late, peer_early, peer_late, cot, cot_peer):
    own_spec = pl.BlockSpec((BLOCK, 4 * HEAD_DIM), lambda i, *_: (0, i))
    peer_spec = pl.BlockSpec((BLOCK, 2 * HEAD_DIM), lambda i, *_: (0, i))
    return pl.pallas_call(
        weight_sums_kernel,
        grid_spec=pltpu.PrefetchScalarGridSpec(
            num_scalar_prefetch=1,
            grid=(4,),
            in_specs=[own_spec, own_spec, peer_spec, peer_spec, fixed((TOK, WIDTH)), fixed((TOK, WIDTH))],
            out_specs=pl.BlockSpec((2 * HEAD_DIM, WIDTH), lambda i, *_: (i, 0)),
        ),
        out_shape=jax.ShapeDtypeStruct((WIDTH // 2, WIDTH), jnp.bfloat16),
        compiler_params=params(),
        cost_estimate=cost(7e9),
        name="weight_sums",
    )(core, early, late, peer_early, peer_late, cot, cot_peer)


def grad_attn_kernel(place_ref, cot_ref, mine_ref, other_ref, out_ref, rows_ref):
    core = place_ref[0]
    rows_ref[:, core] = mine_ref[...]
    rows_ref[:, 1 - core] = other_ref[...]
    out_ref[...] = dot_nt(cot_ref[...], rows_ref[...].reshape(4 * HEAD_DIM, WIDTH)).astype(jnp.bfloat16)


def grad_attention(far, place, cot, mine, other):
    piece = pl.BlockSpec((2, HEAD_DIM, WIDTH), lambda i, *_: (i, 0, 0))
    return pl.pallas_call(
        grad_attn_kernel,
        grid_spec=pltpu.PrefetchScalarGridSpec(
            num_scalar_prefetch=1,
            grid=(2,),
            in_specs=[fixed((TOK, WIDTH)), piece, piece],
            out_specs=pl.BlockSpec((TOK, 4 * HEAD_DIM), lambda i, *_: (0, i)),
            scratch_shapes=[pltpu.VMEM((2, 2, HEAD_DIM, WIDTH), jnp.bfloat16)],
        ),
        out_shape=jax.ShapeDtypeStruct((TOK, WIDTH // 2), jnp.bfloat16),
        compiler_params=params(),
        cost_estimate=cost(7e9),
        name="grad_far" if far else "grad_near",
    )(place, cot, mine, other)


def place_weights(place_ref, refs, rows_ref):
    core = place_ref[0]
    zh = place_ref[1]
    near_ref, far_ref, near_other_ref, far_other_ref = refs
    rows_ref[:, zh, core] = near_ref[...]
    rows_ref[:, 1 - zh, core] = far_ref[...]
    rows_ref[:, zh, 1 - core] = near_other_ref[...]
    rows_ref[:, 1 - zh, 1 - core] = far_other_ref[...]


def project_kernel(place_ref, early_ref, late_ref, *refs):
    *weights, out_ref, rows_ref = refs
    place_weights(place_ref, weights, rows_ref)
    weight = rows_ref[...].reshape(WIDTH, out_ref.shape[1])
    out_ref[:BLOCK] = dot_nn(early_ref[...], weight).astype(jnp.bfloat16)
    out_ref[BLOCK:] = dot_nn(late_ref[...], weight).astype(jnp.bfloat16)


def project(place, early, late, *weights):
    tile = 512
    piece = pl.BlockSpec((4, HEAD_DIM, tile), lambda i, *_: (0, 0, i))
    return pl.pallas_call(
        project_kernel,
        grid_spec=pltpu.PrefetchScalarGridSpec(
            num_scalar_prefetch=1,
            grid=(WIDTH // tile,),
            in_specs=[fixed((BLOCK, WIDTH)), fixed((BLOCK, WIDTH))] + [piece] * 4,
            out_specs=pl.BlockSpec((TOK, tile), lambda i, *_: (0, i)),
            scratch_shapes=[pltpu.VMEM((4, 2, 2, HEAD_DIM, tile), jnp.bfloat16)],
        ),
        out_shape=jax.ShapeDtypeStruct((TOK, WIDTH), jnp.bfloat16),
        compiler_params=params(),
        cost_estimate=cost(8e9),
        name="project",
    )(place, early, late, *weights)


def sum_pieces_kernel(pieces_ref, out_ref):
    total = pieces_ref[0].astype(jnp.float32)
    for i in range(1, pieces_ref.shape[0]):
        total += pieces_ref[i].astype(jnp.float32)
    total = total.astype(jnp.bfloat16)
    for i in range(out_ref.shape[0]):
        out_ref[i] = total


def sum_pieces(pieces, copies):
    count, rows, width = pieces.shape
    tile = 512
    return pl.pallas_call(
        sum_pieces_kernel,
        grid=(width // tile,),
        in_specs=[pl.BlockSpec((count, rows, tile), lambda i: (0, 0, i))],
        out_specs=pl.BlockSpec((copies, rows, tile), lambda i: (0, 0, i)),
        out_shape=jax.ShapeDtypeStruct((copies, rows, width), jnp.bfloat16),
        compiler_params=params(),
        cost_estimate=cost(2e9),
        name="sum_pieces",
    )(pieces)


def swapped(array):
    return lax.ppermute(array, "core", [(0, 1), (1, 0)])


def passed_along(array, by):
    devices = 16
    pairs = [(i, i + by) for i in range(devices) if 0 <= i + by < devices]
    return lax.ppermute(array, GROUP_AXES, pairs)


def across_z(array):
    return lax.ppermute(array, ("zh", "zl"), [(z, 3 - z) for z in range(4)])


def tied(array, *others):
    return lax.optimization_barrier((array, *others))[0]


def on_device(query_rows, key_rows, value_rows, pyramid_start, scale_end, out_weight, cotangent):
    core = lax.axis_index("core").astype(jnp.int32)
    group_index = lax.axis_index(GROUP_AXES).astype(jnp.int32)
    core_arg = core.reshape(1)
    place = jnp.stack([core, lax.axis_index("zh").astype(jnp.int32)])
    start = (pyramid_start - group_index * TOK).reshape(1, TOK)
    end = (scale_end - group_index * TOK).reshape(1, TOK)

    after_rows = jnp.concatenate([key_rows[:AFTER], value_rows[:AFTER]], axis=1)
    after = passed_along(after_rows, -1)
    half = lax.dynamic_slice_in_dim(tied(out_weight, after_rows), core * HEAD_DIM, HEAD_DIM, 0)
    far_half = across_z(half)
    near_halves = jnp.broadcast_to(half, (4, HEAD_DIM, WIDTH))
    near = lax.all_to_all(near_halves, "y", 0, 0, tiled=True)
    before_rows = jnp.concatenate([key_rows[TOK - BEFORE:], value_rows[TOK - BEFORE:]], axis=1)
    before_rows = tied(before_rows, near_halves, after)
    before = passed_along(before_rows, 1)
    cot_peer = swapped(tied(cotangent, half))

    late, late_theirs, late_lse = forward(True, core_arg, start, end, tied(query_rows, far_half), key_rows, value_rows, after)
    far_half = tied(far_half, near, late)
    far = lax.all_to_all(jnp.broadcast_to(far_half, (4, HEAD_DIM, WIDTH)), "y", 0, 0, tiled=True)
    peer_late = swapped(late_theirs)
    early, early_theirs, early_lse = forward(False, core_arg, start, end, query_rows, key_rows, value_rows, before)
    peer_early = swapped(early_theirs)
    near_other = swapped(tied(near, late))
    sums = weight_sums(core_arg, early, late, peer_early, peer_late, cotangent, tied(cot_peer, near_other))
    grad_near = grad_attention(False, place, tied(cotangent, sums), near, near_other)
    far = tied(far, grad_near)
    sums = tied(sums.reshape(4, 2 * HEAD_DIM, WIDTH), far)
    pieces = lax.all_to_all(sums, "y", 0, 0, tiled=True)

    far_other = swapped(far)
    grad_far = grad_attention(True, place, cotangent, far, far_other)
    weights = (near, far, near_other, far_other)
    dq, dk0, dv0, halo = backward(
        False, place, start, end, early_lse, query_rows, grad_near, grad_far, key_rows, value_rows, before)
    from_next = passed_along(halo, -1)
    dq, dk1, dv1, halo = backward(
        True, place, start, end, late_lse, query_rows, grad_near, grad_far, key_rows, value_rows, after, dk0, dv0, dq)
    from_prev = passed_along(halo, 1)

    layer_out = project(place, tied(early, dk1), late, *weights)
    partial = sum_pieces(tied(pieces, layer_out), 1).reshape(16, 16, WIDTH)
    shares = lax.all_to_all(partial, ("zh", "x", "zl"), 0, 0, tiled=True)
    key_grad, value_grad = finish(tied(dk1, partial), dv1, from_next, from_prev)
    summed = sum_pieces(tied(shares, key_grad), 8)
    rows_mine = lax.all_to_all(summed, ("x", "zl"), 0, 0, tiled=True).reshape(HEAD_DIM, WIDTH)
    rows_other = swapped(rows_mine)
    first = jnp.where(core == 0, rows_mine, rows_other)
    second = jnp.where(core == 0, rows_other, rows_mine)
    weight_grad = jnp.concatenate([first, second], axis=0).astype(jnp.float32) * (float(TOKENS) ** -0.5)
    return (layer_out, dq, key_grad, value_grad, weight_grad)


def solution(mesh):
    inner = Mesh(mesh.devices.reshape(SIZES), AXES)
    rows = P(AXES, None)
    shard = P(("y", "zh"), None)
    return jax.shard_map(
        on_device,
        mesh=inner,
        in_specs=(rows, rows, rows, P(AXES), P(AXES), shard, rows),
        out_specs=(rows, rows, rows, rows, shard),
        check_vma=False,
    )
```

time: 278 us -> 182 us (0.65)
  waiting for transfers between devices: 109 us -> 23.5 us
  blocking collectives: 20.8 us -> 10.6 us
  starting transfers between devices: 52.2 us -> 44 us
  Pallas kernels: 77.6 us -> 84.8 us
    ppermute x6 -> x4, waiting for transfers between devices: 53.9 us -> 3.12 us  [passed_along(): return lax.ppermute(array, GROUP_AXES, pairs)]
    all_to_all x2 -> x4, waiting for transfers between devices: 53.5 us -> 12.9 us  [the longest x1 8.98 us: on_device(): shares = lax.all_to_all(partial, ('zh', 'x', 'zl'), 0, 0, tiled=True)]
    all_to_all x2 -> x4, starting transfers between devices: 34 us -> 22.8 us  [the longest x1 8.9 us: on_device(): shares = lax.all_to_all(partial, ('zh', 'x', 'zl'), 0, 0, tiled=True)]
    all_to_all x1, blocking collectives: 20.8 us -> 10.6 us  [on_device(): lax.all_to_all(summed, ('x', 'zl'), 0, 0, tiled=True)]
    ppermute x6 -> x4, starting transfers between devices: 17.5 us -> 11.1 us  [passed_along(): return lax.ppermute(array, GROUP_AXES, pairs)]
    ppermute x4 -> x6, starting transfers between devices: 0.68 us -> 6.22 us  [swapped(): return lax.ppermute(array, 'core', [(0, 1), (1, 0)])]
    pallas_call x2, Pallas kernels: 21 us -> 15.8 us  [forward(): pl.pallas_call(functools.partial(forward_kernel, late=late), grid_spec=pl...]
    ppermute x0 -> x1, waiting for transfers between devices: none -> 4.79 us  [across_z(): return lax.ppermute(array, ('zh', 'zl'), [(z, 3 - z) for z in range(4)])]
  transfers between devices with their start and end apart: 12 -> 15, of which waited for: 6 -> 7; matrix products, arithmetic and copies ran while one was open for 2% -> 4% of each run, Pallas kernels for 19% -> 45%
where the time goes in v2:
time: 182 us; the launch traced here: 181 us
  Pallas kernels  84.8 us (47%)
  starting transfers between devices  44 us (24%)
  waiting for transfers between devices  23.5 us (13%)
  local copies, waits for them, and re-layouts  11.5 us (6%)
  blocking collectives  10.6 us (6%)
  other arithmetic  5.32 us (3%)
    pallas_call x2, Pallas kernels, backward(): pl.pallas_call(functools.partial(backward_kernel, late=late), grid_spec=p...  23.9 us
    pallas_call x2, Pallas kernels, forward(): pl.pallas_call(functools.partial(forward_kernel, late=late), grid_spec=pl...  15.8 us
    pallas_call x2, Pallas kernels, grad_attention(): pl.pallas_call(grad_attn_kernel, grid_spec=pltpu.PrefetchScalarGridSpec(n...  13.2 us
    ppermute x4, starting transfers between devices, passed_along(): return lax.ppermute(array, GROUP_AXES, pairs)  11.1 us
    all_to_all x1, blocking collectives, on_device(): lax.all_to_all(summed, ('x', 'zl'), 0, 0, tiled=True)  10.6 us
    pallas_call x1, Pallas kernels, project(): pl.pallas_call(project_kernel, grid_spec=pltpu.PrefetchScalarGridSpec(num...  9.84 us
    pallas_call x1, Pallas kernels, weight_sums(): pl.pallas_call(weight_sums_kernel, grid_spec=pltpu.PrefetchScalarGridSpec...  9.03 us
    all_to_all x1, waiting for transfers between devices, on_device(): shares = lax.all_to_all(partial, ('zh', 'x', 'zl'), 0, 0, tiled=True)  8.98 us
  transfers between devices with their start and end apart: 15, of which 7 were waited for; matrix products, arithmetic and copies ran while one was open for 4% of the time, Pallas kernels for 45%

profile of v2, /device:TPU:1, one launch (start us, length us, event | category | flops | bytes accessed | tf_op | source)
XLA Modules:
  0.0 180.7 jit_solution(4023279545170017415)
XLA Ops:
  3.2 3.3 %collective-permute-start = (bf16[128,4096]{1,0:T(8,128)(2,1)}, bf16[128,4096]{1,0:T(8,128)(2,1)S(1)}, u32[]{:S(2)}, u32[]{:S(2)}) collective-permute-start(bf16[128,4096]{1,0:T(8,128)(2,1)} %pad_maximum_fusion.1), channel_id=1, source_target_pairs={{1,0},{2,1},{3,2},{4,3},{5,4},{6,5},{7,6},{8,7},{9,8},{10,9},{11,1... | collective-permute-start | bytes 3145736 | tf_op jit(solution)/shard_map/ppermute | solution.py:390
  8.2 4.5 %all-to-all-start = ((bf16[4,128,2048]{2,1,0:T(8,128)(2,1)}), bf16[4,128,2048]{2,1,0:T(8,128)(2,1)}, u32[]{:S(2)}, u32[]{:S(2)}) async-start(bf16[4,128,2048]{2,1,0:T(8,128)(2,1)} %broadcast_in_dim.6), calls=%async_computation | async-start | bytes 4194304 | tf_op jit(solution)/shard_map/all_to_all | solution.py:414
  12.7 3.9 %collective-permute-start.2 = (bf16[128,2048]{1,0:T(8,128)(2,1)}, bf16[128,2048]{1,0:T(8,128)(2,1)}, u32[]{:S(2)}, u32[]{:S(2)}) collective-permute-start(bf16[128,2048]{1,0:T(8,128)(2,1)} %copy-done.7), channel_id=1, source_target_pairs={{0,18},{2,16},{16,2},{18,0},{1,19},{3,17},{17,3},{19,1},{4,22},{6,... | collective-permute-start | bytes 1572872 | tf_op jit(solution)/shard_map/ppermute | solution.py:394
  18.1 3.1 %collective-permute-done.kh_ref.vh_ref = bf16[128,4096]{1,0:T(8,128)(2,1)S(1)} collective-permute-done((bf16[128,4096]{1,0:T(8,128)(2,1)}, bf16[128,4096]{1,0:T(8,128)(2,1)S(1)}, u32[]{:S(2)}, u32[]{:S(2)}) %collective-permute-start) | collective-permute-done | bytes 1048608 | tf_op jit(solution)/shard_map/ppermute | solution.py:390
  24.4 4.8 %collective-permute-done.2 = bf16[128,2048]{1,0:T(8,128)(2,1)} collective-permute-done((bf16[128,2048]{1,0:T(8,128)(2,1)}, bf16[128,2048]{1,0:T(8,128)(2,1)}, u32[]{:S(2)}, u32[]{:S(2)}) %collective-permute-start.2) | collective-permute-done | bytes 524320 | tf_op jit(solution)/shard_map/ppermute | solution.py:394
  29.2 7.7 %attend_late.1 = (bf16[256,2048]{1,0:T(8,128)(2,1)}, bf16[256,1024]{1,0:T(8,128)(2,1)}, f32[16,1,256]{2,1,0:T(1,128)}) custom-call(s32[1]{0:T(128)} %bitcast.core_ref, s32[1,512]{1,0:T(1,128)} %bitcast.16, s32[1,512]{1,0:T(1,128)} %bitcast.12, bf16[512,2048]{1,0:T(8,128)(2,1)} %q_ref.6, bf16[512,2048]{1,0:T(8,128)(2,1)} %ko_ref.7, ...), custom_call_target="tpu_custom_call" | custom-call | flops 8000000 | tf_op jit(solution)/shard_map/attend_late/pallas_call | solution.py:134
  39.9 2.6 %broadcast_in_dim.7 = bf16[4,128,2048]{2,1,0:T(8,128)(2,1)} broadcast(bf16[128,2048]{1,0:T(8,128)(2,1)} %collective-permute-done.2), dimensions={1,2} | broadcast | bytes 2621440 | tf_op jit(solution)/shard_map/broadcast_in_dim | solution.py:422
  42.5 4.6 %all-to-all-start.1 = ((bf16[4,128,2048]{2,1,0:T(8,128)(2,1)}), bf16[4,128,2048]{2,1,0:T(8,128)(2,1)}, u32[]{:S(2)}, u32[]{:S(2)}) async-start(bf16[4,128,2048]{2,1,0:T(8,128)(2,1)} %broadcast_in_dim.7), calls=%async_computation.1 | async-start | bytes 4194304 | tf_op jit(solution)/shard_map/all_to_all | solution.py:422
  48.7 8.1 %attend_early.1 = (bf16[256,2048]{1,0:T(8,128)(2,1)}, bf16[256,1024]{1,0:T(8,128)(2,1)}, f32[16,1,256]{2,1,0:T(1,128)}) custom-call(s32[1]{0:T(128)} %bitcast.core_ref, s32[1,512]{1,0:T(1,128)} %bitcast.17, s32[1,512]{1,0:T(1,128)} %bitcast.13, bf16[512,2048]{1,0:T(8,128)(2,1)} %q_ref.6, bf16[512,2048]{1,0:T(8,128)(2,1)} %ko_ref.7, ...), custom_call_target="tpu_custom_call" | custom-call | flops 8000000 | tf_op jit(solution)/shard_map/attend_early/pallas_call | solution.py:134
  59.7 9.0 %weight_sums.1 = bf16[1024,2048]{1,0:T(8,128)(2,1)} custom-call(s32[1]{0:T(128)} %bitcast.core_ref, bf16[256,2048]{1,0:T(8,128)(2,1)} %get-tuple-element.54.early_ref, bf16[256,2048]{1,0:T(8,128)(2,1)} %get-tuple-element.40.late_ref, bf16[256,1024]{1,0:T(8,128)(2,1)} %copy-done.9, bf16[256,1024]{1,0:T(8,128)(2,1)} %copy-done.8, bf16[512,2048]{1,0:T(8,128)(2,1)} %cot_ref.4, ...), custom_call_target="tpu_custom_call" | custom-call | flops 7000000 | tf_op jit(solution)/shard_map/weight_sums/pallas_call | solution.py:282
  68.8 6.6 %grad_near.1.near_ref = bf16[512,1024]{1,0:T(8,128)(2,1)} custom-call(s32[2]{0:T(128)} %pad_add_fusion.place_ref, bf16[512,2048]{1,0:T(8,128)(2,1)} %cot_ref.4, bf16[4,128,2048]{2,1,0:T(8,128)(2,1)} %all-to-all-done.mine_ref.refs_0_, bf16[4,128,2048]{2,1,0:T(8,128)(2,1)} %collective-permute-done.6.other_ref.refs_2_), custom_call_target="tpu_custom_call" | custom-call | flops 7000000 | tf_op jit(solution)/shard_map/grad_near/pallas_call | solution.py:306
  75.8 4.9 %all-to-all-start.2 = ((bf16[4,256,2048]{2,1,0:T(8,128)(2,1)}), bf16[4,256,2048]{2,1,0:T(8,128)(2,1)}, u32[]{:S(2)}, u32[]{:S(2)}) async-start(bf16[4,256,2048]{2,1,0:T(8,128)(2,1)} %bitcast.9), calls=%async_computation.2 | async-start | bytes 8388608 | tf_op jit(solution)/shard_map/all_to_all | solution.py:431
  82.0 6.6 %grad_far.1.far_ref = bf16[512,1024]{1,0:T(8,128)(2,1)} custom-call(s32[2]{0:T(128)} %pad_add_fusion.place_ref, bf16[512,2048]{1,0:T(8,128)(2,1)} %cot_ref.4, bf16[4,128,2048]{2,1,0:T(8,128)(2,1)} %all-to-all-done.1.mine_ref.refs_1_, bf16[4,128,2048]{2,1,0:T(8,128)(2,1)} %copy-done.4), custom_call_target="tpu_custom_call" | custom-call | flops 7000000 | tf_op jit(solution)/shard_map/grad_far/pallas_call | solution.py:306
  88.6 11.8 %grads_early.1 = (bf16[512,2048]{1,0:T(8,128)(2,1)}, f32[384,2048]{1,0:T(8,128)}, f32[384,2048]{1,0:T(8,128)}, bf16[2,256,2048]{2,1,0:T(8,128)(2,1)}) custom-call(s32[2]{0:T(128)} %pad_add_fusion.place_ref, s32[1,512]{1,0:T(1,128)} %bitcast.18, s32[1,512]{1,0:T(1,128)} %bitcast.14, f32[16,1,256]{2,1,0:T(1,128)} %get-tuple-element.49.lse_ref, ...), custom_call_target="tpu_custom_call" | custom-call | flops 10000000 | tf_op jit(solution)/shard_map/grads_early/pallas_call | solution.py:226
  102.7 12.1 %grads_late.1 = (bf16[512,2048]{1,0:T(8,128)(2,1)}, bf16[512,2048]{1,0:T(8,128)(2,1)}, bf16[512,2048]{1,0:T(8,128)(2,1)}, bf16[2,128,2048]{2,1,0:T(8,128)(2,1)}) custom-call(s32[2]{0:T(128)} %pad_add_fusion.place_ref, s32[1,512]{1,0:T(1,128)} %bitcast.19, s32[1,512]{1,0:T(1,128)} %bitcast.15, ...), custom_call_target="tpu_custom_call", output_to_operand_aliasing={{0}: (13, {})} | custom-call | flops 10000000 | tf_op jit(solution)/shard_map/grads_late/pallas_call | solution.py:226
  114.7 3.6 %collective-permute-start.9 = (bf16[2,128,2048]{2,1,0:T(8,128)(2,1)}, bf16[2,128,2048]{2,1,0:T(8,128)(2,1)}, u32[]{:S(2)}, u32[]{:S(2)}) collective-permute-start(bf16[2,128,2048]{2,1,0:T(8,128)(2,1)} %get-tuple-element.61), channel_id=1, source_target_pairs={{0,1},{1,2},{2,3},{3,4},{4,5},{5,6},{6,7},{7,8},{8,9},{9,10},{10,1... | collective-permute-start | bytes 3145736 | tf_op jit(solution)/shard_map/ppermute | solution.py:390
  118.4 9.8 %project.1 = bf16[512,2048]{1,0:T(8,128)(2,1)} custom-call(s32[2]{0:T(128)} %pad_add_fusion.place_ref, bf16[256,2048]{1,0:T(8,128)(2,1)} %get-tuple-element.54.early_ref, bf16[256,2048]{1,0:T(8,128)(2,1)} %get-tuple-element.40.late_ref, bf16[4,128,2048]{2,1,0:T(8,128)(2,1)} %all-to-all-done.mine_ref.refs_0_, ...), custom_call_target="tpu_custom_call" | custom-call | flops 8000000 | tf_op jit(solution)/shard_map/project/pallas_call | solution.py:343
  129.5 4.2 %sum_pieces.2 = bf16[1,256,2048]{2,1,0:T(8,128)(2,1)} custom-call(bf16[4,256,2048]{2,1,0:T(8,128)(2,1)} %all-to-all-done.2.pieces_ref), custom_call_target="tpu_custom_call" | custom-call | flops 2000000 | tf_op jit(solution)/shard_map/sum_pieces/pallas_call | solution.py:371
  133.8 8.9 %all-to-all-start.3 = ((bf16[16,16,2048]{2,1,0:T(8,128)(2,1)}), bf16[16,16,2048]{2,1,0:T(8,128)(2,1)S(1)}, u32[]{:S(2)}, u32[]{:S(2)}) async-start(bf16[16,16,2048]{2,1,0:T(8,128)(2,1)} %bitcast.10), calls=%async_computation.3 | async-start | bytes 2097152 | tf_op jit(solution)/shard_map/all_to_all | solution.py:445
  144.1 5.4 %finish_grads.1 = (bf16[512,2048]{1,0:T(8,128)(2,1)}, bf16[512,2048]{1,0:T(8,128)(2,1)}) custom-call(bf16[512,2048]{1,0:T(8,128)(2,1)} %get-tuple-element.58.dk_ref, bf16[512,2048]{1,0:T(8,128)(2,1)} %get-tuple-element.59.dv_ref, bf16[2,256,2048]{2,1,0:T(8,128)(2,1)} %copy-done.6, bf16[2,128,2048]{2,1,0:T(8,128)(2,1)} %collective-permute-done.9.prev_ref), custom_call_target="tpu_custom_call" | custom-call | flops 4000000 | tf_op jit(solution)/shard_map/finish_grads/pallas_call | solution.py:257
  149.5 9.0 %all-to-all-done.3.pieces_ref = bf16[16,16,2048]{2,1,0:T(8,128)(2,1)S(1)} async-done(((bf16[16,16,2048]{2,1,0:T(8,128)(2,1)}), bf16[16,16,2048]{2,1,0:T(8,128)(2,1)S(1)}, u32[]{:S(2)}, u32[]{:S(2)}) %all-to-all-start.3) | async-done | bytes 1048608 | tf_op jit(solution)/shard_map/all_to_all | solution.py:445
  159.4 3.4 %sum_pieces.3 = bf16[8,16,2048]{2,1,0:T(8,128)(2,1)} custom-call(bf16[16,16,2048]{2,1,0:T(8,128)(2,1)} %copy-done.5), custom_call_target="tpu_custom_call" | custom-call | flops 2000000 | tf_op jit(solution)/shard_map/sum_pieces/pallas_call | solution.py:371
  162.8 10.6 %all_to_all.25 = bf16[8,16,2048]{2,1,0:T(8,128)(2,1)S(1)} all-to-all(bf16[8,16,2048]{2,1,0:T(8,128)(2,1)} %sum_pieces.3), channel_id=1, replica_groups=mesh['y'=4,'zh'=2,'x'=4,'zl'=2,'core'=2] {'x','zl'}, dimensions={0} | all-to-all | bytes 1048576 | tf_op jit(solution)/shard_map/all_to_all | solution.py:448
  173.4 4.1 %collective-permute-start.10 = (bf16[128,2048]{1,0:T(8,128)(2,1)S(1)}, bf16[128,2048]{1,0:T(8,128)(2,1)S(1)}, u32[]{:S(2)}, u32[]{:S(2)}) collective-permute-start(bf16[128,2048]{1,0:T(8,128)(2,1)S(1)} %bitcast.11), channel_id=1, source_target_pairs={{0,1},{1,0},{2,3},{3,2},{4,5},{5,4},{6,7},{7,6},{8,9},{9,8},{10,11... | collective-permute-start | bytes 1572872 | tf_op jit(solution)/shard_map/ppermute | solution.py:384
  (61 shorter events, 27.1 us)
Async XLA Ops:
  0.6 5.9 %copy-start = (bf16[256,2048]{1,0:T(8,128)(2,1)S(1)}, bf16[256,2048]{1,0:T(8,128)(2,1)}, u32[]{:S(2)}) copy-start(bf16[256,2048]{1,0:T(8,128)(2,1)} %param.12) | copy-start | bytes 3145732
  3.2 18.0 %collective-permute-start = (bf16[128,4096]{1,0:T(8,128)(2,1)}, bf16[128,4096]{1,0:T(8,128)(2,1)S(1)}, u32[]{:S(2)}, u32[]{:S(2)}) collective-permute-start(bf16[128,4096]{1,0:T(8,128)(2,1)} %pad_maximum_fusion.1), channel_id=1, source_target_pairs={{1,0},{2,1},{3,2},{4,3},{5,4},{6,5},{7,6},{8,7},{9,8},{10,9},{11,1... | collective-permute-start | bytes 3145736 | tf_op jit(solution)/shard_map/ppermute | solution.py:390
  6.6 1.6 copy-start.7
  8.2 31.3 %all-to-all-start = ((bf16[4,128,2048]{2,1,0:T(8,128)(2,1)}), bf16[4,128,2048]{2,1,0:T(8,128)(2,1)}, u32[]{:S(2)}, u32[]{:S(2)}) async-start(bf16[4,128,2048]{2,1,0:T(8,128)(2,1)} %broadcast_in_dim.6), calls=%async_computation | async-start | bytes 4194304 | tf_op jit(solution)/shard_map/all_to_all | solution.py:414
  12.7 4.0 %slice-start.1 = ((bf16[512,2048]{1,0:T(8,128)(2,1)}), bf16[256,2048]{1,0:T(8,128)(2,1)S(1)}, s32[]{:S(2)}) async-start(bf16[512,2048]{1,0:T(8,128)(2,1)} %ko_ref.7), calls=%async_computation.6 | async-start | bytes 2097152 | tf_op jit(solution)/shard_map/slice | solution.py:415
  12.7 3.9 %slice-start.3 = ((bf16[512,2048]{1,0:T(8,128)(2,1)}), bf16[256,2048]{1,0:T(8,128)(2,1)S(1)}, s32[]{:S(2)}) async-start(bf16[512,2048]{1,0:T(8,128)(2,1)} %vo_ref.7), calls=%async_computation.8 | async-start | bytes 2097152 | tf_op jit(solution)/shard_map/slice | solution.py:415
  12.7 16.5 %collective-permute-start.2 = (bf16[128,2048]{1,0:T(8,128)(2,1)}, bf16[128,2048]{1,0:T(8,128)(2,1)}, u32[]{:S(2)}, u32[]{:S(2)}) collective-permute-start(bf16[128,2048]{1,0:T(8,128)(2,1)} %copy-done.7), channel_id=1, source_target_pairs={{0,18},{2,16},{16,2},{18,0},{1,19},{3,17},{17,3},{19,1},{4,22},{6,... | collective-permute-start | bytes 1572872 | tf_op jit(solution)/shard_map/ppermute | solution.py:394
  16.6 7.2 %copy-start.10 = (s32[512]{0:T(512)S(1)}, s32[512]{0:T(512)}, u32[]{:S(2)}) copy-start(s32[512]{0:T(512)} %param.11) | copy-start | bytes 6148
  16.6 7.2 %copy-start.11 = (s32[512]{0:T(512)S(1)}, s32[512]{0:T(512)}, u32[]{:S(2)}) copy-start(s32[512]{0:T(512)} %param.10) | copy-start | bytes 6148
  21.2 8.0 %copy-start.3 = (bf16[128,4096]{1,0:T(8,128)(2,1)}, bf16[128,4096]{1,0:T(8,128)(2,1)S(1)}, u32[]{:S(2)}) copy-start(bf16[128,4096]{1,0:T(8,128)(2,1)S(1)} %collective-permute-done.kh_ref.vh_ref) | copy-start | bytes 3145732
  21.2 26.1 %collective-permute-start.1 = (bf16[256,4096]{1,0:T(8,128)(2,1)}, bf16[256,4096]{1,0:T(8,128)(2,1)S(1)}, u32[]{:S(2)}, u32[]{:S(2)}) collective-permute-start(bf16[256,4096]{1,0:T(8,128)(2,1)} %pad_maximum_fusion), channel_id=1, source_target_pairs={{0,1},{1,2},{2,3},{3,4},{4,5},{5,6},{6,7},{7,8},{8,9},{9,10},{10,1... | collective-permute-start | bytes 6291464 | tf_op jit(solution)/shard_map/ppermute | solution.py:390
  23.1 34.6 %collective-permute-start.5 = (bf16[512,2048]{1,0:T(8,128)(2,1)}, bf16[512,2048]{1,0:T(8,128)(2,1)}, u32[]{:S(2)}, u32[]{:S(2)}) collective-permute-start(bf16[512,2048]{1,0:T(8,128)(2,1)} %cot_ref.4), channel_id=1, source_target_pairs={{0,1},{1,0},{2,3},{3,2},{4,5},{5,4},{6,7},{7,6},{8,9},{9,8},{10,11... | collective-permute-start | bytes 6291464 | tf_op jit(solution)/shard_map/ppermute | solution.py:384
  39.5 18.2 %collective-permute-start.6 = (bf16[4,128,2048]{2,1,0:T(8,128)(2,1)}, bf16[4,128,2048]{2,1,0:T(8,128)(2,1)}, u32[]{:S(2)}, u32[]{:S(2)}) collective-permute-start(bf16[4,128,2048]{2,1,0:T(8,128)(2,1)} %all-to-all-done.mine_ref.refs_0_), channel_id=1, source_target_pairs={{0,1},{1,0},{2,3},{3,2},{4,5},{5,4},{6,7},{7,6},{8,9},{9,8},{10,11... | collective-permute-start | bytes 6291464 | tf_op jit(solution)/shard_map/ppermute | solution.py:384
  42.5 4.6 %copy-start.12 = (bf16[256,1024]{1,0:T(8,128)(2,1)S(1)}, bf16[256,1024]{1,0:T(8,128)(2,1)}, u32[]{:S(2)}) copy-start(bf16[256,1024]{1,0:T(8,128)(2,1)} %get-tuple-element.42) | copy-start | bytes 1572868
  42.5 32.9 %all-to-all-start.1 = ((bf16[4,128,2048]{2,1,0:T(8,128)(2,1)}), bf16[4,128,2048]{2,1,0:T(8,128)(2,1)}, u32[]{:S(2)}, u32[]{:S(2)}) async-start(bf16[4,128,2048]{2,1,0:T(8,128)(2,1)} %broadcast_in_dim.7), calls=%async_computation.1 | async-start | bytes 4194304 | tf_op jit(solution)/shard_map/all_to_all | solution.py:422
  47.1 10.6 %collective-permute-start.4 = (bf16[256,1024]{1,0:T(8,128)(2,1)S(1)}, bf16[256,1024]{1,0:T(8,128)(2,1)S(1)}, u32[]{:S(2)}, u32[]{:S(2)}) collective-permute-start(bf16[256,1024]{1,0:T(8,128)(2,1)S(1)} %copy-done.12), channel_id=1, source_target_pairs={{0,1},{1,0},{2,3},{3,2},{4,5},{5,4},{6,7},{7,6},{8,9},{9,8},{10,11... | collective-permute-start | bytes 1572872 | tf_op jit(solution)/shard_map/ppermute | solution.py:384
  56.7 2.2 %collective-permute-start.3 = (bf16[256,1024]{1,0:T(8,128)(2,1)}, bf16[256,1024]{1,0:T(8,128)(2,1)S(1)}, u32[]{:S(2)}, u32[]{:S(2)}) collective-permute-start(bf16[256,1024]{1,0:T(8,128)(2,1)} %get-tuple-element.41), channel_id=1, source_target_pairs={{0,1},{1,0},{2,3},{3,2},{4,5},{5,4},{6,7},{7,6},{8,9},{9,8},{10,11... | collective-permute-start | bytes 1572872 | tf_op jit(solution)/shard_map/ppermute | solution.py:384
  75.4 5.3 %collective-permute-start.7 = (bf16[4,128,2048]{2,1,0:T(8,128)(2,1)}, bf16[4,128,2048]{2,1,0:T(8,128)(2,1)S(1)}, u32[]{:S(2)}, u32[]{:S(2)}) collective-permute-start(bf16[4,128,2048]{2,1,0:T(8,128)(2,1)} %all-to-all-done.1.mine_ref.refs_1_), channel_id=1, source_target_pairs={{0,1},{1,0},{2,3},{3,2},{4,5},{5,4},{6,7},{7,6},{8,9},{9,8},{10,11... | collective-permute-start | bytes 6291464 | tf_op jit(solution)/shard_map/ppermute | solution.py:384
  75.8 53.8 %all-to-all-start.2 = ((bf16[4,256,2048]{2,1,0:T(8,128)(2,1)}), bf16[4,256,2048]{2,1,0:T(8,128)(2,1)}, u32[]{:S(2)}, u32[]{:S(2)}) async-start(bf16[4,256,2048]{2,1,0:T(8,128)(2,1)} %bitcast.9), calls=%async_computation.2 | async-start | bytes 8388608 | tf_op jit(solution)/shard_map/all_to_all | solution.py:431
  100.4 42.3 %collective-permute-start.8 = (bf16[2,256,2048]{2,1,0:T(8,128)(2,1)}, bf16[2,256,2048]{2,1,0:T(8,128)(2,1)S(1)}, u32[]{:S(2)}, u32[]{:S(2)}) collective-permute-start(bf16[2,256,2048]{2,1,0:T(8,128)(2,1)} %get-tuple-element.60), channel_id=1, source_target_pairs={{1,0},{2,1},{3,2},{4,3},{5,4},{6,5},{7,6},{8,7},{9,8},{10,9},{11,1... | collective-permute-start | bytes 6291464 | tf_op jit(solution)/shard_map/ppermute | solution.py:390
  114.7 28.0 %collective-permute-start.9 = (bf16[2,128,2048]{2,1,0:T(8,128)(2,1)}, bf16[2,128,2048]{2,1,0:T(8,128)(2,1)}, u32[]{:S(2)}, u32[]{:S(2)}) collective-permute-start(bf16[2,128,2048]{2,1,0:T(8,128)(2,1)} %get-tuple-element.61), channel_id=1, source_target_pairs={{0,1},{1,2},{2,3},{3,4},{4,5},{5,6},{6,7},{7,8},{8,9},{9,10},{10,1... | collective-permute-start | bytes 3145736 | tf_op jit(solution)/shard_map/ppermute | solution.py:390
  133.8 24.7 %all-to-all-start.3 = ((bf16[16,16,2048]{2,1,0:T(8,128)(2,1)}), bf16[16,16,2048]{2,1,0:T(8,128)(2,1)S(1)}, u32[]{:S(2)}, u32[]{:S(2)}) async-start(bf16[16,16,2048]{2,1,0:T(8,128)(2,1)} %bitcast.10), calls=%async_computation.3 | async-start | bytes 2097152 | tf_op jit(solution)/shard_map/all_to_all | solution.py:445
  173.4 5.6 %collective-permute-start.10 = (bf16[128,2048]{1,0:T(8,128)(2,1)S(1)}, bf16[128,2048]{1,0:T(8,128)(2,1)S(1)}, u32[]{:S(2)}, u32[]{:S(2)}) collective-permute-start(bf16[128,2048]{1,0:T(8,128)(2,1)S(1)} %bitcast.11), channel_id=1, source_target_pairs={{0,1},{1,0},{2,3},{3,2},{4,5},{5,4},{6,7},{7,6},{8,9},{9,8},{10,11... | collective-permute-start | bytes 1572872 | tf_op jit(solution)/shard_map/ppermute | solution.py:384
  179.1 1.7 copy-start.1
  (8 other events, 9.8 us)

commit v3 on v2

v3 whole, which is shorter than its diff:
```python
import functools

import jax
import jax.numpy as jnp
from jax import lax
from jax.experimental import pallas as pl
from jax.experimental.pallas import tpu as pltpu
from jax.sharding import Mesh, PartitionSpec as P

HEADS = 16
HEAD_DIM = 128
WIDTH = HEADS * HEAD_DIM
TOK = 512
BLOCK = 256
BEFORE = 256
AFTER = 128
SENT_AFTER = 112
SPAN = 640
FACTOR = HEAD_DIM ** -0.5
TOKENS = 65536

AXES = ("y", "zh", "x", "zl", "core")
SIZES = (4, 2, 4, 2, 2)
GROUP_AXES = ("x", "zl", "core")
MB = 1024 * 1024
PER_STEP = 4
STEPS = HEADS // PER_STEP
COLS = PER_STEP * HEAD_DIM


def dot_nt(left, right):
    return lax.dot_general(left, right, (((1,), (1,)), ((), ())), preferred_element_type=jnp.float32)


def dot_nn(left, right):
    return lax.dot_general(left, right, (((1,), (0,)), ((), ())), preferred_element_type=jnp.float32)


def dot_tn(left, right):
    return lax.dot_general(left, right, (((0,), (0,)), ((), ())), preferred_element_type=jnp.float32)


def fixed(shape):
    return pl.BlockSpec(shape, lambda i, *_: (0,) * len(shape))


def columns(rows, shift=0, row_block=0):
    return pl.BlockSpec((rows, COLS), lambda i, *_: (row_block, i + shift))


def halo_columns(rows):
    return pl.BlockSpec((2, rows, COLS), lambda i, *_: (0, 0, i))


def cost(flops):
    return pl.CostEstimate(flops=int(flops * 1e-3), bytes_accessed=0, transcendentals=0)


def params():
    return pltpu.CompilerParams(vmem_limit_bytes=56 * MB)


def fill_bias(late, start_ref, end_ref, bias_ref):
    first = 0 if late else -BEFORE
    pos = lax.broadcasted_iota(jnp.int32, (SPAN, BLOCK), 0) + first
    ok = (pos >= start_ref[...]) & (pos < end_ref[...])
    bias_ref[...] = jnp.where(ok, 0.0, -jnp.inf).astype(jnp.float32)


def gather_keys(late, own, halo):
    if late:
        return jnp.concatenate([own, halo], axis=0)
    return jnp.concatenate([halo, own[: SPAN - BEFORE]], axis=0)


HALVES = ((slice(0, 128), slice(0, 512)), (slice(128, 256), slice(128, 640)))


def assemble(first, second):
    none = jnp.zeros((SPAN - 512, 128), first.dtype)
    return jnp.concatenate([jnp.concatenate([first, none], axis=0), jnp.concatenate([none, second], axis=0)], axis=1)


def forward_kernel(core_ref, start_ref, end_ref, q_ref, ko_ref, kh_ref, vo_ref, vh_ref,
                   out_ref, theirs_ref, lse_ref, bias_ref, *, late):
    @pl.when(pl.program_id(0) == 0)
    def _():
        fill_bias(late, start_ref, end_ref, bias_ref)

    even = core_ref[0] == 0
    outs = []

    def head(h):
        return slice(h * HEAD_DIM, (h + 1) * HEAD_DIM)

    def scores(h):
        return dot_nt(gather_keys(late, ko_ref[:, head(h)], kh_ref[:, head(h)]), q_ref[:, head(h)])

    def weigh(s):
        parts = []
        for queries, keys in HALVES:
            part = s[keys, queries] + bias_ref[keys, queries]
            top = jnp.max(part, axis=0, keepdims=True)
            e = jnp.exp((part - top) * FACTOR)
            total = jnp.sum(e, axis=0, keepdims=True)
            parts.append((e.astype(jnp.bfloat16), top, total))
        first, second = parts
        return (assemble(first[0], second[0]), jnp.concatenate([first[1], second[1]], axis=1),
                jnp.concatenate([first[2], second[2]], axis=1))

    def mix(h, e, top, total):
        v = gather_keys(late, vo_ref[:, head(h)], vh_ref[:, head(h)])
        out = (dot_nn(v.T, e) * (1.0 / total)).T.astype(jnp.bfloat16)
        out_ref[:, head(h)] = out
        lse_ref[h] = top * FACTOR + jnp.log(total)
        outs.append(out)
        if h % 2:
            theirs_ref[:, head(h // 2)] = jnp.where(even, outs[h], outs[h - 1])

    ahead = scores(0)
    behind = None
    for h in range(PER_STEP):
        now, ahead = ahead, scores(h + 1) if h + 1 < PER_STEP else None
        weighed = weigh(now)
        if behind is not None:
            mix(h - 1, *behind)
        behind = weighed
    mix(PER_STEP - 1, *behind)


def forward(late, core, start, end, q, k, v, halo):
    row_block = 1 if late else 0
    halo_rows = AFTER if late else BEFORE
    bounds = pl.BlockSpec((1, BLOCK), lambda i, *_: (0, row_block))
    return pl.pallas_call(
        functools.partial(forward_kernel, late=late),
        grid_spec=pltpu.PrefetchScalarGridSpec(
            num_scalar_prefetch=1,
            grid=(STEPS,),
            in_specs=[bounds, bounds, columns(BLOCK, row_block=row_block),
                      columns(TOK), columns(halo_rows), columns(TOK), columns(halo_rows, STEPS)],
            out_specs=[columns(BLOCK),
                       pl.BlockSpec((BLOCK, COLS // 2), lambda i, *_: (0, i)),
                       pl.BlockSpec((PER_STEP, 1, BLOCK), lambda i, *_: (i, 0, 0))],
            scratch_shapes=[pltpu.VMEM((SPAN, BLOCK), jnp.float32)],
        ),
        out_shape=[jax.ShapeDtypeStruct((BLOCK, WIDTH), jnp.bfloat16),
                   jax.ShapeDtypeStruct((BLOCK, WIDTH // 2), jnp.bfloat16),
                   jax.ShapeDtypeStruct((HEADS, 1, BLOCK), jnp.float32)],
        compiler_params=params(),
        cost_estimate=cost(8e9),
        name="attend_late" if late else "attend_early",
    )(core, start, end, q, k, halo, v, halo)


def backward_kernel(start_ref, end_ref, lse_early_ref, lse_late_ref, q_ref, g_ref, ko_ref, kb_ref, ka_ref,
                    vo_ref, vb_ref, va_ref, *refs):
    dq_ref, dk_ref, dv_ref, before_ref, after_ref, bias_ref = refs[-6:]

    @pl.when(pl.program_id(0) == 0)
    def _():
        for late in (False, True):
            block = slice(BLOCK, 2 * BLOCK) if late else slice(0, BLOCK)
            fill_bias(late, start_ref.at[:, block], end_ref.at[:, block], bias_ref.at[int(late)])

    def head(h):
        return slice(h * HEAD_DIM, (h + 1) * HEAD_DIM)

    def products(h, late):
        cols = head(h)
        halves = (ka_ref, va_ref) if late else (kb_ref, vb_ref)
        k = gather_keys(late, ko_ref[:, cols], halves[0][:, cols])
        v = gather_keys(late, vo_ref[:, cols], halves[1][:, cols])
        q = q_ref[late * BLOCK:(late + 1) * BLOCK, cols]
        g = g_ref[late * BLOCK:(late + 1) * BLOCK, cols]
        return k, q, g, [(dot_nt(k[keys], q[queries]), dot_nt(v[keys], g[queries])) for queries, keys in HALVES]

    def differentiate(h, late, k, q, g, pairs):
        lse_ref = lse_late_ref if late else lse_early_ref
        probs = []
        grads = []
        for (queries, keys), (s, dp) in zip(HALVES, pairs):
            p = jnp.exp((s + bias_ref[late, keys, queries]) * FACTOR - lse_ref[h, :, queries])
            inner = jnp.sum(p * dp, axis=0, keepdims=True)
            probs.append(p.astype(jnp.bfloat16))
            grads.append((p * (dp - inner)).astype(jnp.bfloat16))
        return k, q, g, assemble(*probs), assemble(*grads)

    early = {}

    def collect(h, late, k, q, g, p, ds):
        cols = head(h)
        dv = dot_nn(p, g)
        dk = dot_nn(ds, q) * FACTOR
        dq_ref[late * BLOCK:(late + 1) * BLOCK, cols] = (dot_nn(k.T, ds) * FACTOR).T.astype(jnp.bfloat16)
        if not late:
            early[h] = dk, dv
            before_ref[0, :, cols] = dk[:BEFORE].astype(jnp.bfloat16)
            before_ref[1, :, cols] = dv[:BEFORE].astype(jnp.bfloat16)
            return
        keep = SPAN - BEFORE
        for out_ref, first, second, i in ((dk_ref, early[h][0], dk, 0), (dv_ref, early[h][1], dv, 1)):
            out_ref[:keep, cols] = (first[BEFORE:] + second[:keep]).astype(jnp.bfloat16)
            out_ref[keep:, cols] = second[keep:TOK].astype(jnp.bfloat16)
            after_ref[i, :, cols] = second[TOK:TOK + SENT_AFTER].astype(jnp.bfloat16)

    units = [(h, late) for h in range(PER_STEP) for late in (0, 1)]
    ahead = products(*units[0])
    behind = None
    for i, unit in enumerate(units):
        now, ahead = ahead, products(*units[i + 1]) if i + 1 < len(units) else None
        done = differentiate(*unit, *now)
        if behind is not None:
            collect(*units[i - 1], *behind)
        behind = done
    collect(*units[-1], *behind)


def backward(half, start, end, lse_early, lse_late, q, g, k, v, before, after, *earlier):
    shape = jax.ShapeDtypeStruct
    steps = STEPS // 2
    first = half * steps
    lse = pl.BlockSpec((PER_STEP, 1, BLOCK), lambda i: (i + first, 0, 0))
    own = columns(TOK, first)
    return pl.pallas_call(
        backward_kernel,
        grid=(steps,),
        in_specs=[fixed((1, TOK)), fixed((1, TOK)), lse, lse, own, own,
                  own, columns(BEFORE, first), columns(AFTER, first),
                  own, columns(BEFORE, STEPS + first), columns(AFTER, STEPS + first)]
        + [pl.BlockSpec(memory_space=pl.ANY)] * len(earlier),
        out_specs=[own, own, own, halo_columns(BEFORE), halo_columns(SENT_AFTER)],
        out_shape=[shape((TOK, WIDTH), jnp.bfloat16)] * 3
        + [shape((2, BEFORE, WIDTH // 2), jnp.bfloat16), shape((2, SENT_AFTER, WIDTH // 2), jnp.bfloat16)],
        input_output_aliases={12 + i: i for i in range(len(earlier))},
        scratch_shapes=[pltpu.VMEM((2, SPAN, BLOCK), jnp.float32)],
        compiler_params=params(),
        cost_estimate=cost(10e9),
        name="attend_backward_second" if half else "attend_backward_first",
    )(start, end, lse_early, lse_late, q, g, k, before, after, v, before, after, *earlier)


def finish_kernel(dk_ref, dv_ref, first_ref, second_ref, dk_out_ref, dv_out_ref):
    def add(halo_ref):
        for i, own_ref, out_ref in ((0, dk_ref, dk_out_ref), (1, dv_ref, dv_out_ref)):
            total = own_ref[...].astype(jnp.float32) + halo_ref[i].astype(jnp.float32)
            out_ref[...] = total.astype(jnp.bfloat16)

    step = pl.program_id(0)
    pl.when(step < STEPS // 2)(lambda: add(first_ref))
    pl.when(step >= STEPS // 2)(lambda: add(second_ref))


def finish(dk, dv, first, second):
    rows = first.shape[1]
    half = STEPS // 2
    part = columns(rows, row_block=(TOK - rows) // rows if rows == BEFORE else 0)
    return pl.pallas_call(
        finish_kernel,
        grid=(STEPS,),
        in_specs=[part, part,
                  pl.BlockSpec((2, rows, COLS), lambda i: (0, 0, jnp.minimum(i, half - 1))),
                  pl.BlockSpec((2, rows, COLS), lambda i: (0, 0, jnp.maximum(i - half, 0)))],
        out_specs=[part, part],
        out_shape=[jax.ShapeDtypeStruct((TOK, WIDTH), jnp.bfloat16)] * 2,
        input_output_aliases={0: 0, 1: 1},
        compiler_params=params(),
        cost_estimate=cost(2e9),
        name="finish_grads",
    )(dk, dv, first, second)


def weight_sums_kernel(core_ref, early_ref, late_ref, peer_early_ref, peer_late_ref, cot_ref, cot_peer_ref, out_ref):
    own = jnp.concatenate([early_ref[...], late_ref[...]], axis=0)
    peer = jnp.concatenate([peer_early_ref[...], peer_late_ref[...]], axis=0)
    core = core_ref[0]
    parts = [jnp.where(core == 0, own[:, 2 * j * HEAD_DIM:(2 * j + 1) * HEAD_DIM],
                       own[:, (2 * j + 1) * HEAD_DIM:(2 * j + 2) * HEAD_DIM]) for j in range(4)]
    own = jnp.concatenate(parts, axis=1)
    out_ref[...] = (dot_tn(own, cot_ref[...]) + dot_tn(peer, cot_peer_ref[...])).astype(jnp.bfloat16)


def weight_sums(core, early, late, peer_early, peer_late, cot, cot_peer):
    own_spec = pl.BlockSpec((BLOCK, 8 * HEAD_DIM), lambda i, *_: (0, i))
    peer_spec = pl.BlockSpec((BLOCK, 4 * HEAD_DIM), lambda i, *_: (0, i))
    return pl.pallas_call(
        weight_sums_kernel,
        grid_spec=pltpu.PrefetchScalarGridSpec(
            num_scalar_prefetch=1,
            grid=(2,),
            in_specs=[own_spec, own_spec, peer_spec, peer_spec, fixed((TOK, WIDTH)), fixed((TOK, WIDTH))],
            out_specs=pl.BlockSpec((4 * HEAD_DIM, WIDTH), lambda i, *_: (i, 0)),
        ),
        out_shape=jax.ShapeDtypeStruct((WIDTH // 2, WIDTH), jnp.bfloat16),
        compiler_params=params(),
        cost_estimate=cost(7e9),
        name="weight_sums",
    )(core, early, late, peer_early, peer_late, cot, cot_peer)


def place_weights(place_ref, refs, rows_ref):
    core = place_ref[0]
    zh = place_ref[1]
    near_ref, far_ref, near_other_ref, far_other_ref = refs
    rows_ref[:, zh, core] = near_ref[...]
    rows_ref[:, 1 - zh, core] = far_ref[...]
    rows_ref[:, zh, 1 - core] = near_other_ref[...]
    rows_ref[:, 1 - zh, 1 - core] = far_other_ref[...]


def grad_attn_kernel(place_ref, cot_ref, *refs):
    *weights, out_ref, rows_ref = refs
    place_weights(place_ref, weights, rows_ref)
    out_ref[...] = dot_nt(cot_ref[...], rows_ref[...].reshape(4 * HEAD_DIM, WIDTH)).astype(jnp.bfloat16)


def grad_attention(place, cot, *weights):
    piece = pl.BlockSpec((1, HEAD_DIM, WIDTH), lambda i, *_: (i, 0, 0))
    return pl.pallas_call(
        grad_attn_kernel,
        grid_spec=pltpu.PrefetchScalarGridSpec(
            num_scalar_prefetch=1,
            grid=(4,),
            in_specs=[fixed((TOK, WIDTH))] + [piece] * 4,
            out_specs=pl.BlockSpec((TOK, 4 * HEAD_DIM), lambda i, *_: (0, i)),
            scratch_shapes=[pltpu.VMEM((1, 2, 2, HEAD_DIM, WIDTH), jnp.bfloat16)],
        ),
        out_shape=jax.ShapeDtypeStruct((TOK, WIDTH), jnp.bfloat16),
        compiler_params=params(),
        cost_estimate=cost(7e9),
        name="grad_attention",
    )(place, cot, *weights)


def project_kernel(place_ref, early_ref, late_ref, *refs):
    *weights, out_ref, rows_ref, attn_ref = refs

    @pl.when(pl.program_id(0) == 0)
    def _():
        attn_ref[:BLOCK] = early_ref[...]
        attn_ref[BLOCK:] = late_ref[...]

    place_weights(place_ref, weights, rows_ref)
    out_ref[...] = dot_nn(attn_ref[...], rows_ref[...].reshape(WIDTH, out_ref.shape[1])).astype(jnp.bfloat16)


def project(place, early, late, *weights):
    tile = 512
    piece = pl.BlockSpec((4, HEAD_DIM, tile), lambda i, *_: (0, 0, i))
    return pl.pallas_call(
        project_kernel,
        grid_spec=pltpu.PrefetchScalarGridSpec(
            num_scalar_prefetch=1,
            grid=(WIDTH // tile,),
            in_specs=[fixed((BLOCK, WIDTH)), fixed((BLOCK, WIDTH))] + [piece] * 4,
            out_specs=pl.BlockSpec((TOK, tile), lambda i, *_: (0, i)),
            scratch_shapes=[pltpu.VMEM((4, 2, 2, HEAD_DIM, tile), jnp.bfloat16), pltpu.VMEM((TOK, WIDTH), jnp.bfloat16)],
        ),
        out_shape=jax.ShapeDtypeStruct((TOK, WIDTH), jnp.bfloat16),
        compiler_params=params(),
        cost_estimate=cost(8e9),
        name="project",
    )(place, early, late, *weights)


def sum_pieces_kernel(pieces_ref, out_ref):
    total = pieces_ref[0].astype(jnp.float32)
    for i in range(1, pieces_ref.shape[0]):
        total += pieces_ref[i].astype(jnp.float32)
    total = total.astype(jnp.bfloat16)
    for i in range(out_ref.shape[0]):
        out_ref[i] = total


def sum_pieces(pieces, copies, tile):
    count, rows, width = pieces.shape
    return pl.pallas_call(
        sum_pieces_kernel,
        grid=(rows // tile,),
        in_specs=[pl.BlockSpec((count, tile, width), lambda i: (0, i, 0))],
        out_specs=pl.BlockSpec((copies, tile, width), lambda i: (0, i, 0)),
        out_shape=jax.ShapeDtypeStruct((copies, rows, width), jnp.bfloat16),
        compiler_params=params(),
        cost_estimate=cost(2e9),
        name="sum_pieces",
    )(pieces)


def swapped(array):
    return lax.ppermute(array, "core", [(0, 1), (1, 0)])


def passed_along(array, by):
    devices = 16
    pairs = [(i, i + by) for i in range(devices) if 0 <= i + by < devices]
    return lax.ppermute(array, GROUP_AXES, pairs)


def across_z(array):
    return lax.ppermute(array, ("zh", "zl"), [(z, 3 - z) for z in range(4)])


def tied(array, *others):
    return lax.optimization_barrier((array, *others))[0]


def on_device(query_rows, key_rows, value_rows, pyramid_start, scale_end, out_weight, cotangent):
    core = lax.axis_index("core").astype(jnp.int32)
    group_index = lax.axis_index(GROUP_AXES).astype(jnp.int32)
    core_arg = core.reshape(1)
    place = jnp.stack([core, lax.axis_index("zh").astype(jnp.int32)])
    start = (pyramid_start - group_index * TOK).reshape(1, TOK)
    end = (scale_end - group_index * TOK).reshape(1, TOK)

    half = lax.dynamic_slice_in_dim(out_weight, core * HEAD_DIM, HEAD_DIM, 0)
    near_halves = jnp.broadcast_to(half, (4, HEAD_DIM, WIDTH))
    near = lax.all_to_all(near_halves, "y", 0, 0, tiled=True)
    far_half = across_z(half)
    after_rows = jnp.concatenate([key_rows[:AFTER], value_rows[:AFTER]], axis=1)
    after_rows = tied(after_rows, near_halves)
    after = passed_along(after_rows, -1)
    before_rows = jnp.concatenate([key_rows[TOK - BEFORE:], value_rows[TOK - BEFORE:]], axis=1)
    before = passed_along(tied(before_rows, after_rows, after), 1)
    cot_peer = swapped(tied(cotangent, after_rows))
    far_halves = jnp.broadcast_to(far_half, (4, HEAD_DIM, WIDTH))

    late, late_theirs, late_lse = forward(
        True, core_arg, start, end, tied(query_rows, far_halves), key_rows, value_rows, after)
    far = lax.all_to_all(tied(far_halves, near, late), "y", 0, 0, tiled=True)
    peer_late = swapped(late_theirs)
    early, early_theirs, early_lse = forward(
        False, core_arg, start, end, tied(query_rows, peer_late), key_rows, value_rows, before)
    peer_early = swapped(early_theirs)
    near_other = swapped(tied(near, late))
    sums = weight_sums(core_arg, early, late, peer_early, peer_late, cotangent, tied(cot_peer, near_other))
    far = tied(far, sums)
    pieces = lax.all_to_all(tied(sums.reshape(4, 2 * HEAD_DIM, WIDTH), far), "y", 0, 0, tiled=True)
    far_other = swapped(far)
    weights = (near, far, near_other, far_other)
    grad_attn = grad_attention(place, tied(cotangent, far), *weights)
    shared = (start, end, early_lse, late_lse, query_rows, grad_attn, key_rows, value_rows, before, after)
    dq, dk, dv, to_previous, to_next = backward(0, *shared)
    from_next = [passed_along(to_previous, -1)]
    from_prev = [passed_along(to_next, 1)]
    dq, dk, dv, to_previous, to_next = backward(1, *shared, dq, dk, dv)
    from_next.append(passed_along(to_previous, -1))
    from_prev.append(passed_along(to_next, 1))

    partial = tied(sum_pieces(tied(pieces, dk), 1, 128), from_prev[0], from_next[0]).reshape(16, 16, WIDTH)
    shares = lax.all_to_all(partial, ("zh", "x", "zl"), 0, 0, tiled=True)
    layer_out = project(place, tied(early, partial, from_next[1]), late, *weights)
    summed = sum_pieces(tied(shares, layer_out), 8, 16)
    rows_mine = lax.all_to_all(summed, ("x", "zl"), 0, 0, tiled=True).reshape(HEAD_DIM, WIDTH)
    dk, dv = finish(tied(dk, summed), dv, *from_prev)
    key_grad, value_grad = finish(dk, dv, *from_next)
    rows_mine = tied(rows_mine, key_grad)
    rows_other = swapped(rows_mine)
    first = jnp.where(core == 0, rows_mine, rows_other)
    second = jnp.where(core == 0, rows_other, rows_mine)
    weight_grad = jnp.concatenate([first, second], axis=0).astype(jnp.float32) * (float(TOKENS) ** -0.5)
    return (layer_out, dq, key_grad, value_grad, weight_grad)


def solution(mesh):
    inner = Mesh(mesh.devices.reshape(SIZES), AXES)
    rows = P(AXES, None)
    shard = P(("y", "zh"), None)
    return jax.shard_map(
        on_device,
        mesh=inner,
        in_specs=(rows, rows, rows, P(AXES), P(AXES), shard, rows),
        out_specs=(rows, rows, rows, rows, shard),
        check_vma=False,
    )
```

time: 182 us -> 177 us (0.973)
  blocking collectives: 10.6 us -> 0 us
  starting transfers between devices: 44 us -> 51.7 us
  Pallas kernels: 84.8 us -> 79.1 us
  waiting for transfers between devices: 23.5 us -> 26.5 us
    all_to_all x1 -> x0, blocking collectives: 10.6 us -> none  [on_device(): lax.all_to_all(summed, ('x', 'zl'), 0, 0, tiled=True)]
    all_to_all x2 -> x3, waiting for transfers between devices: 1.34 us -> 10.7 us  [the longest x1 8.9 us: on_device(): lax.all_to_all(tied(sums.reshape(4, 2 * HEAD_DIM, WIDTH), far), 'y', 0, 0...]
    all_to_all x1, waiting for transfers between devices: 8.98 us -> 1.5 us  [on_device(): shares = lax.all_to_all(partial, ('zh', 'x', 'zl'), 0, 0, tiled=True)]
    ppermute x4 -> x6, starting transfers between devices: 11.1 us -> 17.3 us  [passed_along(): return lax.ppermute(array, GROUP_AXES, pairs)]
    all_to_all x2 -> x3, starting transfers between devices: 9.46 us -> 13 us  [the longest x1 5.04 us: on_device(): lax.all_to_all(tied(sums.reshape(4, 2 * HEAD_DIM, WIDTH), far), 'y', 0, 0...]
    pallas_call x2 -> x1, Pallas kernels: 13.2 us -> 10.1 us  [grad_attention(): pl.pallas_call(grad_attn_kernel, grid_spec=pltpu.PrefetchScalarGridSpec(n...]
    pallas_call x5 -> x6, Pallas kernels: 36.9 us -> 34.1 us  [the longest x2 20.4 us: backward(): pl.pallas_call(backward_kernel, grid=(steps,), in_specs=[fixed((1, TOK)),...]
    ppermute x6, waiting for transfers between devices: 2.71 us -> 5.38 us  [swapped(): return lax.ppermute(array, 'core', [(0, 1), (1, 0)])]
  transfers between devices with their start and end apart: 15 -> 18, of which waited for: 7 -> 9; matrix products, arithmetic and copies ran while one was open for 4% -> 3% of each run, Pallas kernels for 45% -> 45%
where the time goes in v3:
time: 177 us; the launch traced here: 175 us
  Pallas kernels  79.1 us (45%)
  starting transfers between devices  51.7 us (29%)
  waiting for transfers between devices  26.5 us (15%)
  local copies, waits for them, and re-layouts  12.5 us (7%)
  other arithmetic  4.43 us (3%)
    pallas_call x2, Pallas kernels, backward(): pl.pallas_call(backward_kernel, grid=(steps,), in_specs=[fixed((1, TOK)),...  20.4 us
    ppermute x6, starting transfers between devices, passed_along(): return lax.ppermute(array, GROUP_AXES, pairs)  17.3 us
    pallas_call x2, Pallas kernels, forward(): pl.pallas_call(functools.partial(forward_kernel, late=late), grid_spec=pl...  15.7 us
    pallas_call x1, Pallas kernels, grad_attention(): pl.pallas_call(grad_attn_kernel, grid_spec=pltpu.PrefetchScalarGridSpec(n...  10.1 us
    pallas_call x1, Pallas kernels, project(): pl.pallas_call(project_kernel, grid_spec=pltpu.PrefetchScalarGridSpec(num...  9.98 us
    pallas_call x1, Pallas kernels, weight_sums(): pl.pallas_call(weight_sums_kernel, grid_spec=pltpu.PrefetchScalarGridSpec...  9.2 us
    all_to_all x1, waiting for transfers between devices, on_device(): lax.all_to_all(tied(sums.reshape(4, 2 * HEAD_DIM, WIDTH), far), 'y', 0, 0...  8.9 us
    pallas_call x2, Pallas kernels, finish(): pl.pallas_call(finish_kernel, grid=(STEPS,), in_specs=[part, part, pl.Blo...  8.16 us
  transfers between devices with their start and end apart: 18, of which 9 were waited for; matrix products, arithmetic and copies ran while one was open for 3% of the time, Pallas kernels for 45%

profile of v3, /device:TPU:1, one launch (start us, length us, event | category | flops | bytes accessed | tf_op | source)
XLA Modules:
  0.0 175.2 jit_solution(14690226971200065123)
XLA Ops:
  2.8 2.6 %broadcast_in_dim.7 = bf16[4,128,2048]{2,1,0:T(8,128)(2,1)} broadcast(bf16[128,2048]{1,0:T(8,128)(2,1)} %constant_dynamic-slice_fusion), dimensions={1,2} | broadcast | bytes 2621440 | tf_op jit(solution)/shard_map/broadcast_in_dim | solution.py:416
  5.4 3.3 %collective-permute-start.1 = (bf16[128,4096]{1,0:T(8,128)(2,1)S(1)}, bf16[128,4096]{1,0:T(8,128)(2,1)}, u32[]{:S(2)}, u32[]{:S(2)}) collective-permute-start(bf16[128,4096]{1,0:T(8,128)(2,1)S(1)} %pad_maximum_fusion.1), channel_id=1, source_target_pairs={{1,0},{2,1},{3,2},{4,3},{5,4},{6,5},{7,6},{8,7},{9,8},{10,9},{11,1... | collective-permute-start | bytes 3145736 | tf_op jit(solution)/shard_map/ppermute | solution.py:396
  8.7 4.5 %all-to-all-start = ((bf16[4,128,2048]{2,1,0:T(8,128)(2,1)}), bf16[4,128,2048]{2,1,0:T(8,128)(2,1)}, u32[]{:S(2)}, u32[]{:S(2)}) async-start(bf16[4,128,2048]{2,1,0:T(8,128)(2,1)} %broadcast_in_dim.7), calls=%async_computation | async-start | bytes 4194304 | tf_op jit(solution)/shard_map/all_to_all | solution.py:417
  13.3 3.9 %collective-permute-start = (bf16[128,2048]{1,0:T(8,128)(2,1)}, bf16[128,2048]{1,0:T(8,128)(2,1)}, u32[]{:S(2)}, u32[]{:S(2)}) collective-permute-start(bf16[128,2048]{1,0:T(8,128)(2,1)} %constant_dynamic-slice_fusion), channel_id=1, source_target_pairs={{0,18},{2,16},{16,2},{18,0},{1,19},{3,17},{17,3},{19,1},{4,22},{6,... | collective-permute-start | bytes 1572872 | tf_op jit(solution)/shard_map/ppermute | solution.py:400
  18.7 4.5 %collective-permute-done.1.kh_ref.vh_ref.ka_ref.va_ref = bf16[128,4096]{1,0:T(8,128)(2,1)} collective-permute-done((bf16[128,4096]{1,0:T(8,128)(2,1)S(1)}, bf16[128,4096]{1,0:T(8,128)(2,1)}, u32[]{:S(2)}, u32[]{:S(2)}) %collective-permute-start.1) | collective-permute-done | bytes 1048608 | tf_op jit(solution)/shard_map/ppermute | solution.py:396
  26.4 3.3 %collective-permute-done = bf16[128,2048]{1,0:T(8,128)(2,1)} collective-permute-done((bf16[128,2048]{1,0:T(8,128)(2,1)}, bf16[128,2048]{1,0:T(8,128)(2,1)}, u32[]{:S(2)}, u32[]{:S(2)}) %collective-permute-start) | collective-permute-done | bytes 524320 | tf_op jit(solution)/shard_map/ppermute | solution.py:400
  32.4 7.8 %attend_late.1 = (bf16[256,2048]{1,0:T(8,128)(2,1)}, bf16[256,1024]{1,0:T(8,128)(2,1)}, f32[16,1,256]{2,1,0:T(1,128)}) custom-call(s32[1]{0:T(128)} %bitcast.core_ref, s32[1,512]{1,0:T(1,128)} %bitcast.15, s32[1,512]{1,0:T(1,128)} %bitcast.11, bf16[512,2048]{1,0:T(8,128)(2,1)} %q_ref.5, bf16[512,2048]{1,0:T(8,128)(2,1)} %ko_ref.7, ...), custom_call_target="tpu_custom_call" | custom-call | flops 8000000 | tf_op jit(solution)/shard_map/attend_late/pallas_call | solution.py:135
  40.9 4.4 %all-to-all-start.1 = ((bf16[4,128,2048]{2,1,0:T(8,128)(2,1)}), bf16[4,128,2048]{2,1,0:T(8,128)(2,1)}, u32[]{:S(2)}, u32[]{:S(2)}) async-start(bf16[4,128,2048]{2,1,0:T(8,128)(2,1)} %broadcast_in_dim.6), calls=%async_computation.1 | async-start | bytes 4194304 | tf_op jit(solution)/shard_map/all_to_all | solution.py:429
  49.7 7.9 %attend_early.1 = (bf16[256,2048]{1,0:T(8,128)(2,1)}, bf16[256,1024]{1,0:T(8,128)(2,1)}, f32[16,1,256]{2,1,0:T(1,128)}) custom-call(s32[1]{0:T(128)} %bitcast.core_ref, s32[1,512]{1,0:T(1,128)} %bitcast.16, s32[1,512]{1,0:T(1,128)} %bitcast.12, bf16[512,2048]{1,0:T(8,128)(2,1)} %q_ref.5, bf16[512,2048]{1,0:T(8,128)(2,1)} %ko_ref.7, ...), custom_call_target="tpu_custom_call" | custom-call | flops 8000000 | tf_op jit(solution)/shard_map/attend_early/pallas_call | solution.py:135
  60.7 9.2 %weight_sums.1 = bf16[1024,2048]{1,0:T(8,128)(2,1)} custom-call(s32[1]{0:T(128)} %bitcast.core_ref, bf16[256,2048]{1,0:T(8,128)(2,1)} %get-tuple-element.68.early_ref, bf16[256,2048]{1,0:T(8,128)(2,1)} %get-tuple-element.48.late_ref, bf16[256,1024]{1,0:T(8,128)(2,1)} %copy-done.7, bf16[256,1024]{1,0:T(8,128)(2,1)} %copy-done.6, bf16[512,2048]{1,0:T(8,128)(2,1)} %cot_ref.2, ...), custom_call_target="tpu_custom_call" | custom-call | flops 7000000 | tf_op jit(solution)/shard_map/weight_sums/pallas_call | solution.py:286
  72.7 5.0 %all-to-all-start.2 = ((bf16[4,256,2048]{2,1,0:T(8,128)(2,1)}), bf16[4,256,2048]{2,1,0:T(8,128)(2,1)}, u32[]{:S(2)}, u32[]{:S(2)}) async-start(bf16[4,256,2048]{2,1,0:T(8,128)(2,1)} %bitcast.7), calls=%async_computation.2 | async-start | bytes 8388608 | tf_op jit(solution)/shard_map/all_to_all | solution.py:437
  79.6 10.1 %grad_attention.1.g_ref = bf16[512,2048]{1,0:T(8,128)(2,1)} custom-call(s32[2]{0:T(128)} %pad_add_fusion.place_ref, bf16[512,2048]{1,0:T(8,128)(2,1)} %cot_ref.2, bf16[4,128,2048]{2,1,0:T(8,128)(2,1)} %all-to-all-done.refs_0_, bf16[4,128,2048]{2,1,0:T(8,128)(2,1)} %all-to-all-done.1.refs_1_, bf16[4,128,2048]{2,1,0:T(8,128)(2,1)} %collective-permute-done.6.refs_2_, ...), custom_call_target="tpu_custom_call" | custom-call | flops 7000000 | tf_op jit(solution)/shard_map/grad_attention/pallas_call | solution.py:319
  89.7 10.1 %attend_backward_first.1 = (bf16[512,2048]{1,0:T(8,128)(2,1)}, bf16[512,2048]{1,0:T(8,128)(2,1)}, bf16[512,2048]{1,0:T(8,128)(2,1)}, bf16[2,256,1024]{2,1,0:T(8,128)(2,1)}, bf16[2,112,1024]{2,1,0:T(8,128)(2,1)}) custom-call(s32[1,512]{1,0:T(1,128)} %bitcast.17, s32[1,512]{1,0:T(1,128)} %bitcast.13, f32[16,1,256]{2,1,0:T(1,128)} %get-tuple-element.56.lse_early_ref, ...), custom_call_target="tpu_custom_call" | custom-call | flops 10000000 | tf_op jit(solution)/shard_map/attend_backward_first/pallas_call | solution.py:225
  101.8 3.6 %collective-permute-start.8 = (bf16[2,112,1024]{2,1,0:T(8,128)(2,1)}, bf16[2,112,1024]{2,1,0:T(8,128)(2,1)S(1)}, u32[]{:S(2)}, u32[]{:S(2)}) collective-permute-start(bf16[2,112,1024]{2,1,0:T(8,128)(2,1)} %get-tuple-element.64), channel_id=1, source_target_pairs={{0,1},{1,2},{2,3},{3,4},{4,5},{5,6},{6,7},{7,8},{8,9},{9,10},{10,1... | collective-permute-start | bytes 1376264 | tf_op jit(solution)/shard_map/ppermute | solution.py:396
  105.4 10.3 %attend_backward_second.1 = (bf16[512,2048]{1,0:T(8,128)(2,1)}, bf16[512,2048]{1,0:T(8,128)(2,1)}, bf16[512,2048]{1,0:T(8,128)(2,1)}, bf16[2,256,1024]{2,1,0:T(8,128)(2,1)}, bf16[2,112,1024]{2,1,0:T(8,128)(2,1)}) custom-call(s32[1,512]{1,0:T(1,128)} %bitcast.18, s32[1,512]{1,0:T(1,128)} %bitcast.14, ...), custom_call_target="tpu_custom_call", output_to_operand_aliasing={{0}: (12, {}), {1}: (13, {}), {2}: (14, {})} | custom-call | flops 10000000 | tf_op jit(solution)/shard_map/attend_backward_second/pallas_call | solution.py:225
  117.7 8.9 %all-to-all-done.2.pieces_ref = bf16[4,256,2048]{2,1,0:T(8,128)(2,1)} async-done(((bf16[4,256,2048]{2,1,0:T(8,128)(2,1)}), bf16[4,256,2048]{2,1,0:T(8,128)(2,1)}, u32[]{:S(2)}, u32[]{:S(2)}) %all-to-all-start.2) | async-done | bytes 4194336 | tf_op jit(solution)/shard_map/all_to_all | solution.py:437
  126.6 3.3 %sum_pieces.2 = bf16[1,256,2048]{2,1,0:T(8,128)(2,1)} custom-call(bf16[4,256,2048]{2,1,0:T(8,128)(2,1)} %all-to-all-done.2.pieces_ref), custom_call_target="tpu_custom_call" | custom-call | flops 2000000 | tf_op jit(solution)/shard_map/sum_pieces/pallas_call | solution.py:377
  129.9 7.6 %all-to-all-start.3 = ((bf16[16,16,2048]{2,1,0:T(8,128)(2,1)}), bf16[16,16,2048]{2,1,0:T(8,128)(2,1)S(1)}, u32[]{:S(2)}, u32[]{:S(2)}) async-start(bf16[16,16,2048]{2,1,0:T(8,128)(2,1)} %bitcast.8), calls=%async_computation.3 | async-start | bytes 2097152 | tf_op jit(solution)/shard_map/all_to_all | solution.py:450
  137.5 4.5 %collective-permute-start.11 = (bf16[2,112,1024]{2,1,0:T(8,128)(2,1)}, bf16[2,112,1024]{2,1,0:T(8,128)(2,1)S(1)}, u32[]{:S(2)}, u32[]{:S(2)}) collective-permute-start(bf16[2,112,1024]{2,1,0:T(8,128)(2,1)} %get-tuple-element.73), channel_id=1, source_target_pairs={{0,1},{1,2},{2,3},{3,4},{4,5},{5,6},{6,7},{7,8},{8,9},{9,10},{10,1... | collective-permute-start | bytes 1376264 | tf_op jit(solution)/shard_map/ppermute | solution.py:396
  142.0 10.0 %project.1 = bf16[512,2048]{1,0:T(8,128)(2,1)} custom-call(s32[2]{0:T(128)} %pad_add_fusion.place_ref, bf16[256,2048]{1,0:T(8,128)(2,1)} %get-tuple-element.68.early_ref, bf16[256,2048]{1,0:T(8,128)(2,1)} %get-tuple-element.48.late_ref, bf16[4,128,2048]{2,1,0:T(8,128)(2,1)} %all-to-all-done.refs_0_, bf16[4,128,2048]{2,1,0:T(8,128)(2,1)} %all-to-all-done.1.refs_1_, ...), custom_call_target="tpu_custom_call" | custom-call | flops 8000000 | tf_op jit(solution)/shard_map/project/pallas_call | solution.py:350
  156.7 3.5 %all-to-all-start.4 = ((bf16[8,16,2048]{2,1,0:T(8,128)(2,1)}), bf16[8,16,2048]{2,1,0:T(8,128)(2,1)S(1)}, u32[]{:S(2)}, u32[]{:S(2)}) async-start(bf16[8,16,2048]{2,1,0:T(8,128)(2,1)} %sum_pieces.3), calls=%async_computation.4 | async-start | bytes 1048576 | tf_op jit(solution)/shard_map/all_to_all | solution.py:453
  161.0 3.7 %finish_grads.2 = (bf16[512,2048]{1,0:T(8,128)(2,1)}, bf16[512,2048]{1,0:T(8,128)(2,1)}) custom-call(bf16[512,2048]{1,0:T(8,128)(2,1)} %get-tuple-element.71.dk_ref, bf16[512,2048]{1,0:T(8,128)(2,1)} %get-tuple-element.72.dv_ref, bf16[2,112,1024]{2,1,0:T(8,128)(2,1)} %copy-done.8, ...), custom_call_target="tpu_custom_call", output_to_operand_aliasing={{0}: (0, {}), {1}: (1, {})} | custom-call | flops 2000000 | tf_op jit(solution)/shard_map/finish_grads/pallas_call | solution.py:258
  164.7 4.4 %finish_grads.3 = (bf16[512,2048]{1,0:T(8,128)(2,1)}, bf16[512,2048]{1,0:T(8,128)(2,1)}) custom-call(bf16[512,2048]{1,0:T(8,128)(2,1)} %get-tuple-element.74.dk_ref, bf16[512,2048]{1,0:T(8,128)(2,1)} %get-tuple-element.75.dv_ref, bf16[2,256,1024]{2,1,0:T(8,128)(2,1)} %copy-done.5, ...), custom_call_target="tpu_custom_call", output_to_operand_aliasing={{0}: (0, {}), {1}: (1, {})} | custom-call | flops 2000000 | tf_op jit(solution)/shard_map/finish_grads/pallas_call | solution.py:258
  169.2 2.8 %collective-permute-start.12 = (bf16[128,2048]{1,0:T(8,128)(2,1)S(1)}, bf16[128,2048]{1,0:T(8,128)(2,1)S(1)}, u32[]{:S(2)}, u32[]{:S(2)}) collective-permute-start(bf16[128,2048]{1,0:T(8,128)(2,1)S(1)} %bitcast.9), channel_id=1, source_target_pairs={{0,1},{1,0},{2,3},{3,2},{4,5},{5,4},{6,7},{7,6},{8,9},{9,8},{10,11... | collective-permute-start | bytes 1572872 | tf_op jit(solution)/shard_map/ppermute | solution.py:390
  (66 shorter events, 34.7 us)
Async XLA Ops:
  5.4 17.8 %collective-permute-start.1 = (bf16[128,4096]{1,0:T(8,128)(2,1)S(1)}, bf16[128,4096]{1,0:T(8,128)(2,1)}, u32[]{:S(2)}, u32[]{:S(2)}) collective-permute-start(bf16[128,4096]{1,0:T(8,128)(2,1)S(1)} %pad_maximum_fusion.1), channel_id=1, source_target_pairs={{1,0},{2,1},{3,2},{4,3},{5,4},{6,5},{7,6},{8,7},{9,8},{10,9},{11,1... | collective-permute-start | bytes 3145736 | tf_op jit(solution)/shard_map/ppermute | solution.py:396
  8.7 31.5 %all-to-all-start = ((bf16[4,128,2048]{2,1,0:T(8,128)(2,1)}), bf16[4,128,2048]{2,1,0:T(8,128)(2,1)}, u32[]{:S(2)}, u32[]{:S(2)}) async-start(bf16[4,128,2048]{2,1,0:T(8,128)(2,1)} %broadcast_in_dim.7), calls=%async_computation | async-start | bytes 4194304 | tf_op jit(solution)/shard_map/all_to_all | solution.py:417
  13.3 16.5 %collective-permute-start = (bf16[128,2048]{1,0:T(8,128)(2,1)}, bf16[128,2048]{1,0:T(8,128)(2,1)}, u32[]{:S(2)}, u32[]{:S(2)}) collective-permute-start(bf16[128,2048]{1,0:T(8,128)(2,1)} %constant_dynamic-slice_fusion), channel_id=1, source_target_pairs={{0,18},{2,16},{16,2},{18,0},{1,19},{3,17},{17,3},{19,1},{4,22},{6,... | collective-permute-start | bytes 1572872 | tf_op jit(solution)/shard_map/ppermute | solution.py:400
  17.2 8.7 %copy-start.10 = (s32[512]{0:T(512)S(1)}, s32[512]{0:T(512)}, u32[]{:S(2)}) copy-start(s32[512]{0:T(512)} %param.11) | copy-start | bytes 6148
  17.2 8.7 %copy-start.11 = (s32[512]{0:T(512)S(1)}, s32[512]{0:T(512)}, u32[]{:S(2)}) copy-start(s32[512]{0:T(512)} %param.10) | copy-start | bytes 6148
  23.2 25.2 %collective-permute-start.3 = (bf16[256,4096]{1,0:T(8,128)(2,1)}, bf16[256,4096]{1,0:T(8,128)(2,1)S(1)}, u32[]{:S(2)}, u32[]{:S(2)}) collective-permute-start(bf16[256,4096]{1,0:T(8,128)(2,1)} %pad_maximum_fusion), channel_id=1, source_target_pairs={{0,1},{1,2},{2,3},{3,4},{4,5},{5,6},{6,7},{7,8},{8,9},{9,10},{10,1... | collective-permute-start | bytes 6291464 | tf_op jit(solution)/shard_map/ppermute | solution.py:396
  25.1 32.6 %collective-permute-start.5 = (bf16[512,2048]{1,0:T(8,128)(2,1)}, bf16[512,2048]{1,0:T(8,128)(2,1)}, u32[]{:S(2)}, u32[]{:S(2)}) collective-permute-start(bf16[512,2048]{1,0:T(8,128)(2,1)} %cot_ref.2), channel_id=1, source_target_pairs={{0,1},{1,0},{2,3},{3,2},{4,5},{5,4},{6,7},{7,6},{8,9},{9,8},{10,11... | collective-permute-start | bytes 6291464 | tf_op jit(solution)/shard_map/ppermute | solution.py:390
  40.2 5.1 %copy-start.12 = (bf16[256,1024]{1,0:T(8,128)(2,1)S(1)}, bf16[256,1024]{1,0:T(8,128)(2,1)}, u32[]{:S(2)}) copy-start(bf16[256,1024]{1,0:T(8,128)(2,1)} %get-tuple-element.44) | copy-start | bytes 1572868
  40.2 17.6 %collective-permute-start.6 = (bf16[4,128,2048]{2,1,0:T(8,128)(2,1)}, bf16[4,128,2048]{2,1,0:T(8,128)(2,1)}, u32[]{:S(2)}, u32[]{:S(2)}) collective-permute-start(bf16[4,128,2048]{2,1,0:T(8,128)(2,1)} %all-to-all-done.refs_0_), channel_id=1, source_target_pairs={{0,1},{1,0},{2,3},{3,2},{4,5},{5,4},{6,7},{7,6},{8,9},{9,8},{10,11... | collective-permute-start | bytes 6291464 | tf_op jit(solution)/shard_map/ppermute | solution.py:390
  40.9 30.8 %all-to-all-start.1 = ((bf16[4,128,2048]{2,1,0:T(8,128)(2,1)}), bf16[4,128,2048]{2,1,0:T(8,128)(2,1)}, u32[]{:S(2)}, u32[]{:S(2)}) async-start(bf16[4,128,2048]{2,1,0:T(8,128)(2,1)} %broadcast_in_dim.6), calls=%async_computation.1 | async-start | bytes 4194304 | tf_op jit(solution)/shard_map/all_to_all | solution.py:429
  45.3 2.0 %collective-permute-start.2 = (bf16[256,1024]{1,0:T(8,128)(2,1)S(1)}, bf16[256,1024]{1,0:T(8,128)(2,1)S(1)}, u32[]{:S(2)}, u32[]{:S(2)}) collective-permute-start(bf16[256,1024]{1,0:T(8,128)(2,1)S(1)} %copy-done.12), channel_id=1, source_target_pairs={{0,1},{1,0},{2,3},{3,2},{4,5},{5,4},{6,7},{7,6},{8,9},{9,8},{10,11... | collective-permute-start | bytes 1572872 | tf_op jit(solution)/shard_map/ppermute | solution.py:390
  47.3 12.5 %copy-start.6 = (bf16[256,1024]{1,0:T(8,128)(2,1)}, bf16[256,1024]{1,0:T(8,128)(2,1)S(1)}, u32[]{:S(2)}) copy-start(bf16[256,1024]{1,0:T(8,128)(2,1)S(1)} %collective-permute-done.2.peer_late_ref) | copy-start | bytes 1572868
  57.7 2.2 %collective-permute-start.4 = (bf16[256,1024]{1,0:T(8,128)(2,1)}, bf16[256,1024]{1,0:T(8,128)(2,1)S(1)}, u32[]{:S(2)}, u32[]{:S(2)}) collective-permute-start(bf16[256,1024]{1,0:T(8,128)(2,1)} %get-tuple-element.49), channel_id=1, source_target_pairs={{0,1},{1,0},{2,3},{3,2},{4,5},{5,4},{6,7},{7,6},{8,9},{9,8},{10,11... | collective-permute-start | bytes 1572872 | tf_op jit(solution)/shard_map/ppermute | solution.py:390
  71.7 6.7 %collective-permute-start.7 = (bf16[4,128,2048]{2,1,0:T(8,128)(2,1)}, bf16[4,128,2048]{2,1,0:T(8,128)(2,1)S(1)}, u32[]{:S(2)}, u32[]{:S(2)}) collective-permute-start(bf16[4,128,2048]{2,1,0:T(8,128)(2,1)} %all-to-all-done.1.refs_1_), channel_id=1, source_target_pairs={{0,1},{1,0},{2,3},{3,2},{4,5},{5,4},{6,7},{7,6},{8,9},{9,8},{10,11... | collective-permute-start | bytes 6291464 | tf_op jit(solution)/shard_map/ppermute | solution.py:390
  72.7 53.9 %all-to-all-start.2 = ((bf16[4,256,2048]{2,1,0:T(8,128)(2,1)}), bf16[4,256,2048]{2,1,0:T(8,128)(2,1)}, u32[]{:S(2)}, u32[]{:S(2)}) async-start(bf16[4,256,2048]{2,1,0:T(8,128)(2,1)} %bitcast.7), calls=%async_computation.2 | async-start | bytes 8388608 | tf_op jit(solution)/shard_map/all_to_all | solution.py:437
  99.9 30.0 %collective-permute-start.9 = (bf16[2,256,1024]{2,1,0:T(8,128)(2,1)}, bf16[2,256,1024]{2,1,0:T(8,128)(2,1)S(1)}, u32[]{:S(2)}, u32[]{:S(2)}) collective-permute-start(bf16[2,256,1024]{2,1,0:T(8,128)(2,1)} %get-tuple-element.65), channel_id=1, source_target_pairs={{1,0},{2,1},{3,2},{4,3},{5,4},{6,5},{7,6},{8,7},{9,8},{10,9},{11,1... | collective-permute-start | bytes 3145736 | tf_op jit(solution)/shard_map/ppermute | solution.py:396
  101.8 28.1 %collective-permute-start.8 = (bf16[2,112,1024]{2,1,0:T(8,128)(2,1)}, bf16[2,112,1024]{2,1,0:T(8,128)(2,1)S(1)}, u32[]{:S(2)}, u32[]{:S(2)}) collective-permute-start(bf16[2,112,1024]{2,1,0:T(8,128)(2,1)} %get-tuple-element.64), channel_id=1, source_target_pairs={{0,1},{1,2},{2,3},{3,4},{4,5},{5,6},{6,7},{7,8},{8,9},{9,10},{10,1... | collective-permute-start | bytes 1376264 | tf_op jit(solution)/shard_map/ppermute | solution.py:396
  115.7 26.3 %collective-permute-start.10 = (bf16[2,256,1024]{2,1,0:T(8,128)(2,1)}, bf16[2,256,1024]{2,1,0:T(8,128)(2,1)}, u32[]{:S(2)}, u32[]{:S(2)}) collective-permute-start(bf16[2,256,1024]{2,1,0:T(8,128)(2,1)} %get-tuple-element.67), channel_id=1, source_target_pairs={{1,0},{2,1},{3,2},{4,3},{5,4},{6,5},{7,6},{8,7},{9,8},{10,9},{11,1... | collective-permute-start | bytes 3145736 | tf_op jit(solution)/shard_map/ppermute | solution.py:396
  129.9 22.1 %copy-start.8 = (bf16[2,112,1024]{2,1,0:T(8,128)(2,1)}, bf16[2,112,1024]{2,1,0:T(8,128)(2,1)S(1)}, u32[]{:S(2)}) copy-start(bf16[2,112,1024]{2,1,0:T(8,128)(2,1)S(1)} %collective-permute-done.8.first_ref) | copy-start | bytes 1376260
  129.9 22.1 %copy-start.5 = (bf16[2,256,1024]{2,1,0:T(8,128)(2,1)}, bf16[2,256,1024]{2,1,0:T(8,128)(2,1)S(1)}, u32[]{:S(2)}) copy-start(bf16[2,256,1024]{2,1,0:T(8,128)(2,1)S(1)} %collective-permute-done.9.first_ref) | copy-start | bytes 3145732
  129.9 23.6 %all-to-all-start.3 = ((bf16[16,16,2048]{2,1,0:T(8,128)(2,1)}), bf16[16,16,2048]{2,1,0:T(8,128)(2,1)S(1)}, u32[]{:S(2)}, u32[]{:S(2)}) async-start(bf16[16,16,2048]{2,1,0:T(8,128)(2,1)} %bitcast.8), calls=%async_computation.3 | async-start | bytes 2097152 | tf_op jit(solution)/shard_map/all_to_all | solution.py:450
  137.5 22.7 %collective-permute-start.11 = (bf16[2,112,1024]{2,1,0:T(8,128)(2,1)}, bf16[2,112,1024]{2,1,0:T(8,128)(2,1)S(1)}, u32[]{:S(2)}, u32[]{:S(2)}) collective-permute-start(bf16[2,112,1024]{2,1,0:T(8,128)(2,1)} %get-tuple-element.73), channel_id=1, source_target_pairs={{0,1},{1,2},{2,3},{3,4},{4,5},{5,6},{6,7},{7,8},{8,9},{9,10},{10,1... | collective-permute-start | bytes 1376264 | tf_op jit(solution)/shard_map/ppermute | solution.py:396
  156.7 12.5 %all-to-all-start.4 = ((bf16[8,16,2048]{2,1,0:T(8,128)(2,1)}), bf16[8,16,2048]{2,1,0:T(8,128)(2,1)S(1)}, u32[]{:S(2)}, u32[]{:S(2)}) async-start(bf16[8,16,2048]{2,1,0:T(8,128)(2,1)} %sum_pieces.3), calls=%async_computation.4 | async-start | bytes 1048576 | tf_op jit(solution)/shard_map/all_to_all | solution.py:453
  169.2 4.4 %collective-permute-start.12 = (bf16[128,2048]{1,0:T(8,128)(2,1)S(1)}, bf16[128,2048]{1,0:T(8,128)(2,1)S(1)}, u32[]{:S(2)}, u32[]{:S(2)}) collective-permute-start(bf16[128,2048]{1,0:T(8,128)(2,1)S(1)} %bitcast.9), channel_id=1, source_target_pairs={{0,1},{1,0},{2,3},{3,2},{4,5},{5,4},{6,7},{7,6},{8,9},{9,8},{10,11... | collective-permute-start | bytes 1572872 | tf_op jit(solution)/shard_map/ppermute | solution.py:390
  (11 other events, 20.0 us)

commit v4 on v3

--- a/solution.py
+++ b/solution.py
@@ -240,34 +240,64 @@
     )(start, end, lse_early, lse_late, q, g, k, before, after, v, before, after, *earlier)
 
 
-def finish_kernel(dk_ref, dv_ref, first_ref, second_ref, dk_out_ref, dv_out_ref):
-    def add(halo_ref):
+def finish_kernel(dk_ref, dv_ref, prev_first_ref, prev_second_ref, next_first_ref, next_second_ref,
+                  dk_out_ref, dv_out_ref):
+    def add(prev_ref, next_ref):
+        f32 = jnp.float32
+        last = TOK - BEFORE
         for i, own_ref, out_ref in ((0, dk_ref, dk_out_ref), (1, dv_ref, dv_out_ref)):
-            total = own_ref[...].astype(jnp.float32) + halo_ref[i].astype(jnp.float32)
-            out_ref[...] = total.astype(jnp.bfloat16)
+            head = own_ref[:SENT_AFTER].astype(f32) + prev_ref[i].astype(f32)
+            tail = own_ref[last:].astype(f32) + next_ref[i].astype(f32)
+            out_ref[:SENT_AFTER] = head.astype(jnp.bfloat16)
+            out_ref[SENT_AFTER:last] = own_ref[SENT_AFTER:last]
+            out_ref[last:] = tail.astype(jnp.bfloat16)
 
     step = pl.program_id(0)
-    pl.when(step < STEPS // 2)(lambda: add(first_ref))
-    pl.when(step >= STEPS // 2)(lambda: add(second_ref))
-
-
-def finish(dk, dv, first, second):
-    rows = first.shape[1]
+    pl.when(step < STEPS // 2)(lambda: add(prev_first_ref, next_first_ref))
+    pl.when(step >= STEPS // 2)(lambda: add(prev_second_ref, next_second_ref))
+
+
+def finish(dk, dv, from_prev, from_next):
     half = STEPS // 2
-    part = columns(rows, row_block=(TOK - rows) // rows if rows == BEFORE else 0)
+
+    def halo(rows, shift):
+        return pl.BlockSpec((2, rows, COLS), lambda i: (0, 0, jnp.clip(i - shift, 0, half - 1)))
+
     return pl.pallas_call(
         finish_kernel,
         grid=(STEPS,),
-        in_specs=[part, part,
-                  pl.BlockSpec((2, rows, COLS), lambda i: (0, 0, jnp.minimum(i, half - 1))),
-                  pl.BlockSpec((2, rows, COLS), lambda i: (0, 0, jnp.maximum(i - half, 0)))],
-        out_specs=[part, part],
+        in_specs=[columns(TOK), columns(TOK), halo(SENT_AFTER, 0), halo(SENT_AFTER, half), halo(BEFORE, 0), halo(BEFORE, half)],
+        out_specs=[columns(TOK)] * 2,
         out_shape=[jax.ShapeDtypeStruct((TOK, WIDTH), jnp.bfloat16)] * 2,
-        input_output_aliases={0: 0, 1: 1},
         compiler_params=params(),
         cost_estimate=cost(2e9),
         name="finish_grads",
-    )(dk, dv, first, second)
+    )(dk, dv, *from_prev, *from_next)
+
+
+def scale_kernel(core_ref, mine_ref, other_ref, out_ref):
+    core = core_ref[0]
+    scale = float(TOKENS) ** -0.5
+    out_ref[core] = mine_ref[...].astype(jnp.float32) * scale
+    out_ref[1 - core] = other_ref[...].astype(jnp.float32) * scale
+
+
+def scale_rows(core, mine, other):
+    tile = 1024
+    rows = pl.BlockSpec((HEAD_DIM, tile), lambda i, *_: (0, i))
+    return pl.pallas_call(
+        scale_kernel,
+        grid_spec=pltpu.PrefetchScalarGridSpec(
+            num_scalar_prefetch=1,
+            grid=(WIDTH // tile,),
+            in_specs=[rows, rows],
+            out_specs=pl.BlockSpec((2, HEAD_DIM, tile), lambda i, *_: (0, 0, i)),
+        ),
+        out_shape=jax.ShapeDtypeStruct((2, HEAD_DIM, WIDTH), jnp.float32),
+        compiler_params=params(),
+        cost_estimate=cost(1e9),
+        name="scale_rows",
+    )(core, mine, other).reshape(2 * HEAD_DIM, WIDTH)
 
 
 def weight_sums_kernel(core_ref, early_ref, late_ref, peer_early_ref, peer_late_ref, cot_ref, cot_peer_ref, out_ref):
@@ -451,13 +481,9 @@
     layer_out = project(place, tied(early, partial, from_next[1]), late, *weights)
     summed = sum_pieces(tied(shares, layer_out), 8, 16)
     rows_mine = lax.all_to_all(summed, ("x", "zl"), 0, 0, tiled=True).reshape(HEAD_DIM, WIDTH)
-    dk, dv = finish(tied(dk, summed), dv, *from_prev)
-    key_grad, value_grad = finish(dk, dv, *from_next)
+    key_grad, value_grad = finish(tied(dk, summed), dv, from_prev, from_next)
     rows_mine = tied(rows_mine, key_grad)
-    rows_other = swapped(rows_mine)
-    first = jnp.where(core == 0, rows_mine, rows_other)
-    second = jnp.where(core == 0, rows_other, rows_mine)
-    weight_grad = jnp.concatenate([first, second], axis=0).astype(jnp.float32) * (float(TOKENS) ** -0.5)
+    weight_grad = scale_rows(core_arg, rows_mine, swapped(rows_mine))
     return (layer_out, dq, key_grad, value_grad, weight_grad)
 
 

time: 177 us -> 177 us (level)
    unnamed x26 -> x30, local copies, waits for them, and re-layouts: 6.39 us -> 7.21 us
  transfers between devices with their start and end apart: 18 -> 18, of which waited for: 9 -> 10; matrix products, arithmetic and copies ran while one was open for 3% -> 3% of each run, Pallas kernels for 45% -> 44%
where the time goes in v4:
time: 177 us; the launch traced here: 176 us
  Pallas kernels  79.1 us (45%)
  starting transfers between devices  52.6 us (30%)
  waiting for transfers between devices  27 us (15%)
  local copies, waits for them, and re-layouts  13.3 us (8%)
  other arithmetic  2.81 us (2%)
    pallas_call x2, Pallas kernels, backward(): pl.pallas_call(backward_kernel, grid=(steps,), in_specs=[fixed((1, TOK)),...  20.5 us
    ppermute x6, starting transfers between devices, passed_along(): return lax.ppermute(array, GROUP_AXES, pairs)  17.3 us
    pallas_call x2, Pallas kernels, forward(): pl.pallas_call(functools.partial(forward_kernel, late=late), grid_spec=pl...  15.9 us
    pallas_call x1, Pallas kernels, grad_attention(): pl.pallas_call(grad_attn_kernel, grid_spec=pltpu.PrefetchScalarGridSpec(n...  10.1 us
    pallas_call x1, Pallas kernels, project(): pl.pallas_call(project_kernel, grid_spec=pltpu.PrefetchScalarGridSpec(num...  9.98 us
    pallas_call x1, Pallas kernels, weight_sums(): pl.pallas_call(weight_sums_kernel, grid_spec=pltpu.PrefetchScalarGridSpec...  9.15 us
    all_to_all x1, waiting for transfers between devices, on_device(): lax.all_to_all(tied(sums.reshape(4, 2 * HEAD_DIM, WIDTH), far), 'y', 0, 0...  8.73 us
    all_to_all x1, starting transfers between devices, on_device(): shares = lax.all_to_all(partial, ('zh', 'x', 'zl'), 0, 0, tiled=True)  7.47 us
  transfers between devices with their start and end apart: 18, of which 10 were waited for; matrix products, arithmetic and copies ran while one was open for 3% of the time, Pallas kernels for 44%

profile of v4, /device:TPU:1, one launch (start us, length us, event | category | flops | bytes accessed | tf_op | source)
XLA Modules:
  0.0 175.8 jit_solution(2938283435275868841)
XLA Ops:
  2.8 2.6 %broadcast_in_dim.7 = bf16[4,128,2048]{2,1,0:T(8,128)(2,1)} broadcast(bf16[128,2048]{1,0:T(8,128)(2,1)} %constant_dynamic-slice_fusion), dimensions={1,2} | broadcast | bytes 2621440 | tf_op jit(solution)/shard_map/broadcast_in_dim | solution.py:446
  5.4 3.3 %collective-permute-start.1 = (bf16[128,4096]{1,0:T(8,128)(2,1)S(1)}, bf16[128,4096]{1,0:T(8,128)(2,1)}, u32[]{:S(2)}, u32[]{:S(2)}) collective-permute-start(bf16[128,4096]{1,0:T(8,128)(2,1)S(1)} %pad_maximum_fusion.1), channel_id=1, source_target_pairs={{1,0},{2,1},{3,2},{4,3},{5,4},{6,5},{7,6},{8,7},{9,8},{10,9},{11,1... | collective-permute-start | bytes 3145736 | tf_op jit(solution)/shard_map/ppermute | solution.py:426
  8.7 4.5 %all-to-all-start = ((bf16[4,128,2048]{2,1,0:T(8,128)(2,1)}), bf16[4,128,2048]{2,1,0:T(8,128)(2,1)}, u32[]{:S(2)}, u32[]{:S(2)}) async-start(bf16[4,128,2048]{2,1,0:T(8,128)(2,1)} %broadcast_in_dim.7), calls=%async_computation | async-start | bytes 4194304 | tf_op jit(solution)/shard_map/all_to_all | solution.py:447
  13.3 3.9 %collective-permute-start = (bf16[128,2048]{1,0:T(8,128)(2,1)}, bf16[128,2048]{1,0:T(8,128)(2,1)}, u32[]{:S(2)}, u32[]{:S(2)}) collective-permute-start(bf16[128,2048]{1,0:T(8,128)(2,1)} %constant_dynamic-slice_fusion), channel_id=1, source_target_pairs={{0,18},{2,16},{16,2},{18,0},{1,19},{3,17},{17,3},{19,1},{4,22},{6,... | collective-permute-start | bytes 1572872 | tf_op jit(solution)/shard_map/ppermute | solution.py:430
  18.7 4.5 %collective-permute-done.1.kh_ref.vh_ref.ka_ref.va_ref = bf16[128,4096]{1,0:T(8,128)(2,1)} collective-permute-done((bf16[128,4096]{1,0:T(8,128)(2,1)S(1)}, bf16[128,4096]{1,0:T(8,128)(2,1)}, u32[]{:S(2)}, u32[]{:S(2)}) %collective-permute-start.1) | collective-permute-done | bytes 1048608 | tf_op jit(solution)/shard_map/ppermute | solution.py:426
  26.4 3.4 %collective-permute-done = bf16[128,2048]{1,0:T(8,128)(2,1)} collective-permute-done((bf16[128,2048]{1,0:T(8,128)(2,1)}, bf16[128,2048]{1,0:T(8,128)(2,1)}, u32[]{:S(2)}, u32[]{:S(2)}) %collective-permute-start) | collective-permute-done | bytes 524320 | tf_op jit(solution)/shard_map/ppermute | solution.py:430
  29.8 2.6 %broadcast_in_dim.6 = bf16[4,128,2048]{2,1,0:T(8,128)(2,1)} broadcast(bf16[128,2048]{1,0:T(8,128)(2,1)} %collective-permute-done), dimensions={1,2} | broadcast | bytes 2621440 | tf_op jit(solution)/shard_map/broadcast_in_dim | solution.py:455
  32.4 7.9 %attend_late.1 = (bf16[256,2048]{1,0:T(8,128)(2,1)}, bf16[256,1024]{1,0:T(8,128)(2,1)}, f32[16,1,256]{2,1,0:T(1,128)}) custom-call(s32[1]{0:T(128)} %bitcast.core_ref, s32[1,512]{1,0:T(1,128)} %bitcast.17, s32[1,512]{1,0:T(1,128)} %bitcast.13, bf16[512,2048]{1,0:T(8,128)(2,1)} %q_ref.5, bf16[512,2048]{1,0:T(8,128)(2,1)} %ko_ref.7, ...), custom_call_target="tpu_custom_call" | custom-call | flops 8000000 | tf_op jit(solution)/shard_map/attend_late/pallas_call | solution.py:135
  41.0 4.4 %all-to-all-start.1 = ((bf16[4,128,2048]{2,1,0:T(8,128)(2,1)}), bf16[4,128,2048]{2,1,0:T(8,128)(2,1)}, u32[]{:S(2)}, u32[]{:S(2)}) async-start(bf16[4,128,2048]{2,1,0:T(8,128)(2,1)} %broadcast_in_dim.6), calls=%async_computation.1 | async-start | bytes 4194304 | tf_op jit(solution)/shard_map/all_to_all | solution.py:459
  49.7 8.0 %attend_early.1 = (bf16[256,2048]{1,0:T(8,128)(2,1)}, bf16[256,1024]{1,0:T(8,128)(2,1)}, f32[16,1,256]{2,1,0:T(1,128)}) custom-call(s32[1]{0:T(128)} %bitcast.core_ref, s32[1,512]{1,0:T(1,128)} %bitcast.18, s32[1,512]{1,0:T(1,128)} %bitcast.14, bf16[512,2048]{1,0:T(8,128)(2,1)} %q_ref.5, bf16[512,2048]{1,0:T(8,128)(2,1)} %ko_ref.7, ...), custom_call_target="tpu_custom_call" | custom-call | flops 8000000 | tf_op jit(solution)/shard_map/attend_early/pallas_call | solution.py:135
  60.7 9.2 %weight_sums.1 = bf16[1024,2048]{1,0:T(8,128)(2,1)} custom-call(s32[1]{0:T(128)} %bitcast.core_ref, bf16[256,2048]{1,0:T(8,128)(2,1)} %get-tuple-element.66.early_ref, bf16[256,2048]{1,0:T(8,128)(2,1)} %get-tuple-element.46.late_ref, bf16[256,1024]{1,0:T(8,128)(2,1)} %copy-done.8, bf16[256,1024]{1,0:T(8,128)(2,1)} %copy-done.7, bf16[512,2048]{1,0:T(8,128)(2,1)} %cot_ref.2, ...), custom_call_target="tpu_custom_call" | custom-call | flops 7000000 | tf_op jit(solution)/shard_map/weight_sums/pallas_call | solution.py:316
  72.8 5.1 %all-to-all-start.2 = ((bf16[4,256,2048]{2,1,0:T(8,128)(2,1)}), bf16[4,256,2048]{2,1,0:T(8,128)(2,1)}, u32[]{:S(2)}, u32[]{:S(2)}) async-start(bf16[4,256,2048]{2,1,0:T(8,128)(2,1)} %bitcast.8), calls=%async_computation.2 | async-start | bytes 8388608 | tf_op jit(solution)/shard_map/all_to_all | solution.py:467
  79.8 10.1 %grad_attention.1.g_ref = bf16[512,2048]{1,0:T(8,128)(2,1)} custom-call(s32[2]{0:T(128)} %pad_add_fusion.place_ref, bf16[512,2048]{1,0:T(8,128)(2,1)} %cot_ref.2, bf16[4,128,2048]{2,1,0:T(8,128)(2,1)} %all-to-all-done.refs_0_, bf16[4,128,2048]{2,1,0:T(8,128)(2,1)} %all-to-all-done.1.refs_1_, bf16[4,128,2048]{2,1,0:T(8,128)(2,1)} %collective-permute-done.6.refs_2_, ...), custom_call_target="tpu_custom_call" | custom-call | flops 7000000 | tf_op jit(solution)/shard_map/grad_attention/pallas_call | solution.py:349
  89.9 10.2 %attend_backward_first.1 = (bf16[512,2048]{1,0:T(8,128)(2,1)}, bf16[512,2048]{1,0:T(8,128)(2,1)}, bf16[512,2048]{1,0:T(8,128)(2,1)}, bf16[2,256,1024]{2,1,0:T(8,128)(2,1)}, bf16[2,112,1024]{2,1,0:T(8,128)(2,1)}) custom-call(s32[1,512]{1,0:T(1,128)} %bitcast.19, s32[1,512]{1,0:T(1,128)} %bitcast.15, f32[16,1,256]{2,1,0:T(1,128)} %get-tuple-element.54.lse_early_ref, ...), custom_call_target="tpu_custom_call" | custom-call | flops 10000000 | tf_op jit(solution)/shard_map/attend_backward_first/pallas_call | solution.py:225
  102.1 3.6 %collective-permute-start.8 = (bf16[2,112,1024]{2,1,0:T(8,128)(2,1)}, bf16[2,112,1024]{2,1,0:T(8,128)(2,1)S(1)}, u32[]{:S(2)}, u32[]{:S(2)}) collective-permute-start(bf16[2,112,1024]{2,1,0:T(8,128)(2,1)} %get-tuple-element.62), channel_id=1, source_target_pairs={{0,1},{1,2},{2,3},{3,4},{4,5},{5,6},{6,7},{7,8},{8,9},{9,10},{10,1... | collective-permute-start | bytes 1376264 | tf_op jit(solution)/shard_map/ppermute | solution.py:426
  105.7 10.3 %attend_backward_second.1 = (bf16[512,2048]{1,0:T(8,128)(2,1)}, bf16[512,2048]{1,0:T(8,128)(2,1)}, bf16[512,2048]{1,0:T(8,128)(2,1)}, bf16[2,256,1024]{2,1,0:T(8,128)(2,1)}, bf16[2,112,1024]{2,1,0:T(8,128)(2,1)}) custom-call(s32[1,512]{1,0:T(1,128)} %bitcast.20, s32[1,512]{1,0:T(1,128)} %bitcast.16, ...), custom_call_target="tpu_custom_call", output_to_operand_aliasing={{0}: (12, {}), {1}: (13, {}), {2}: (14, {})} | custom-call | flops 10000000 | tf_op jit(solution)/shard_map/attend_backward_second/pallas_call | solution.py:225
  117.9 8.7 %all-to-all-done.2.pieces_ref = bf16[4,256,2048]{2,1,0:T(8,128)(2,1)} async-done(((bf16[4,256,2048]{2,1,0:T(8,128)(2,1)}), bf16[4,256,2048]{2,1,0:T(8,128)(2,1)}, u32[]{:S(2)}, u32[]{:S(2)}) %all-to-all-start.2) | async-done | bytes 4194336 | tf_op jit(solution)/shard_map/all_to_all | solution.py:467
  126.7 3.3 %sum_pieces.2 = bf16[1,256,2048]{2,1,0:T(8,128)(2,1)} custom-call(bf16[4,256,2048]{2,1,0:T(8,128)(2,1)} %all-to-all-done.2.pieces_ref), custom_call_target="tpu_custom_call" | custom-call | flops 2000000 | tf_op jit(solution)/shard_map/sum_pieces/pallas_call | solution.py:407
  130.0 7.5 %all-to-all-start.3 = ((bf16[16,16,2048]{2,1,0:T(8,128)(2,1)}), bf16[16,16,2048]{2,1,0:T(8,128)(2,1)S(1)}, u32[]{:S(2)}, u32[]{:S(2)}) async-start(bf16[16,16,2048]{2,1,0:T(8,128)(2,1)} %bitcast.9), calls=%async_computation.3 | async-start | bytes 2097152 | tf_op jit(solution)/shard_map/all_to_all | solution.py:480
  137.4 4.5 %collective-permute-start.11 = (bf16[2,112,1024]{2,1,0:T(8,128)(2,1)}, bf16[2,112,1024]{2,1,0:T(8,128)(2,1)S(1)}, u32[]{:S(2)}, u32[]{:S(2)}) collective-permute-start(bf16[2,112,1024]{2,1,0:T(8,128)(2,1)} %get-tuple-element.71), channel_id=1, source_target_pairs={{0,1},{1,2},{2,3},{3,4},{4,5},{5,6},{6,7},{7,8},{8,9},{9,10},{10,1... | collective-permute-start | bytes 1376264 | tf_op jit(solution)/shard_map/ppermute | solution.py:426
  142.0 10.0 %project.1 = bf16[512,2048]{1,0:T(8,128)(2,1)} custom-call(s32[2]{0:T(128)} %pad_add_fusion.place_ref, bf16[256,2048]{1,0:T(8,128)(2,1)} %get-tuple-element.66.early_ref, bf16[256,2048]{1,0:T(8,128)(2,1)} %get-tuple-element.46.late_ref, bf16[4,128,2048]{2,1,0:T(8,128)(2,1)} %all-to-all-done.refs_0_, bf16[4,128,2048]{2,1,0:T(8,128)(2,1)} %all-to-all-done.1.refs_1_, ...), custom_call_target="tpu_custom_call" | custom-call | flops 8000000 | tf_op jit(solution)/shard_map/project/pallas_call | solution.py:380
  156.6 3.5 %all-to-all-start.4 = ((bf16[8,16,2048]{2,1,0:T(8,128)(2,1)}), bf16[8,16,2048]{2,1,0:T(8,128)(2,1)S(1)}, u32[]{:S(2)}, u32[]{:S(2)}) async-start(bf16[8,16,2048]{2,1,0:T(8,128)(2,1)} %sum_pieces.3), calls=%async_computation.4 | async-start | bytes 1048576 | tf_op jit(solution)/shard_map/all_to_all | solution.py:483
  160.9 5.6 %finish_grads.1 = (bf16[512,2048]{1,0:T(8,128)(2,1)}, bf16[512,2048]{1,0:T(8,128)(2,1)}) custom-call(bf16[512,2048]{1,0:T(8,128)(2,1)} %get-tuple-element.69.dk_ref, bf16[512,2048]{1,0:T(8,128)(2,1)} %get-tuple-element.70.dv_ref, bf16[2,112,1024]{2,1,0:T(8,128)(2,1)} %copy-done.10, bf16[2,112,1024]{2,1,0:T(8,128)(2,1)} %copy-done.11, ...), custom_call_target="tpu_custom_call" | custom-call | flops 2000000 | tf_op jit(solution)/shard_map/finish_grads/pallas_call | solution.py:266
  167.2 3.8 %collective-permute-start.12 = (bf16[128,2048]{1,0:T(8,128)(2,1)S(1)}, bf16[128,2048]{1,0:T(8,128)(2,1)S(1)}, u32[]{:S(2)}, u32[]{:S(2)}) collective-permute-start(bf16[128,2048]{1,0:T(8,128)(2,1)S(1)} %bitcast.11), channel_id=1, source_target_pairs={{0,1},{1,0},{2,3},{3,2},{4,5},{5,4},{6,7},{7,6},{8,9},{9,8},{10,11... | collective-permute-start | bytes 1572872 | tf_op jit(solution)/shard_map/ppermute | solution.py:420
  (68 shorter events, 34.3 us)
Async XLA Ops:
  5.4 17.8 %collective-permute-start.1 = (bf16[128,4096]{1,0:T(8,128)(2,1)S(1)}, bf16[128,4096]{1,0:T(8,128)(2,1)}, u32[]{:S(2)}, u32[]{:S(2)}) collective-permute-start(bf16[128,4096]{1,0:T(8,128)(2,1)S(1)} %pad_maximum_fusion.1), channel_id=1, source_target_pairs={{1,0},{2,1},{3,2},{4,3},{5,4},{6,5},{7,6},{8,7},{9,8},{10,9},{11,1... | collective-permute-start | bytes 3145736 | tf_op jit(solution)/shard_map/ppermute | solution.py:426
  8.7 31.5 %all-to-all-start = ((bf16[4,128,2048]{2,1,0:T(8,128)(2,1)}), bf16[4,128,2048]{2,1,0:T(8,128)(2,1)}, u32[]{:S(2)}, u32[]{:S(2)}) async-start(bf16[4,128,2048]{2,1,0:T(8,128)(2,1)} %broadcast_in_dim.7), calls=%async_computation | async-start | bytes 4194304 | tf_op jit(solution)/shard_map/all_to_all | solution.py:447
  13.3 16.5 %collective-permute-start = (bf16[128,2048]{1,0:T(8,128)(2,1)}, bf16[128,2048]{1,0:T(8,128)(2,1)}, u32[]{:S(2)}, u32[]{:S(2)}) collective-permute-start(bf16[128,2048]{1,0:T(8,128)(2,1)} %constant_dynamic-slice_fusion), channel_id=1, source_target_pairs={{0,18},{2,16},{16,2},{18,0},{1,19},{3,17},{17,3},{19,1},{4,22},{6,... | collective-permute-start | bytes 1572872 | tf_op jit(solution)/shard_map/ppermute | solution.py:430
  17.2 8.7 %copy-start.12 = (s32[512]{0:T(512)S(1)}, s32[512]{0:T(512)}, u32[]{:S(2)}) copy-start(s32[512]{0:T(512)} %param.11) | copy-start | bytes 6148
  17.2 8.7 %copy-start.13 = (s32[512]{0:T(512)S(1)}, s32[512]{0:T(512)}, u32[]{:S(2)}) copy-start(s32[512]{0:T(512)} %param.10) | copy-start | bytes 6148
  23.2 25.2 %collective-permute-start.3 = (bf16[256,4096]{1,0:T(8,128)(2,1)}, bf16[256,4096]{1,0:T(8,128)(2,1)S(1)}, u32[]{:S(2)}, u32[]{:S(2)}) collective-permute-start(bf16[256,4096]{1,0:T(8,128)(2,1)} %pad_maximum_fusion), channel_id=1, source_target_pairs={{0,1},{1,2},{2,3},{3,4},{4,5},{5,6},{6,7},{7,8},{8,9},{9,10},{10,1... | collective-permute-start | bytes 6291464 | tf_op jit(solution)/shard_map/ppermute | solution.py:426
  25.1 32.7 %collective-permute-start.5 = (bf16[512,2048]{1,0:T(8,128)(2,1)}, bf16[512,2048]{1,0:T(8,128)(2,1)}, u32[]{:S(2)}, u32[]{:S(2)}) collective-permute-start(bf16[512,2048]{1,0:T(8,128)(2,1)} %cot_ref.2), channel_id=1, source_target_pairs={{0,1},{1,0},{2,3},{3,2},{4,5},{5,4},{6,7},{7,6},{8,9},{9,8},{10,11... | collective-permute-start | bytes 6291464 | tf_op jit(solution)/shard_map/ppermute | solution.py:420
  40.3 17.5 %collective-permute-start.6 = (bf16[4,128,2048]{2,1,0:T(8,128)(2,1)}, bf16[4,128,2048]{2,1,0:T(8,128)(2,1)}, u32[]{:S(2)}, u32[]{:S(2)}) collective-permute-start(bf16[4,128,2048]{2,1,0:T(8,128)(2,1)} %all-to-all-done.refs_0_), channel_id=1, source_target_pairs={{0,1},{1,0},{2,3},{3,2},{4,5},{5,4},{6,7},{7,6},{8,9},{9,8},{10,11... | collective-permute-start | bytes 6291464 | tf_op jit(solution)/shard_map/ppermute | solution.py:420
  41.0 30.8 %all-to-all-start.1 = ((bf16[4,128,2048]{2,1,0:T(8,128)(2,1)}), bf16[4,128,2048]{2,1,0:T(8,128)(2,1)}, u32[]{:S(2)}, u32[]{:S(2)}) async-start(bf16[4,128,2048]{2,1,0:T(8,128)(2,1)} %broadcast_in_dim.6), calls=%async_computation.1 | async-start | bytes 4194304 | tf_op jit(solution)/shard_map/all_to_all | solution.py:459
  45.4 2.0 %collective-permute-start.2 = (bf16[256,1024]{1,0:T(8,128)(2,1)S(1)}, bf16[256,1024]{1,0:T(8,128)(2,1)S(1)}, u32[]{:S(2)}, u32[]{:S(2)}) collective-permute-start(bf16[256,1024]{1,0:T(8,128)(2,1)S(1)} %copy-done.14), channel_id=1, source_target_pairs={{0,1},{1,0},{2,3},{3,2},{4,5},{5,4},{6,7},{7,6},{8,9},{9,8},{10,11... | collective-permute-start | bytes 1572872 | tf_op jit(solution)/shard_map/ppermute | solution.py:420
  47.4 12.5 %copy-start.7 = (bf16[256,1024]{1,0:T(8,128)(2,1)}, bf16[256,1024]{1,0:T(8,128)(2,1)S(1)}, u32[]{:S(2)}) copy-start(bf16[256,1024]{1,0:T(8,128)(2,1)S(1)} %collective-permute-done.2.peer_late_ref) | copy-start | bytes 1572868
  57.7 2.2 %collective-permute-start.4 = (bf16[256,1024]{1,0:T(8,128)(2,1)}, bf16[256,1024]{1,0:T(8,128)(2,1)S(1)}, u32[]{:S(2)}, u32[]{:S(2)}) collective-permute-start(bf16[256,1024]{1,0:T(8,128)(2,1)} %get-tuple-element.47), channel_id=1, source_target_pairs={{0,1},{1,0},{2,3},{3,2},{4,5},{5,4},{6,7},{7,6},{8,9},{9,8},{10,11... | collective-permute-start | bytes 1572872 | tf_op jit(solution)/shard_map/ppermute | solution.py:420
  71.7 6.7 %collective-permute-start.7 = (bf16[4,128,2048]{2,1,0:T(8,128)(2,1)}, bf16[4,128,2048]{2,1,0:T(8,128)(2,1)S(1)}, u32[]{:S(2)}, u32[]{:S(2)}) collective-permute-start(bf16[4,128,2048]{2,1,0:T(8,128)(2,1)} %all-to-all-done.1.refs_1_), channel_id=1, source_target_pairs={{0,1},{1,0},{2,3},{3,2},{4,5},{5,4},{6,7},{7,6},{8,9},{9,8},{10,11... | collective-permute-start | bytes 6291464 | tf_op jit(solution)/shard_map/ppermute | solution.py:420
  72.8 53.9 %all-to-all-start.2 = ((bf16[4,256,2048]{2,1,0:T(8,128)(2,1)}), bf16[4,256,2048]{2,1,0:T(8,128)(2,1)}, u32[]{:S(2)}, u32[]{:S(2)}) async-start(bf16[4,256,2048]{2,1,0:T(8,128)(2,1)} %bitcast.8), calls=%async_computation.2 | async-start | bytes 8388608 | tf_op jit(solution)/shard_map/all_to_all | solution.py:467
  100.1 29.8 %collective-permute-start.9 = (bf16[2,256,1024]{2,1,0:T(8,128)(2,1)}, bf16[2,256,1024]{2,1,0:T(8,128)(2,1)S(1)}, u32[]{:S(2)}, u32[]{:S(2)}) collective-permute-start(bf16[2,256,1024]{2,1,0:T(8,128)(2,1)} %get-tuple-element.63), channel_id=1, source_target_pairs={{1,0},{2,1},{3,2},{4,3},{5,4},{6,5},{7,6},{8,7},{9,8},{10,9},{11,1... | collective-permute-start | bytes 3145736 | tf_op jit(solution)/shard_map/ppermute | solution.py:426
  102.1 27.9 %collective-permute-start.8 = (bf16[2,112,1024]{2,1,0:T(8,128)(2,1)}, bf16[2,112,1024]{2,1,0:T(8,128)(2,1)S(1)}, u32[]{:S(2)}, u32[]{:S(2)}) collective-permute-start(bf16[2,112,1024]{2,1,0:T(8,128)(2,1)} %get-tuple-element.62), channel_id=1, source_target_pairs={{0,1},{1,2},{2,3},{3,4},{4,5},{5,6},{6,7},{7,8},{8,9},{9,10},{10,1... | collective-permute-start | bytes 1376264 | tf_op jit(solution)/shard_map/ppermute | solution.py:426
  116.0 26.0 %collective-permute-start.10 = (bf16[2,256,1024]{2,1,0:T(8,128)(2,1)}, bf16[2,256,1024]{2,1,0:T(8,128)(2,1)}, u32[]{:S(2)}, u32[]{:S(2)}) collective-permute-start(bf16[2,256,1024]{2,1,0:T(8,128)(2,1)} %get-tuple-element.65), channel_id=1, source_target_pairs={{1,0},{2,1},{3,2},{4,3},{5,4},{6,5},{7,6},{8,7},{9,8},{10,9},{11,1... | collective-permute-start | bytes 3145736 | tf_op jit(solution)/shard_map/ppermute | solution.py:426
  129.9 22.0 %copy-start.10 = (bf16[2,112,1024]{2,1,0:T(8,128)(2,1)}, bf16[2,112,1024]{2,1,0:T(8,128)(2,1)S(1)}, u32[]{:S(2)}) copy-start(bf16[2,112,1024]{2,1,0:T(8,128)(2,1)S(1)} %collective-permute-done.8.prev_first_ref) | copy-start | bytes 1376260
  130.0 22.0 %copy-start.6 = (bf16[2,256,1024]{2,1,0:T(8,128)(2,1)}, bf16[2,256,1024]{2,1,0:T(8,128)(2,1)S(1)}, u32[]{:S(2)}) copy-start(bf16[2,256,1024]{2,1,0:T(8,128)(2,1)S(1)} %collective-permute-done.9.next_first_ref) | copy-start | bytes 3145732
  130.0 23.5 %all-to-all-start.3 = ((bf16[16,16,2048]{2,1,0:T(8,128)(2,1)}), bf16[16,16,2048]{2,1,0:T(8,128)(2,1)S(1)}, u32[]{:S(2)}, u32[]{:S(2)}) async-start(bf16[16,16,2048]{2,1,0:T(8,128)(2,1)} %bitcast.9), calls=%async_computation.3 | async-start | bytes 2097152 | tf_op jit(solution)/shard_map/all_to_all | solution.py:480
  137.4 22.7 %collective-permute-start.11 = (bf16[2,112,1024]{2,1,0:T(8,128)(2,1)}, bf16[2,112,1024]{2,1,0:T(8,128)(2,1)S(1)}, u32[]{:S(2)}, u32[]{:S(2)}) collective-permute-start(bf16[2,112,1024]{2,1,0:T(8,128)(2,1)} %get-tuple-element.71), channel_id=1, source_target_pairs={{0,1},{1,2},{2,3},{3,4},{4,5},{5,6},{6,7},{7,8},{8,9},{9,10},{10,1... | collective-permute-start | bytes 1376264 | tf_op jit(solution)/shard_map/ppermute | solution.py:426
  156.6 10.5 %all-to-all-start.4 = ((bf16[8,16,2048]{2,1,0:T(8,128)(2,1)}), bf16[8,16,2048]{2,1,0:T(8,128)(2,1)S(1)}, u32[]{:S(2)}, u32[]{:S(2)}) async-start(bf16[8,16,2048]{2,1,0:T(8,128)(2,1)} %sum_pieces.3), calls=%async_computation.4 | async-start | bytes 1048576 | tf_op jit(solution)/shard_map/all_to_all | solution.py:483
  160.9 14.9 %copy-start.1 = (bf16[256,2048]{1,0:T(8,128)(2,1)S(1)}, bf16[256,2048]{1,0:T(8,128)(2,1)}, u32[]{:S(2)}) copy-start(bf16[256,2048]{1,0:T(8,128)(2,1)} %param.12) | copy-start | bytes 3145732
  167.2 5.4 %collective-permute-start.12 = (bf16[128,2048]{1,0:T(8,128)(2,1)S(1)}, bf16[128,2048]{1,0:T(8,128)(2,1)S(1)}, u32[]{:S(2)}, u32[]{:S(2)}) collective-permute-start(bf16[128,2048]{1,0:T(8,128)(2,1)S(1)} %bitcast.11), channel_id=1, source_target_pairs={{0,1},{1,0},{2,3},{3,2},{4,5},{5,4},{6,7},{7,6},{8,9},{9,8},{10,11... | collective-permute-start | bytes 1572872 | tf_op jit(solution)/shard_map/ppermute | solution.py:420
  (13 other events, 29.7 us)

commit v5 on v3

--- a/solution.py
+++ b/solution.py
@@ -15,6 +15,7 @@
 BEFORE = 256
 AFTER = 128
 SENT_AFTER = 112
+TOP = 96
 SPAN = 640
 FACTOR = HEAD_DIM ** -0.5
 TOKENS = 65536
@@ -301,11 +302,10 @@
 def place_weights(place_ref, refs, rows_ref):
     core = place_ref[0]
     zh = place_ref[1]
-    near_ref, far_ref, near_other_ref, far_other_ref = refs
-    rows_ref[:, zh, core] = near_ref[...]
-    rows_ref[:, 1 - zh, core] = far_ref[...]
-    rows_ref[:, zh, 1 - core] = near_other_ref[...]
-    rows_ref[:, 1 - zh, 1 - core] = far_other_ref[...]
+    for at, (near_ref, top_ref, low_ref) in ((core, refs[:3]), (1 - core, refs[3:])):
+        rows_ref[:, zh, at] = near_ref[...]
+        rows_ref[:, 1 - zh, at, :TOP] = top_ref[...]
+        rows_ref[:, 1 - zh, at, TOP:] = low_ref[...]
 
 
 def grad_attn_kernel(place_ref, cot_ref, *refs):
@@ -315,13 +315,13 @@
 
 
 def grad_attention(place, cot, *weights):
-    piece = pl.BlockSpec((1, HEAD_DIM, WIDTH), lambda i, *_: (i, 0, 0))
+    pieces = [pl.BlockSpec((1, rows, WIDTH), lambda i, *_: (i, 0, 0)) for rows in (HEAD_DIM, TOP, HEAD_DIM - TOP)]
     return pl.pallas_call(
         grad_attn_kernel,
         grid_spec=pltpu.PrefetchScalarGridSpec(
             num_scalar_prefetch=1,
             grid=(4,),
-            in_specs=[fixed((TOK, WIDTH))] + [piece] * 4,
+            in_specs=[fixed((TOK, WIDTH))] + pieces * 2,
             out_specs=pl.BlockSpec((TOK, 4 * HEAD_DIM), lambda i, *_: (0, i)),
             scratch_shapes=[pltpu.VMEM((1, 2, 2, HEAD_DIM, WIDTH), jnp.bfloat16)],
         ),
@@ -346,13 +346,13 @@
 
 def project(place, early, late, *weights):
     tile = 512
-    piece = pl.BlockSpec((4, HEAD_DIM, tile), lambda i, *_: (0, 0, i))
+    pieces = [pl.BlockSpec((4, rows, tile), lambda i, *_: (0, 0, i)) for rows in (HEAD_DIM, TOP, HEAD_DIM - TOP)]
     return pl.pallas_call(
         project_kernel,
         grid_spec=pltpu.PrefetchScalarGridSpec(
             num_scalar_prefetch=1,
             grid=(WIDTH // tile,),
-            in_specs=[fixed((BLOCK, WIDTH)), fixed((BLOCK, WIDTH))] + [piece] * 4,
+            in_specs=[fixed((BLOCK, WIDTH)), fixed((BLOCK, WIDTH))] + pieces * 2,
             out_specs=pl.BlockSpec((TOK, tile), lambda i, *_: (0, i)),
             scratch_shapes=[pltpu.VMEM((4, 2, 2, HEAD_DIM, tile), jnp.bfloat16), pltpu.VMEM((TOK, WIDTH), jnp.bfloat16)],
         ),
@@ -384,6 +384,25 @@
         cost_estimate=cost(2e9),
         name="sum_pieces",
     )(pieces)
+
+
+def copy_kernel(in_ref, out_ref):
+    out_ref[...] = in_ref[...]
+
+
+def low_rows(near):
+    y, rows, width = near.shape
+    low = rows - TOP
+    return pl.pallas_call(
+        copy_kernel,
+        grid=(2,),
+        in_specs=[pl.BlockSpec((y // 2, low, width), lambda i: (i, TOP // low, 0))],
+        out_specs=pl.BlockSpec((y // 2, low, width), lambda i: (i, 0, 0)),
+        out_shape=jax.ShapeDtypeStruct((y, low, width), near.dtype),
+        compiler_params=params(),
+        cost_estimate=cost(1e9),
+        name="low_rows",
+    )(near)
 
 
 def swapped(array):
@@ -422,22 +441,24 @@
     before_rows = jnp.concatenate([key_rows[TOK - BEFORE:], value_rows[TOK - BEFORE:]], axis=1)
     before = passed_along(tied(before_rows, after_rows, after), 1)
     cot_peer = swapped(tied(cotangent, after_rows))
-    far_halves = jnp.broadcast_to(far_half, (4, HEAD_DIM, WIDTH))
+    far_tops = jnp.broadcast_to(far_half[:TOP], (4, TOP, WIDTH))
 
     late, late_theirs, late_lse = forward(
-        True, core_arg, start, end, tied(query_rows, far_halves), key_rows, value_rows, after)
-    far = lax.all_to_all(tied(far_halves, near, late), "y", 0, 0, tiled=True)
+        True, core_arg, start, end, tied(query_rows, far_tops), key_rows, value_rows, after)
+    far_top = lax.all_to_all(tied(far_tops, near, late), "y", 0, 0, tiled=True)
+    low = low_rows(tied(near, late))
+    far_low = across_z(low)
     peer_late = swapped(late_theirs)
     early, early_theirs, early_lse = forward(
-        False, core_arg, start, end, tied(query_rows, peer_late), key_rows, value_rows, before)
+        False, core_arg, start, end, tied(query_rows, peer_late, low), key_rows, value_rows, before)
     peer_early = swapped(early_theirs)
     near_other = swapped(tied(near, late))
     sums = weight_sums(core_arg, early, late, peer_early, peer_late, cotangent, tied(cot_peer, near_other))
-    far = tied(far, sums)
-    pieces = lax.all_to_all(tied(sums.reshape(4, 2 * HEAD_DIM, WIDTH), far), "y", 0, 0, tiled=True)
-    far_other = swapped(far)
-    weights = (near, far, near_other, far_other)
-    grad_attn = grad_attention(place, tied(cotangent, far), *weights)
+    far_top = tied(far_top, sums)
+    far_low = tied(far_low, sums)
+    pieces = lax.all_to_all(tied(sums.reshape(4, 2 * HEAD_DIM, WIDTH), far_top), "y", 0, 0, tiled=True)
+    weights = (near, far_top, far_low, near_other, swapped(far_top), swapped(far_low))
+    grad_attn = grad_attention(place, tied(cotangent, far_top), *weights)
     shared = (start, end, early_lse, late_lse, query_rows, grad_attn, key_rows, value_rows, before, after)
     dq, dk, dv, to_previous, to_next = backward(0, *shared)
     from_next = [passed_along(to_previous, -1)]

time: 177 us -> 198 us (1.12)
  starting transfers between devices: 51.7 us -> 68 us
  Pallas kernels: 79.1 us -> 81.3 us
  waiting for transfers between devices: 26.5 us -> 28.7 us
    all_to_all x1, starting transfers between devices: 3.49 us -> 17.6 us  [on_device(): lax.all_to_all(summed, ('x', 'zl'), 0, 0, tiled=True)]
    ppermute x1 -> x2, waiting for transfers between devices: 3.34 us -> 15.6 us  [across_z(): return lax.ppermute(array, ('zh', 'zl'), [(z, 3 - z) for z in range(4)])]
    all_to_all x2, waiting for transfers between devices: 10.7 us -> 0.01 us  [the longest x1 0.01 us: on_device(): far_top = lax.all_to_all(tied(far_tops, near, late), 'y', 0, 0, tiled=True)]
    ppermute x1 -> x2, starting transfers between devices: 3.92 us -> 8.39 us  [across_z(): return lax.ppermute(array, ('zh', 'zl'), [(z, 3 - z) for z in range(4)])]
    ppermute x6 -> x7, starting transfers between devices: 5.55 us -> 3.1 us  [swapped(): return lax.ppermute(array, 'core', [(0, 1), (1, 0)])]
    ppermute x6 -> x7, waiting for transfers between devices: 5.38 us -> 4.52 us  [swapped(): return lax.ppermute(array, 'core', [(0, 1), (1, 0)])]
    unnamed x26 -> x32, local copies, waits for them, and re-layouts: 6.39 us -> 7.05 us
  transfers between devices with their start and end apart: 18 -> 20, of which waited for: 9 -> 11; matrix products, arithmetic and copies ran while one was open for 3% -> 3% of each run, Pallas kernels for 45% -> 41%
where the time goes in v5:
time: 198 us; the launch traced here: 196 us
  Pallas kernels  81.3 us (41%)
  starting transfers between devices  68 us (34%)
  waiting for transfers between devices  28.7 us (14%)
  local copies, waits for them, and re-layouts  12.9 us (7%)
  other arithmetic  4.47 us (2%)
    pallas_call x2, Pallas kernels, backward(): pl.pallas_call(backward_kernel, grid=(steps,), in_specs=[fixed((1, TOK)),...  20.6 us
    ppermute x6, starting transfers between devices, passed_along(): return lax.ppermute(array, GROUP_AXES, pairs)  18 us
    all_to_all x1, starting transfers between devices, on_device(): lax.all_to_all(summed, ('x', 'zl'), 0, 0, tiled=True)  17.6 us
    pallas_call x2, Pallas kernels, forward(): pl.pallas_call(functools.partial(forward_kernel, late=late), grid_spec=pl...  15.9 us
    ppermute x2, waiting for transfers between devices, across_z(): return lax.ppermute(array, ('zh', 'zl'), [(z, 3 - z) for z in range(4)])  15.6 us
    pallas_call x1, Pallas kernels, grad_attention(): pl.pallas_call(grad_attn_kernel, grid_spec=pltpu.PrefetchScalarGridSpec(n...  10.2 us
    pallas_call x1, Pallas kernels, project(): pl.pallas_call(project_kernel, grid_spec=pltpu.PrefetchScalarGridSpec(num...  10.1 us
    pallas_call x1, Pallas kernels, weight_sums(): pl.pallas_call(weight_sums_kernel, grid_spec=pltpu.PrefetchScalarGridSpec...  9.19 us
  transfers between devices with their start and end apart: 20, of which 11 were waited for; matrix products, arithmetic and copies ran while one was open for 3% of the time, Pallas kernels for 41%

profile of v5, /device:TPU:1, one launch (start us, length us, event | category | flops | bytes accessed | tf_op | source)
XLA Modules:
  0.0 196.3 jit_solution(9708237863301519869)
XLA Ops:
  2.8 2.6 %broadcast_in_dim.7 = bf16[4,128,2048]{2,1,0:T(8,128)(2,1)} broadcast(bf16[128,2048]{1,0:T(8,128)(2,1)} %constant_dynamic-slice_fusion), dimensions={1,2} | broadcast | bytes 2621440 | tf_op jit(solution)/shard_map/broadcast_in_dim | solution.py:435
  5.4 3.3 %collective-permute-start.1 = (bf16[128,4096]{1,0:T(8,128)(2,1)S(1)}, bf16[128,4096]{1,0:T(8,128)(2,1)}, u32[]{:S(2)}, u32[]{:S(2)}) collective-permute-start(bf16[128,4096]{1,0:T(8,128)(2,1)S(1)} %pad_maximum_fusion.1), channel_id=1, source_target_pairs={{1,0},{2,1},{3,2},{4,3},{5,4},{6,5},{7,6},{8,7},{9,8},{10,9},{11,1... | collective-permute-start | bytes 3145736 | tf_op jit(solution)/shard_map/ppermute | solution.py:415
  8.7 4.5 %all-to-all-start = ((bf16[4,128,2048]{2,1,0:T(8,128)(2,1)}), bf16[4,128,2048]{2,1,0:T(8,128)(2,1)}, u32[]{:S(2)}, u32[]{:S(2)}) async-start(bf16[4,128,2048]{2,1,0:T(8,128)(2,1)} %broadcast_in_dim.7), calls=%async_computation | async-start | bytes 4194304 | tf_op jit(solution)/shard_map/all_to_all | solution.py:436
  13.2 3.9 %collective-permute-start = (bf16[128,2048]{1,0:T(8,128)(2,1)}, bf16[128,2048]{1,0:T(8,128)(2,1)}, u32[]{:S(2)}, u32[]{:S(2)}) collective-permute-start(bf16[128,2048]{1,0:T(8,128)(2,1)} %constant_dynamic-slice_fusion), channel_id=1, source_target_pairs={{0,18},{2,16},{16,2},{18,0},{1,19},{3,17},{17,3},{19,1},{4,22},{6,... | collective-permute-start | bytes 1572872 | tf_op jit(solution)/shard_map/ppermute | solution.py:419
  18.7 4.5 %collective-permute-done.1.kh_ref.vh_ref.ka_ref.va_ref = bf16[128,4096]{1,0:T(8,128)(2,1)} collective-permute-done((bf16[128,4096]{1,0:T(8,128)(2,1)S(1)}, bf16[128,4096]{1,0:T(8,128)(2,1)}, u32[]{:S(2)}, u32[]{:S(2)}) %collective-permute-start.1) | collective-permute-done | bytes 1048608 | tf_op jit(solution)/shard_map/ppermute | solution.py:415
  26.4 3.3 %collective-permute-done = bf16[128,2048]{1,0:T(8,128)(2,1)} collective-permute-done((bf16[128,2048]{1,0:T(8,128)(2,1)}, bf16[128,2048]{1,0:T(8,128)(2,1)}, u32[]{:S(2)}, u32[]{:S(2)}) %collective-permute-start) | collective-permute-done | bytes 524320 | tf_op jit(solution)/shard_map/ppermute | solution.py:419
  32.1 7.7 %attend_late.1 = (bf16[256,2048]{1,0:T(8,128)(2,1)}, bf16[256,1024]{1,0:T(8,128)(2,1)}, f32[16,1,256]{2,1,0:T(1,128)}) custom-call(s32[1]{0:T(128)} %bitcast.core_ref, s32[1,512]{1,0:T(1,128)} %bitcast.15, s32[1,512]{1,0:T(1,128)} %bitcast.11, bf16[512,2048]{1,0:T(8,128)(2,1)} %q_ref.5, bf16[512,2048]{1,0:T(8,128)(2,1)} %ko_ref.7, ...), custom_call_target="tpu_custom_call" | custom-call | flops 8000000 | tf_op jit(solution)/shard_map/attend_late/pallas_call | solution.py:136
  40.6 4.3 %all-to-all-start.1 = ((bf16[4,96,2048]{2,1,0:T(8,128)(2,1)}), bf16[4,96,2048]{2,1,0:T(8,128)(2,1)}, u32[]{:S(2)}, u32[]{:S(2)}) async-start(bf16[4,96,2048]{2,1,0:T(8,128)(2,1)} %broadcast_in_dim.6), calls=%async_computation.1 | async-start | bytes 3145728 | tf_op jit(solution)/shard_map/all_to_all | solution.py:448
  49.7 8.1 %attend_early.1 = (bf16[256,2048]{1,0:T(8,128)(2,1)}, bf16[256,1024]{1,0:T(8,128)(2,1)}, f32[16,1,256]{2,1,0:T(1,128)}) custom-call(s32[1]{0:T(128)} %bitcast.core_ref, s32[1,512]{1,0:T(1,128)} %bitcast.16, s32[1,512]{1,0:T(1,128)} %bitcast.12, bf16[512,2048]{1,0:T(8,128)(2,1)} %q_ref.5, bf16[512,2048]{1,0:T(8,128)(2,1)} %ko_ref.7, ...), custom_call_target="tpu_custom_call" | custom-call | flops 8000000 | tf_op jit(solution)/shard_map/attend_early/pallas_call | solution.py:136
  60.8 9.2 %weight_sums.1 = bf16[1024,2048]{1,0:T(8,128)(2,1)} custom-call(s32[1]{0:T(128)} %bitcast.core_ref, bf16[256,2048]{1,0:T(8,128)(2,1)} %get-tuple-element.70.early_ref, bf16[256,2048]{1,0:T(8,128)(2,1)} %get-tuple-element.46.late_ref, bf16[256,1024]{1,0:T(8,128)(2,1)} %copy-done.10, bf16[256,1024]{1,0:T(8,128)(2,1)} %copy-done.9, bf16[512,2048]{1,0:T(8,128)(2,1)} %cot_ref.2, ...), custom_call_target="tpu_custom_call" | custom-call | flops 7000000 | tf_op jit(solution)/shard_map/weight_sums/pallas_call | solution.py:287
  70.0 5.0 %all-to-all-start.2 = ((bf16[4,256,2048]{2,1,0:T(8,128)(2,1)}), bf16[4,256,2048]{2,1,0:T(8,128)(2,1)}, u32[]{:S(2)}, u32[]{:S(2)}) async-start(bf16[4,256,2048]{2,1,0:T(8,128)(2,1)} %bitcast.7), calls=%async_computation.2 | async-start | bytes 8388608 | tf_op jit(solution)/shard_map/all_to_all | solution.py:459
  75.3 4.5 %collective-permute-start.7 = (bf16[4,32,2048]{2,1,0:T(8,128)(2,1)S(1)}, bf16[4,32,2048]{2,1,0:T(8,128)(2,1)S(1)}, u32[]{:S(2)}, u32[]{:S(2)}) collective-permute-start(bf16[4,32,2048]{2,1,0:T(8,128)(2,1)S(1)} %copy-done.8), channel_id=1, source_target_pairs={{0,18},{2,16},{16,2},{18,0},{1,19},{3,17},{17,3},{19,1},{4,22},{6,... | collective-permute-start | bytes 1572872 | tf_op jit(solution)/shard_map/ppermute | solution.py:419
  79.8 12.3 %collective-permute-done.7.refs_2_ = bf16[4,32,2048]{2,1,0:T(8,128)(2,1)S(1)} collective-permute-done((bf16[4,32,2048]{2,1,0:T(8,128)(2,1)S(1)}, bf16[4,32,2048]{2,1,0:T(8,128)(2,1)S(1)}, u32[]{:S(2)}, u32[]{:S(2)}) %collective-permute-start.7) | collective-permute-done | bytes 524320 | tf_op jit(solution)/shard_map/ppermute | solution.py:419
  96.1 10.2 %grad_attention.1.g_ref = bf16[512,2048]{1,0:T(8,128)(2,1)} custom-call(s32[2]{0:T(128)} %pad_add_fusion.place_ref, bf16[512,2048]{1,0:T(8,128)(2,1)} %cot_ref.2, bf16[4,128,2048]{2,1,0:T(8,128)(2,1)} %all-to-all-done.in_ref.refs_0_, bf16[4,96,2048]{2,1,0:T(8,128)(2,1)} %all-to-all-done.1.refs_1_, bf16[4,32,2048]{2,1,0:T(8,128)(2,1)} %copy-done.5, ...), custom_call_target="tpu_custom_call" | custom-call | flops 7000000 | tf_op jit(solution)/shard_map/grad_attention/pallas_call | solution.py:319
  106.4 10.2 %attend_backward_first.1 = (bf16[512,2048]{1,0:T(8,128)(2,1)}, bf16[512,2048]{1,0:T(8,128)(2,1)}, bf16[512,2048]{1,0:T(8,128)(2,1)}, bf16[2,256,1024]{2,1,0:T(8,128)(2,1)}, bf16[2,112,1024]{2,1,0:T(8,128)(2,1)}) custom-call(s32[1,512]{1,0:T(1,128)} %bitcast.17, s32[1,512]{1,0:T(1,128)} %bitcast.13, f32[16,1,256]{2,1,0:T(1,128)} %get-tuple-element.57.lse_early_ref, ...), custom_call_target="tpu_custom_call" | custom-call | flops 10000000 | tf_op jit(solution)/shard_map/attend_backward_first/pallas_call | solution.py:226
  118.9 3.3 %collective-permute-start.10 = (bf16[2,112,1024]{2,1,0:T(8,128)(2,1)}, bf16[2,112,1024]{2,1,0:T(8,128)(2,1)S(1)}, u32[]{:S(2)}, u32[]{:S(2)}) collective-permute-start(bf16[2,112,1024]{2,1,0:T(8,128)(2,1)} %get-tuple-element.66), channel_id=1, source_target_pairs={{0,1},{1,2},{2,3},{3,4},{4,5},{5,6},{6,7},{7,8},{8,9},{9,10},{10,1... | collective-permute-start | bytes 1376264 | tf_op jit(solution)/shard_map/ppermute | solution.py:415
  122.2 10.3 %attend_backward_second.1 = (bf16[512,2048]{1,0:T(8,128)(2,1)}, bf16[512,2048]{1,0:T(8,128)(2,1)}, bf16[512,2048]{1,0:T(8,128)(2,1)}, bf16[2,256,1024]{2,1,0:T(8,128)(2,1)}, bf16[2,112,1024]{2,1,0:T(8,128)(2,1)}) custom-call(s32[1,512]{1,0:T(1,128)} %bitcast.18, s32[1,512]{1,0:T(1,128)} %bitcast.14, ...), custom_call_target="tpu_custom_call", output_to_operand_aliasing={{0}: (12, {}), {1}: (13, {}), {2}: (14, {})} | custom-call | flops 10000000 | tf_op jit(solution)/shard_map/attend_backward_second/pallas_call | solution.py:226
  134.4 3.3 %sum_pieces.2 = bf16[1,256,2048]{2,1,0:T(8,128)(2,1)} custom-call(bf16[4,256,2048]{2,1,0:T(8,128)(2,1)} %all-to-all-done.2.pieces_ref), custom_call_target="tpu_custom_call" | custom-call | flops 2000000 | tf_op jit(solution)/shard_map/sum_pieces/pallas_call | solution.py:377
  138.1 7.1 %all-to-all-start.3 = ((bf16[16,16,2048]{2,1,0:T(8,128)(2,1)}), bf16[16,16,2048]{2,1,0:T(8,128)(2,1)S(1)}, u32[]{:S(2)}, u32[]{:S(2)}) async-start(bf16[16,16,2048]{2,1,0:T(8,128)(2,1)} %bitcast.8), calls=%async_computation.3 | async-start | bytes 2097152 | tf_op jit(solution)/shard_map/all_to_all | solution.py:471
  145.2 5.3 %collective-permute-start.13 = (bf16[2,112,1024]{2,1,0:T(8,128)(2,1)}, bf16[2,112,1024]{2,1,0:T(8,128)(2,1)S(1)}, u32[]{:S(2)}, u32[]{:S(2)}) collective-permute-start(bf16[2,112,1024]{2,1,0:T(8,128)(2,1)} %get-tuple-element.75), channel_id=1, source_target_pairs={{0,1},{1,2},{2,3},{3,4},{4,5},{5,6},{6,7},{7,8},{8,9},{9,10},{10,1... | collective-permute-start | bytes 1376264 | tf_op jit(solution)/shard_map/ppermute | solution.py:415
  151.6 10.1 %project.1 = bf16[512,2048]{1,0:T(8,128)(2,1)} custom-call(s32[2]{0:T(128)} %pad_add_fusion.place_ref, bf16[256,2048]{1,0:T(8,128)(2,1)} %get-tuple-element.70.early_ref, bf16[256,2048]{1,0:T(8,128)(2,1)} %get-tuple-element.46.late_ref, bf16[4,128,2048]{2,1,0:T(8,128)(2,1)} %all-to-all-done.in_ref.refs_0_, bf16[4,96,2048]{2,1,0:T(8,128)(2,1)} %all-to-all-done.1.refs_1_, ...), custom_call_target="tpu_custom_call" | custom-call | flops 8000000 | tf_op jit(solution)/shard_map/project/pallas_call | solution.py:350
  164.9 17.6 %all-to-all-start.4 = ((bf16[8,16,2048]{2,1,0:T(8,128)(2,1)}), bf16[8,16,2048]{2,1,0:T(8,128)(2,1)S(1)}, u32[]{:S(2)}, u32[]{:S(2)}) async-start(bf16[8,16,2048]{2,1,0:T(8,128)(2,1)} %sum_pieces.3), calls=%async_computation.4 | async-start | bytes 1048576 | tf_op jit(solution)/shard_map/all_to_all | solution.py:474
  183.3 3.7 %finish_grads.2 = (bf16[512,2048]{1,0:T(8,128)(2,1)}, bf16[512,2048]{1,0:T(8,128)(2,1)}) custom-call(bf16[512,2048]{1,0:T(8,128)(2,1)} %get-tuple-element.73.dk_ref, bf16[512,2048]{1,0:T(8,128)(2,1)} %get-tuple-element.74.dv_ref, bf16[2,112,1024]{2,1,0:T(8,128)(2,1)} %copy-done.11, ...), custom_call_target="tpu_custom_call", output_to_operand_aliasing={{0}: (0, {}), {1}: (1, {})} | custom-call | flops 2000000 | tf_op jit(solution)/shard_map/finish_grads/pallas_call | solution.py:259
  187.0 4.4 %finish_grads.3 = (bf16[512,2048]{1,0:T(8,128)(2,1)}, bf16[512,2048]{1,0:T(8,128)(2,1)}) custom-call(bf16[512,2048]{1,0:T(8,128)(2,1)} %get-tuple-element.76.dk_ref, bf16[512,2048]{1,0:T(8,128)(2,1)} %get-tuple-element.77.dv_ref, bf16[2,256,1024]{2,1,0:T(8,128)(2,1)} %copy-done.7, ...), custom_call_target="tpu_custom_call", output_to_operand_aliasing={{0}: (0, {}), {1}: (1, {})} | custom-call | flops 2000000 | tf_op jit(solution)/shard_map/finish_grads/pallas_call | solution.py:259
  (78 shorter events, 36.4 us)
Async XLA Ops:
  5.4 17.8 %collective-permute-start.1 = (bf16[128,4096]{1,0:T(8,128)(2,1)S(1)}, bf16[128,4096]{1,0:T(8,128)(2,1)}, u32[]{:S(2)}, u32[]{:S(2)}) collective-permute-start(bf16[128,4096]{1,0:T(8,128)(2,1)S(1)} %pad_maximum_fusion.1), channel_id=1, source_target_pairs={{1,0},{2,1},{3,2},{4,3},{5,4},{6,5},{7,6},{8,7},{9,8},{10,9},{11,1... | collective-permute-start | bytes 3145736 | tf_op jit(solution)/shard_map/ppermute | solution.py:415
  8.7 31.3 %all-to-all-start = ((bf16[4,128,2048]{2,1,0:T(8,128)(2,1)}), bf16[4,128,2048]{2,1,0:T(8,128)(2,1)}, u32[]{:S(2)}, u32[]{:S(2)}) async-start(bf16[4,128,2048]{2,1,0:T(8,128)(2,1)} %broadcast_in_dim.7), calls=%async_computation | async-start | bytes 4194304 | tf_op jit(solution)/shard_map/all_to_all | solution.py:436
  13.2 16.5 %collective-permute-start = (bf16[128,2048]{1,0:T(8,128)(2,1)}, bf16[128,2048]{1,0:T(8,128)(2,1)}, u32[]{:S(2)}, u32[]{:S(2)}) collective-permute-start(bf16[128,2048]{1,0:T(8,128)(2,1)} %constant_dynamic-slice_fusion), channel_id=1, source_target_pairs={{0,18},{2,16},{16,2},{18,0},{1,19},{3,17},{17,3},{19,1},{4,22},{6,... | collective-permute-start | bytes 1572872 | tf_op jit(solution)/shard_map/ppermute | solution.py:419
  17.2 8.7 %copy-start.14 = (s32[512]{0:T(512)S(1)}, s32[512]{0:T(512)}, u32[]{:S(2)}) copy-start(s32[512]{0:T(512)} %param.10) | copy-start | bytes 6148
  23.2 25.2 %collective-permute-start.3 = (bf16[256,4096]{1,0:T(8,128)(2,1)}, bf16[256,4096]{1,0:T(8,128)(2,1)S(1)}, u32[]{:S(2)}, u32[]{:S(2)}) collective-permute-start(bf16[256,4096]{1,0:T(8,128)(2,1)} %pad_maximum_fusion), channel_id=1, source_target_pairs={{0,1},{1,2},{2,3},{3,4},{4,5},{5,6},{6,7},{7,8},{8,9},{9,10},{10,1... | collective-permute-start | bytes 6291464 | tf_op jit(solution)/shard_map/ppermute | solution.py:415
  25.1 32.8 %collective-permute-start.5 = (bf16[512,2048]{1,0:T(8,128)(2,1)}, bf16[512,2048]{1,0:T(8,128)(2,1)}, u32[]{:S(2)}, u32[]{:S(2)}) collective-permute-start(bf16[512,2048]{1,0:T(8,128)(2,1)} %cot_ref.2), channel_id=1, source_target_pairs={{0,1},{1,0},{2,3},{3,2},{4,5},{5,4},{6,7},{7,6},{8,9},{9,8},{10,11... | collective-permute-start | bytes 6291464 | tf_op jit(solution)/shard_map/ppermute | solution.py:409
  40.1 17.9 %collective-permute-start.6 = (bf16[4,128,2048]{2,1,0:T(8,128)(2,1)}, bf16[4,128,2048]{2,1,0:T(8,128)(2,1)}, u32[]{:S(2)}, u32[]{:S(2)}) collective-permute-start(bf16[4,128,2048]{2,1,0:T(8,128)(2,1)} %all-to-all-done.in_ref.refs_0_), channel_id=1, source_target_pairs={{0,1},{1,0},{2,3},{3,2},{4,5},{5,4},{6,7},{7,6},{8,9},{9,8},{10,11... | collective-permute-start | bytes 6291464 | tf_op jit(solution)/shard_map/ppermute | solution.py:409
  40.6 29.5 %all-to-all-start.1 = ((bf16[4,96,2048]{2,1,0:T(8,128)(2,1)}), bf16[4,96,2048]{2,1,0:T(8,128)(2,1)}, u32[]{:S(2)}, u32[]{:S(2)}) async-start(bf16[4,96,2048]{2,1,0:T(8,128)(2,1)} %broadcast_in_dim.6), calls=%async_computation.1 | async-start | bytes 3145728 | tf_op jit(solution)/shard_map/all_to_all | solution.py:448
  44.9 2.0 %collective-permute-start.2 = (bf16[256,1024]{1,0:T(8,128)(2,1)S(1)}, bf16[256,1024]{1,0:T(8,128)(2,1)S(1)}, u32[]{:S(2)}, u32[]{:S(2)}) collective-permute-start(bf16[256,1024]{1,0:T(8,128)(2,1)S(1)} %copy-done.15), channel_id=1, source_target_pairs={{0,1},{1,0},{2,3},{3,2},{4,5},{5,4},{6,7},{7,6},{8,9},{9,8},{10,11... | collective-permute-start | bytes 1572872 | tf_op jit(solution)/shard_map/ppermute | solution.py:409
  46.9 13.1 %copy-start.9 = (bf16[256,1024]{1,0:T(8,128)(2,1)}, bf16[256,1024]{1,0:T(8,128)(2,1)S(1)}, u32[]{:S(2)}) copy-start(bf16[256,1024]{1,0:T(8,128)(2,1)S(1)} %collective-permute-done.2.peer_late_ref) | copy-start | bytes 1572868
  57.8 2.2 %collective-permute-start.4 = (bf16[256,1024]{1,0:T(8,128)(2,1)}, bf16[256,1024]{1,0:T(8,128)(2,1)S(1)}, u32[]{:S(2)}, u32[]{:S(2)}) collective-permute-start(bf16[256,1024]{1,0:T(8,128)(2,1)} %get-tuple-element.51), channel_id=1, source_target_pairs={{0,1},{1,0},{2,3},{3,2},{4,5},{5,4},{6,7},{7,6},{8,9},{9,8},{10,11... | collective-permute-start | bytes 1572872 | tf_op jit(solution)/shard_map/ppermute | solution.py:409
  70.0 64.4 %all-to-all-start.2 = ((bf16[4,256,2048]{2,1,0:T(8,128)(2,1)}), bf16[4,256,2048]{2,1,0:T(8,128)(2,1)}, u32[]{:S(2)}, u32[]{:S(2)}) async-start(bf16[4,256,2048]{2,1,0:T(8,128)(2,1)} %bitcast.7), calls=%async_computation.2 | async-start | bytes 8388608 | tf_op jit(solution)/shard_map/all_to_all | solution.py:459
  75.1 19.1 %collective-permute-start.8 = (bf16[4,96,2048]{2,1,0:T(8,128)(2,1)}, bf16[4,96,2048]{2,1,0:T(8,128)(2,1)S(1)}, u32[]{:S(2)}, u32[]{:S(2)}) collective-permute-start(bf16[4,96,2048]{2,1,0:T(8,128)(2,1)} %all-to-all-done.1.refs_1_), channel_id=1, source_target_pairs={{0,1},{1,0},{2,3},{3,2},{4,5},{5,4},{6,7},{7,6},{8,9},{9,8},{10,11... | collective-permute-start | bytes 4718600 | tf_op jit(solution)/shard_map/ppermute | solution.py:409
  75.3 16.7 %collective-permute-start.7 = (bf16[4,32,2048]{2,1,0:T(8,128)(2,1)S(1)}, bf16[4,32,2048]{2,1,0:T(8,128)(2,1)S(1)}, u32[]{:S(2)}, u32[]{:S(2)}) collective-permute-start(bf16[4,32,2048]{2,1,0:T(8,128)(2,1)S(1)} %copy-done.8), channel_id=1, source_target_pairs={{0,18},{2,16},{16,2},{18,0},{1,19},{3,17},{17,3},{19,1},{4,22},{6,... | collective-permute-start | bytes 1572872 | tf_op jit(solution)/shard_map/ppermute | solution.py:419
  92.0 2.1 %collective-permute-start.9 = (bf16[4,32,2048]{2,1,0:T(8,128)(2,1)S(1)}, bf16[4,32,2048]{2,1,0:T(8,128)(2,1)S(1)}, u32[]{:S(2)}, u32[]{:S(2)}) collective-permute-start(bf16[4,32,2048]{2,1,0:T(8,128)(2,1)S(1)} %collective-permute-done.7.refs_2_), channel_id=1, source_target_pairs={{0,1},{1,0},{2,3},{3,2},{4,5},{5,4},{6,7},{7,6},{8,9},{9,8},{10,11... | collective-permute-start | bytes 1572872 | tf_op jit(solution)/shard_map/ppermute | solution.py:409
  116.6 21.5 %collective-permute-start.11 = (bf16[2,256,1024]{2,1,0:T(8,128)(2,1)}, bf16[2,256,1024]{2,1,0:T(8,128)(2,1)S(1)}, u32[]{:S(2)}, u32[]{:S(2)}) collective-permute-start(bf16[2,256,1024]{2,1,0:T(8,128)(2,1)} %get-tuple-element.67), channel_id=1, source_target_pairs={{1,0},{2,1},{3,2},{4,3},{5,4},{6,5},{7,6},{8,7},{9,8},{10,9},{11,1... | collective-permute-start | bytes 3145736 | tf_op jit(solution)/shard_map/ppermute | solution.py:415
  118.9 19.2 %collective-permute-start.10 = (bf16[2,112,1024]{2,1,0:T(8,128)(2,1)}, bf16[2,112,1024]{2,1,0:T(8,128)(2,1)S(1)}, u32[]{:S(2)}, u32[]{:S(2)}) collective-permute-start(bf16[2,112,1024]{2,1,0:T(8,128)(2,1)} %get-tuple-element.66), channel_id=1, source_target_pairs={{0,1},{1,2},{2,3},{3,4},{4,5},{5,6},{6,7},{7,8},{8,9},{9,10},{10,1... | collective-permute-start | bytes 1376264 | tf_op jit(solution)/shard_map/ppermute | solution.py:415
  132.5 19.1 %collective-permute-start.12 = (bf16[2,256,1024]{2,1,0:T(8,128)(2,1)}, bf16[2,256,1024]{2,1,0:T(8,128)(2,1)}, u32[]{:S(2)}, u32[]{:S(2)}) collective-permute-start(bf16[2,256,1024]{2,1,0:T(8,128)(2,1)} %get-tuple-element.69), channel_id=1, source_target_pairs={{1,0},{2,1},{3,2},{4,3},{5,4},{6,5},{7,6},{8,7},{9,8},{10,9},{11,1... | collective-permute-start | bytes 3145736 | tf_op jit(solution)/shard_map/ppermute | solution.py:415
  138.1 23.6 %copy-start.11 = (bf16[2,112,1024]{2,1,0:T(8,128)(2,1)}, bf16[2,112,1024]{2,1,0:T(8,128)(2,1)S(1)}, u32[]{:S(2)}) copy-start(bf16[2,112,1024]{2,1,0:T(8,128)(2,1)S(1)} %collective-permute-done.10.first_ref) | copy-start | bytes 1376260
  138.1 23.6 %copy-start.7 = (bf16[2,256,1024]{2,1,0:T(8,128)(2,1)}, bf16[2,256,1024]{2,1,0:T(8,128)(2,1)S(1)}, u32[]{:S(2)}) copy-start(bf16[2,256,1024]{2,1,0:T(8,128)(2,1)S(1)} %collective-permute-done.11.first_ref) | copy-start | bytes 3145732
  138.1 23.6 %all-to-all-start.3 = ((bf16[16,16,2048]{2,1,0:T(8,128)(2,1)}), bf16[16,16,2048]{2,1,0:T(8,128)(2,1)S(1)}, u32[]{:S(2)}, u32[]{:S(2)}) async-start(bf16[16,16,2048]{2,1,0:T(8,128)(2,1)} %bitcast.8), calls=%async_computation.3 | async-start | bytes 2097152 | tf_op jit(solution)/shard_map/all_to_all | solution.py:471
  145.2 37.3 %collective-permute-start.13 = (bf16[2,112,1024]{2,1,0:T(8,128)(2,1)}, bf16[2,112,1024]{2,1,0:T(8,128)(2,1)S(1)}, u32[]{:S(2)}, u32[]{:S(2)}) collective-permute-start(bf16[2,112,1024]{2,1,0:T(8,128)(2,1)} %get-tuple-element.75), channel_id=1, source_target_pairs={{0,1},{1,2},{2,3},{3,4},{4,5},{5,6},{6,7},{7,8},{8,9},{9,10},{10,1... | collective-permute-start | bytes 1376264 | tf_op jit(solution)/shard_map/ppermute | solution.py:415
  164.9 27.5 %all-to-all-start.4 = ((bf16[8,16,2048]{2,1,0:T(8,128)(2,1)}), bf16[8,16,2048]{2,1,0:T(8,128)(2,1)S(1)}, u32[]{:S(2)}, u32[]{:S(2)}) async-start(bf16[8,16,2048]{2,1,0:T(8,128)(2,1)} %sum_pieces.3), calls=%async_computation.4 | async-start | bytes 1048576 | tf_op jit(solution)/shard_map/all_to_all | solution.py:474
  192.4 2.3 %collective-permute-start.14 = (bf16[128,2048]{1,0:T(8,128)(2,1)S(1)}, bf16[128,2048]{1,0:T(8,128)(2,1)S(1)}, u32[]{:S(2)}, u32[]{:S(2)}) collective-permute-start(bf16[128,2048]{1,0:T(8,128)(2,1)S(1)} %bitcast.9), channel_id=1, source_target_pairs={{0,1},{1,0},{2,3},{3,2},{4,5},{5,4},{6,7},{7,6},{8,9},{9,8},{10,11... | collective-permute-start | bytes 1572872 | tf_op jit(solution)/shard_map/ppermute | solution.py:409
  (16 other events, 41.8 us)

commit v6 on v4

--- a/solution.py
+++ b/solution.py
@@ -273,31 +273,6 @@
         cost_estimate=cost(2e9),
         name="finish_grads",
     )(dk, dv, *from_prev, *from_next)
-
-
-def scale_kernel(core_ref, mine_ref, other_ref, out_ref):
-    core = core_ref[0]
-    scale = float(TOKENS) ** -0.5
-    out_ref[core] = mine_ref[...].astype(jnp.float32) * scale
-    out_ref[1 - core] = other_ref[...].astype(jnp.float32) * scale
-
-
-def scale_rows(core, mine, other):
-    tile = 1024
-    rows = pl.BlockSpec((HEAD_DIM, tile), lambda i, *_: (0, i))
-    return pl.pallas_call(
-        scale_kernel,
-        grid_spec=pltpu.PrefetchScalarGridSpec(
-            num_scalar_prefetch=1,
-            grid=(WIDTH // tile,),
-            in_specs=[rows, rows],
-            out_specs=pl.BlockSpec((2, HEAD_DIM, tile), lambda i, *_: (0, 0, i)),
-        ),
-        out_shape=jax.ShapeDtypeStruct((2, HEAD_DIM, WIDTH), jnp.float32),
-        compiler_params=params(),
-        cost_estimate=cost(1e9),
-        name="scale_rows",
-    )(core, mine, other).reshape(2 * HEAD_DIM, WIDTH)
 
 
 def weight_sums_kernel(core_ref, early_ref, late_ref, peer_early_ref, peer_late_ref, cot_ref, cot_peer_ref, out_ref):
@@ -483,7 +458,10 @@
     rows_mine = lax.all_to_all(summed, ("x", "zl"), 0, 0, tiled=True).reshape(HEAD_DIM, WIDTH)
     key_grad, value_grad = finish(tied(dk, summed), dv, from_prev, from_next)
     rows_mine = tied(rows_mine, key_grad)
-    weight_grad = scale_rows(core_arg, rows_mine, swapped(rows_mine))
+    rows_other = swapped(rows_mine)
+    first = jnp.where(core == 0, rows_mine, rows_other)
+    second = jnp.where(core == 0, rows_other, rows_mine)
+    weight_grad = jnp.concatenate([first, second], axis=0).astype(jnp.float32) * (float(TOKENS) ** -0.5)
     return (layer_out, dq, key_grad, value_grad, weight_grad)
 
 

time: 177 us -> 175 us (0.989)
  Pallas kernels: 79.1 us -> 76.5 us
    pallas_call x1 -> x0, Pallas kernels: 2.42 us -> none  [scale_rows(): pl.pallas_call(scale_kernel, grid_spec=pltpu.PrefetchScalarGridSpec(num_s...]
    unnamed x30 -> x26, local copies, waits for them, and re-layouts: 7.21 us -> 6.4 us
where the time goes in v6:
time: 175 us; the launch traced here: 174 us
  Pallas kernels  76.5 us (44%)
  starting transfers between devices  52.6 us (30%)
  waiting for transfers between devices  27.3 us (16%)
  local copies, waits for them, and re-layouts  12.5 us (7%)
  other arithmetic  4.4 us (3%)
    pallas_call x2, Pallas kernels, backward(): pl.pallas_call(backward_kernel, grid=(steps,), in_specs=[fixed((1, TOK)),...  20.5 us
    ppermute x6, starting transfers between devices, passed_along(): return lax.ppermute(array, GROUP_AXES, pairs)  17.2 us
    pallas_call x2, Pallas kernels, forward(): pl.pallas_call(functools.partial(forward_kernel, late=late), grid_spec=pl...  15.7 us
    pallas_call x1, Pallas kernels, grad_attention(): pl.pallas_call(grad_attn_kernel, grid_spec=pltpu.PrefetchScalarGridSpec(n...  10.1 us
    pallas_call x1, Pallas kernels, project(): pl.pallas_call(project_kernel, grid_spec=pltpu.PrefetchScalarGridSpec(num...  9.98 us
    pallas_call x1, Pallas kernels, weight_sums(): pl.pallas_call(weight_sums_kernel, grid_spec=pltpu.PrefetchScalarGridSpec...  9.15 us
    all_to_all x1, waiting for transfers between devices, on_device(): lax.all_to_all(tied(sums.reshape(4, 2 * HEAD_DIM, WIDTH), far), 'y', 0, 0...  8.81 us
    all_to_all x1, starting transfers between devices, on_device(): shares = lax.all_to_all(partial, ('zh', 'x', 'zl'), 0, 0, tiled=True)  7.61 us
  transfers between devices with their start and end apart: 18, of which 10 were waited for; matrix products, arithmetic and copies ran while one was open for 3% of the time, Pallas kernels for 44%

profile of v6, /device:TPU:1, one launch (start us, length us, event | category | flops | bytes accessed | tf_op | source)
XLA Modules:
  0.0 174.2 jit_solution(17823739743220384594)
XLA Ops:
  2.8 2.6 %broadcast_in_dim.7 = bf16[4,128,2048]{2,1,0:T(8,128)(2,1)} broadcast(bf16[128,2048]{1,0:T(8,128)(2,1)} %constant_dynamic-slice_fusion), dimensions={1,2} | broadcast | bytes 2621440 | tf_op jit(solution)/shard_map/broadcast_in_dim | solution.py:421
  5.4 3.3 %collective-permute-start.1 = (bf16[128,4096]{1,0:T(8,128)(2,1)S(1)}, bf16[128,4096]{1,0:T(8,128)(2,1)}, u32[]{:S(2)}, u32[]{:S(2)}) collective-permute-start(bf16[128,4096]{1,0:T(8,128)(2,1)S(1)} %pad_maximum_fusion.1), channel_id=1, source_target_pairs={{1,0},{2,1},{3,2},{4,3},{5,4},{6,5},{7,6},{8,7},{9,8},{10,9},{11,1... | collective-permute-start | bytes 3145736 | tf_op jit(solution)/shard_map/ppermute | solution.py:401
  8.7 4.5 %all-to-all-start = ((bf16[4,128,2048]{2,1,0:T(8,128)(2,1)}), bf16[4,128,2048]{2,1,0:T(8,128)(2,1)}, u32[]{:S(2)}, u32[]{:S(2)}) async-start(bf16[4,128,2048]{2,1,0:T(8,128)(2,1)} %broadcast_in_dim.7), calls=%async_computation | async-start | bytes 4194304 | tf_op jit(solution)/shard_map/all_to_all | solution.py:422
  13.3 3.9 %collective-permute-start = (bf16[128,2048]{1,0:T(8,128)(2,1)}, bf16[128,2048]{1,0:T(8,128)(2,1)}, u32[]{:S(2)}, u32[]{:S(2)}) collective-permute-start(bf16[128,2048]{1,0:T(8,128)(2,1)} %constant_dynamic-slice_fusion), channel_id=1, source_target_pairs={{0,18},{2,16},{16,2},{18,0},{1,19},{3,17},{17,3},{19,1},{4,22},{6,... | collective-permute-start | bytes 1572872 | tf_op jit(solution)/shard_map/ppermute | solution.py:405
  18.7 4.5 %collective-permute-done.1.kh_ref.vh_ref.ka_ref.va_ref = bf16[128,4096]{1,0:T(8,128)(2,1)} collective-permute-done((bf16[128,4096]{1,0:T(8,128)(2,1)S(1)}, bf16[128,4096]{1,0:T(8,128)(2,1)}, u32[]{:S(2)}, u32[]{:S(2)}) %collective-permute-start.1) | collective-permute-done | bytes 1048608 | tf_op jit(solution)/shard_map/ppermute | solution.py:401
  26.4 3.3 %collective-permute-done = bf16[128,2048]{1,0:T(8,128)(2,1)} collective-permute-done((bf16[128,2048]{1,0:T(8,128)(2,1)}, bf16[128,2048]{1,0:T(8,128)(2,1)}, u32[]{:S(2)}, u32[]{:S(2)}) %collective-permute-start) | collective-permute-done | bytes 524320 | tf_op jit(solution)/shard_map/ppermute | solution.py:405
  29.8 2.6 %broadcast_in_dim.6 = bf16[4,128,2048]{2,1,0:T(8,128)(2,1)} broadcast(bf16[128,2048]{1,0:T(8,128)(2,1)} %collective-permute-done), dimensions={1,2} | broadcast | bytes 2621440 | tf_op jit(solution)/shard_map/broadcast_in_dim | solution.py:430
  32.4 7.8 %attend_late.1 = (bf16[256,2048]{1,0:T(8,128)(2,1)}, bf16[256,1024]{1,0:T(8,128)(2,1)}, f32[16,1,256]{2,1,0:T(1,128)}) custom-call(s32[1]{0:T(128)} %bitcast.core_ref, s32[1,512]{1,0:T(1,128)} %bitcast.15, s32[1,512]{1,0:T(1,128)} %bitcast.11, bf16[512,2048]{1,0:T(8,128)(2,1)} %q_ref.5, bf16[512,2048]{1,0:T(8,128)(2,1)} %ko_ref.7, ...), custom_call_target="tpu_custom_call" | custom-call | flops 8000000 | tf_op jit(solution)/shard_map/attend_late/pallas_call | solution.py:135
  40.8 4.4 %all-to-all-start.1 = ((bf16[4,128,2048]{2,1,0:T(8,128)(2,1)}), bf16[4,128,2048]{2,1,0:T(8,128)(2,1)}, u32[]{:S(2)}, u32[]{:S(2)}) async-start(bf16[4,128,2048]{2,1,0:T(8,128)(2,1)} %broadcast_in_dim.6), calls=%async_computation.1 | async-start | bytes 4194304 | tf_op jit(solution)/shard_map/all_to_all | solution.py:434
  49.7 8.0 %attend_early.1 = (bf16[256,2048]{1,0:T(8,128)(2,1)}, bf16[256,1024]{1,0:T(8,128)(2,1)}, f32[16,1,256]{2,1,0:T(1,128)}) custom-call(s32[1]{0:T(128)} %bitcast.core_ref, s32[1,512]{1,0:T(1,128)} %bitcast.16, s32[1,512]{1,0:T(1,128)} %bitcast.12, bf16[512,2048]{1,0:T(8,128)(2,1)} %q_ref.5, bf16[512,2048]{1,0:T(8,128)(2,1)} %ko_ref.7, ...), custom_call_target="tpu_custom_call" | custom-call | flops 8000000 | tf_op jit(solution)/shard_map/attend_early/pallas_call | solution.py:135
  60.7 9.1 %weight_sums.1 = bf16[1024,2048]{1,0:T(8,128)(2,1)} custom-call(s32[1]{0:T(128)} %bitcast.core_ref, bf16[256,2048]{1,0:T(8,128)(2,1)} %get-tuple-element.66.early_ref, bf16[256,2048]{1,0:T(8,128)(2,1)} %get-tuple-element.46.late_ref, bf16[256,1024]{1,0:T(8,128)(2,1)} %copy-done.7, bf16[256,1024]{1,0:T(8,128)(2,1)} %copy-done.6, bf16[512,2048]{1,0:T(8,128)(2,1)} %cot_ref.2, ...), custom_call_target="tpu_custom_call" | custom-call | flops 7000000 | tf_op jit(solution)/shard_map/weight_sums/pallas_call | solution.py:291
  72.6 5.0 %all-to-all-start.2 = ((bf16[4,256,2048]{2,1,0:T(8,128)(2,1)}), bf16[4,256,2048]{2,1,0:T(8,128)(2,1)}, u32[]{:S(2)}, u32[]{:S(2)}) async-start(bf16[4,256,2048]{2,1,0:T(8,128)(2,1)} %bitcast.7), calls=%async_computation.2 | async-start | bytes 8388608 | tf_op jit(solution)/shard_map/all_to_all | solution.py:442
  79.6 10.1 %grad_attention.1.g_ref = bf16[512,2048]{1,0:T(8,128)(2,1)} custom-call(s32[2]{0:T(128)} %pad_add_fusion.place_ref, bf16[512,2048]{1,0:T(8,128)(2,1)} %cot_ref.2, bf16[4,128,2048]{2,1,0:T(8,128)(2,1)} %all-to-all-done.refs_0_, bf16[4,128,2048]{2,1,0:T(8,128)(2,1)} %all-to-all-done.1.refs_1_, bf16[4,128,2048]{2,1,0:T(8,128)(2,1)} %collective-permute-done.6.refs_2_, ...), custom_call_target="tpu_custom_call" | custom-call | flops 7000000 | tf_op jit(solution)/shard_map/grad_attention/pallas_call | solution.py:324
  89.7 10.1 %attend_backward_first.1 = (bf16[512,2048]{1,0:T(8,128)(2,1)}, bf16[512,2048]{1,0:T(8,128)(2,1)}, bf16[512,2048]{1,0:T(8,128)(2,1)}, bf16[2,256,1024]{2,1,0:T(8,128)(2,1)}, bf16[2,112,1024]{2,1,0:T(8,128)(2,1)}) custom-call(s32[1,512]{1,0:T(1,128)} %bitcast.17, s32[1,512]{1,0:T(1,128)} %bitcast.13, f32[16,1,256]{2,1,0:T(1,128)} %get-tuple-element.54.lse_early_ref, ...), custom_call_target="tpu_custom_call" | custom-call | flops 10000000 | tf_op jit(solution)/shard_map/attend_backward_first/pallas_call | solution.py:225
  101.8 3.6 %collective-permute-start.8 = (bf16[2,112,1024]{2,1,0:T(8,128)(2,1)}, bf16[2,112,1024]{2,1,0:T(8,128)(2,1)S(1)}, u32[]{:S(2)}, u32[]{:S(2)}) collective-permute-start(bf16[2,112,1024]{2,1,0:T(8,128)(2,1)} %get-tuple-element.62), channel_id=1, source_target_pairs={{0,1},{1,2},{2,3},{3,4},{4,5},{5,6},{6,7},{7,8},{8,9},{9,10},{10,1... | collective-permute-start | bytes 1376264 | tf_op jit(solution)/shard_map/ppermute | solution.py:401
  105.4 10.4 %attend_backward_second.1 = (bf16[512,2048]{1,0:T(8,128)(2,1)}, bf16[512,2048]{1,0:T(8,128)(2,1)}, bf16[512,2048]{1,0:T(8,128)(2,1)}, bf16[2,256,1024]{2,1,0:T(8,128)(2,1)}, bf16[2,112,1024]{2,1,0:T(8,128)(2,1)}) custom-call(s32[1,512]{1,0:T(1,128)} %bitcast.18, s32[1,512]{1,0:T(1,128)} %bitcast.14, ...), custom_call_target="tpu_custom_call", output_to_operand_aliasing={{0}: (12, {}), {1}: (13, {}), {2}: (14, {})} | custom-call | flops 10000000 | tf_op jit(solution)/shard_map/attend_backward_second/pallas_call | solution.py:225
  117.7 8.8 %all-to-all-done.2.pieces_ref = bf16[4,256,2048]{2,1,0:T(8,128)(2,1)} async-done(((bf16[4,256,2048]{2,1,0:T(8,128)(2,1)}), bf16[4,256,2048]{2,1,0:T(8,128)(2,1)}, u32[]{:S(2)}, u32[]{:S(2)}) %all-to-all-start.2) | async-done | bytes 4194336 | tf_op jit(solution)/shard_map/all_to_all | solution.py:442
  126.6 3.3 %sum_pieces.2 = bf16[1,256,2048]{2,1,0:T(8,128)(2,1)} custom-call(bf16[4,256,2048]{2,1,0:T(8,128)(2,1)} %all-to-all-done.2.pieces_ref), custom_call_target="tpu_custom_call" | custom-call | flops 2000000 | tf_op jit(solution)/shard_map/sum_pieces/pallas_call | solution.py:382
  129.8 7.6 %all-to-all-start.3 = ((bf16[16,16,2048]{2,1,0:T(8,128)(2,1)}), bf16[16,16,2048]{2,1,0:T(8,128)(2,1)S(1)}, u32[]{:S(2)}, u32[]{:S(2)}) async-start(bf16[16,16,2048]{2,1,0:T(8,128)(2,1)} %bitcast.8), calls=%async_computation.3 | async-start | bytes 2097152 | tf_op jit(solution)/shard_map/all_to_all | solution.py:455
  137.5 4.5 %collective-permute-start.11 = (bf16[2,112,1024]{2,1,0:T(8,128)(2,1)}, bf16[2,112,1024]{2,1,0:T(8,128)(2,1)S(1)}, u32[]{:S(2)}, u32[]{:S(2)}) collective-permute-start(bf16[2,112,1024]{2,1,0:T(8,128)(2,1)} %get-tuple-element.71), channel_id=1, source_target_pairs={{0,1},{1,2},{2,3},{3,4},{4,5},{5,6},{6,7},{7,8},{8,9},{9,10},{10,1... | collective-permute-start | bytes 1376264 | tf_op jit(solution)/shard_map/ppermute | solution.py:401
  142.0 10.0 %project.1 = bf16[512,2048]{1,0:T(8,128)(2,1)} custom-call(s32[2]{0:T(128)} %pad_add_fusion.place_ref, bf16[256,2048]{1,0:T(8,128)(2,1)} %get-tuple-element.66.early_ref, bf16[256,2048]{1,0:T(8,128)(2,1)} %get-tuple-element.46.late_ref, bf16[4,128,2048]{2,1,0:T(8,128)(2,1)} %all-to-all-done.refs_0_, bf16[4,128,2048]{2,1,0:T(8,128)(2,1)} %all-to-all-done.1.refs_1_, ...), custom_call_target="tpu_custom_call" | custom-call | flops 8000000 | tf_op jit(solution)/shard_map/project/pallas_call | solution.py:355
  156.7 3.5 %all-to-all-start.4 = ((bf16[8,16,2048]{2,1,0:T(8,128)(2,1)}), bf16[8,16,2048]{2,1,0:T(8,128)(2,1)S(1)}, u32[]{:S(2)}, u32[]{:S(2)}) async-start(bf16[8,16,2048]{2,1,0:T(8,128)(2,1)} %sum_pieces.3), calls=%async_computation.4 | async-start | bytes 1048576 | tf_op jit(solution)/shard_map/all_to_all | solution.py:458
  161.0 5.6 %finish_grads.1 = (bf16[512,2048]{1,0:T(8,128)(2,1)}, bf16[512,2048]{1,0:T(8,128)(2,1)}) custom-call(bf16[512,2048]{1,0:T(8,128)(2,1)} %get-tuple-element.69.dk_ref, bf16[512,2048]{1,0:T(8,128)(2,1)} %get-tuple-element.70.dv_ref, bf16[2,112,1024]{2,1,0:T(8,128)(2,1)} %copy-done.8, bf16[2,112,1024]{2,1,0:T(8,128)(2,1)} %copy-done.9, ...), custom_call_target="tpu_custom_call" | custom-call | flops 2000000 | tf_op jit(solution)/shard_map/finish_grads/pallas_call | solution.py:266
  167.3 3.7 %collective-permute-start.12 = (bf16[128,2048]{1,0:T(8,128)(2,1)S(1)}, bf16[128,2048]{1,0:T(8,128)(2,1)S(1)}, u32[]{:S(2)}, u32[]{:S(2)}) collective-permute-start(bf16[128,2048]{1,0:T(8,128)(2,1)S(1)} %bitcast.9), channel_id=1, source_target_pairs={{0,1},{1,0},{2,3},{3,2},{4,5},{5,4},{6,7},{7,6},{8,9},{9,8},{10,11... | collective-permute-start | bytes 1572872 | tf_op jit(solution)/shard_map/ppermute | solution.py:395
  (65 shorter events, 32.9 us)
Async XLA Ops:
  5.4 17.8 %collective-permute-start.1 = (bf16[128,4096]{1,0:T(8,128)(2,1)S(1)}, bf16[128,4096]{1,0:T(8,128)(2,1)}, u32[]{:S(2)}, u32[]{:S(2)}) collective-permute-start(bf16[128,4096]{1,0:T(8,128)(2,1)S(1)} %pad_maximum_fusion.1), channel_id=1, source_target_pairs={{1,0},{2,1},{3,2},{4,3},{5,4},{6,5},{7,6},{8,7},{9,8},{10,9},{11,1... | collective-permute-start | bytes 3145736 | tf_op jit(solution)/shard_map/ppermute | solution.py:401
  8.7 31.4 %all-to-all-start = ((bf16[4,128,2048]{2,1,0:T(8,128)(2,1)}), bf16[4,128,2048]{2,1,0:T(8,128)(2,1)}, u32[]{:S(2)}, u32[]{:S(2)}) async-start(bf16[4,128,2048]{2,1,0:T(8,128)(2,1)} %broadcast_in_dim.7), calls=%async_computation | async-start | bytes 4194304 | tf_op jit(solution)/shard_map/all_to_all | solution.py:422
  13.3 16.5 %collective-permute-start = (bf16[128,2048]{1,0:T(8,128)(2,1)}, bf16[128,2048]{1,0:T(8,128)(2,1)}, u32[]{:S(2)}, u32[]{:S(2)}) collective-permute-start(bf16[128,2048]{1,0:T(8,128)(2,1)} %constant_dynamic-slice_fusion), channel_id=1, source_target_pairs={{0,18},{2,16},{16,2},{18,0},{1,19},{3,17},{17,3},{19,1},{4,22},{6,... | collective-permute-start | bytes 1572872 | tf_op jit(solution)/shard_map/ppermute | solution.py:405
  17.2 8.7 %copy-start.10 = (s32[512]{0:T(512)S(1)}, s32[512]{0:T(512)}, u32[]{:S(2)}) copy-start(s32[512]{0:T(512)} %param.11) | copy-start | bytes 6148
  17.2 8.7 %copy-start.11 = (s32[512]{0:T(512)S(1)}, s32[512]{0:T(512)}, u32[]{:S(2)}) copy-start(s32[512]{0:T(512)} %param.10) | copy-start | bytes 6148
  23.2 25.2 %collective-permute-start.3 = (bf16[256,4096]{1,0:T(8,128)(2,1)}, bf16[256,4096]{1,0:T(8,128)(2,1)S(1)}, u32[]{:S(2)}, u32[]{:S(2)}) collective-permute-start(bf16[256,4096]{1,0:T(8,128)(2,1)} %pad_maximum_fusion), channel_id=1, source_target_pairs={{0,1},{1,2},{2,3},{3,4},{4,5},{5,6},{6,7},{7,8},{8,9},{9,10},{10,1... | collective-permute-start | bytes 6291464 | tf_op jit(solution)/shard_map/ppermute | solution.py:401
  25.1 32.6 %collective-permute-start.5 = (bf16[512,2048]{1,0:T(8,128)(2,1)}, bf16[512,2048]{1,0:T(8,128)(2,1)}, u32[]{:S(2)}, u32[]{:S(2)}) collective-permute-start(bf16[512,2048]{1,0:T(8,128)(2,1)} %cot_ref.2), channel_id=1, source_target_pairs={{0,1},{1,0},{2,3},{3,2},{4,5},{5,4},{6,7},{7,6},{8,9},{9,8},{10,11... | collective-permute-start | bytes 6291464 | tf_op jit(solution)/shard_map/ppermute | solution.py:395
  40.2 5.1 %copy-start.12 = (bf16[256,1024]{1,0:T(8,128)(2,1)S(1)}, bf16[256,1024]{1,0:T(8,128)(2,1)}, u32[]{:S(2)}) copy-start(bf16[256,1024]{1,0:T(8,128)(2,1)} %get-tuple-element.42) | copy-start | bytes 1572868
  40.2 17.6 %collective-permute-start.6 = (bf16[4,128,2048]{2,1,0:T(8,128)(2,1)}, bf16[4,128,2048]{2,1,0:T(8,128)(2,1)}, u32[]{:S(2)}, u32[]{:S(2)}) collective-permute-start(bf16[4,128,2048]{2,1,0:T(8,128)(2,1)} %all-to-all-done.refs_0_), channel_id=1, source_target_pairs={{0,1},{1,0},{2,3},{3,2},{4,5},{5,4},{6,7},{7,6},{8,9},{9,8},{10,11... | collective-permute-start | bytes 6291464 | tf_op jit(solution)/shard_map/ppermute | solution.py:395
  40.8 30.8 %all-to-all-start.1 = ((bf16[4,128,2048]{2,1,0:T(8,128)(2,1)}), bf16[4,128,2048]{2,1,0:T(8,128)(2,1)}, u32[]{:S(2)}, u32[]{:S(2)}) async-start(bf16[4,128,2048]{2,1,0:T(8,128)(2,1)} %broadcast_in_dim.6), calls=%async_computation.1 | async-start | bytes 4194304 | tf_op jit(solution)/shard_map/all_to_all | solution.py:434
  45.3 2.0 %collective-permute-start.2 = (bf16[256,1024]{1,0:T(8,128)(2,1)S(1)}, bf16[256,1024]{1,0:T(8,128)(2,1)S(1)}, u32[]{:S(2)}, u32[]{:S(2)}) collective-permute-start(bf16[256,1024]{1,0:T(8,128)(2,1)S(1)} %copy-done.12), channel_id=1, source_target_pairs={{0,1},{1,0},{2,3},{3,2},{4,5},{5,4},{6,7},{7,6},{8,9},{9,8},{10,11... | collective-permute-start | bytes 1572872 | tf_op jit(solution)/shard_map/ppermute | solution.py:395
  47.3 12.6 %copy-start.6 = (bf16[256,1024]{1,0:T(8,128)(2,1)}, bf16[256,1024]{1,0:T(8,128)(2,1)S(1)}, u32[]{:S(2)}) copy-start(bf16[256,1024]{1,0:T(8,128)(2,1)S(1)} %collective-permute-done.2.peer_late_ref) | copy-start | bytes 1572868
  57.7 2.2 %collective-permute-start.4 = (bf16[256,1024]{1,0:T(8,128)(2,1)}, bf16[256,1024]{1,0:T(8,128)(2,1)S(1)}, u32[]{:S(2)}, u32[]{:S(2)}) collective-permute-start(bf16[256,1024]{1,0:T(8,128)(2,1)} %get-tuple-element.47), channel_id=1, source_target_pairs={{0,1},{1,0},{2,3},{3,2},{4,5},{5,4},{6,7},{7,6},{8,9},{9,8},{10,11... | collective-permute-start | bytes 1572872 | tf_op jit(solution)/shard_map/ppermute | solution.py:395
  71.6 6.7 %collective-permute-start.7 = (bf16[4,128,2048]{2,1,0:T(8,128)(2,1)}, bf16[4,128,2048]{2,1,0:T(8,128)(2,1)S(1)}, u32[]{:S(2)}, u32[]{:S(2)}) collective-permute-start(bf16[4,128,2048]{2,1,0:T(8,128)(2,1)} %all-to-all-done.1.refs_1_), channel_id=1, source_target_pairs={{0,1},{1,0},{2,3},{3,2},{4,5},{5,4},{6,7},{7,6},{8,9},{9,8},{10,11... | collective-permute-start | bytes 6291464 | tf_op jit(solution)/shard_map/ppermute | solution.py:395
  72.6 53.9 %all-to-all-start.2 = ((bf16[4,256,2048]{2,1,0:T(8,128)(2,1)}), bf16[4,256,2048]{2,1,0:T(8,128)(2,1)}, u32[]{:S(2)}, u32[]{:S(2)}) async-start(bf16[4,256,2048]{2,1,0:T(8,128)(2,1)} %bitcast.7), calls=%async_computation.2 | async-start | bytes 8388608 | tf_op jit(solution)/shard_map/all_to_all | solution.py:442
  99.9 30.0 %collective-permute-start.9 = (bf16[2,256,1024]{2,1,0:T(8,128)(2,1)}, bf16[2,256,1024]{2,1,0:T(8,128)(2,1)S(1)}, u32[]{:S(2)}, u32[]{:S(2)}) collective-permute-start(bf16[2,256,1024]{2,1,0:T(8,128)(2,1)} %get-tuple-element.63), channel_id=1, source_target_pairs={{1,0},{2,1},{3,2},{4,3},{5,4},{6,5},{7,6},{8,7},{9,8},{10,9},{11,1... | collective-permute-start | bytes 3145736 | tf_op jit(solution)/shard_map/ppermute | solution.py:401
  101.8 28.0 %collective-permute-start.8 = (bf16[2,112,1024]{2,1,0:T(8,128)(2,1)}, bf16[2,112,1024]{2,1,0:T(8,128)(2,1)S(1)}, u32[]{:S(2)}, u32[]{:S(2)}) collective-permute-start(bf16[2,112,1024]{2,1,0:T(8,128)(2,1)} %get-tuple-element.62), channel_id=1, source_target_pairs={{0,1},{1,2},{2,3},{3,4},{4,5},{5,6},{6,7},{7,8},{8,9},{9,10},{10,1... | collective-permute-start | bytes 1376264 | tf_op jit(solution)/shard_map/ppermute | solution.py:401
  115.8 26.2 %collective-permute-start.10 = (bf16[2,256,1024]{2,1,0:T(8,128)(2,1)}, bf16[2,256,1024]{2,1,0:T(8,128)(2,1)}, u32[]{:S(2)}, u32[]{:S(2)}) collective-permute-start(bf16[2,256,1024]{2,1,0:T(8,128)(2,1)} %get-tuple-element.65), channel_id=1, source_target_pairs={{1,0},{2,1},{3,2},{4,3},{5,4},{6,5},{7,6},{8,7},{9,8},{10,9},{11,1... | collective-permute-start | bytes 3145736 | tf_op jit(solution)/shard_map/ppermute | solution.py:401
  129.8 22.1 %copy-start.8 = (bf16[2,112,1024]{2,1,0:T(8,128)(2,1)}, bf16[2,112,1024]{2,1,0:T(8,128)(2,1)S(1)}, u32[]{:S(2)}) copy-start(bf16[2,112,1024]{2,1,0:T(8,128)(2,1)S(1)} %collective-permute-done.8.prev_first_ref) | copy-start | bytes 1376260
  129.8 22.1 %copy-start.5 = (bf16[2,256,1024]{2,1,0:T(8,128)(2,1)}, bf16[2,256,1024]{2,1,0:T(8,128)(2,1)S(1)}, u32[]{:S(2)}) copy-start(bf16[2,256,1024]{2,1,0:T(8,128)(2,1)S(1)} %collective-permute-done.9.next_first_ref) | copy-start | bytes 3145732
  129.8 23.8 %all-to-all-start.3 = ((bf16[16,16,2048]{2,1,0:T(8,128)(2,1)}), bf16[16,16,2048]{2,1,0:T(8,128)(2,1)S(1)}, u32[]{:S(2)}, u32[]{:S(2)}) async-start(bf16[16,16,2048]{2,1,0:T(8,128)(2,1)} %bitcast.8), calls=%async_computation.3 | async-start | bytes 2097152 | tf_op jit(solution)/shard_map/all_to_all | solution.py:455
  137.5 22.8 %collective-permute-start.11 = (bf16[2,112,1024]{2,1,0:T(8,128)(2,1)}, bf16[2,112,1024]{2,1,0:T(8,128)(2,1)S(1)}, u32[]{:S(2)}, u32[]{:S(2)}) collective-permute-start(bf16[2,112,1024]{2,1,0:T(8,128)(2,1)} %get-tuple-element.71), channel_id=1, source_target_pairs={{0,1},{1,2},{2,3},{3,4},{4,5},{5,6},{6,7},{7,8},{8,9},{9,10},{10,1... | collective-permute-start | bytes 1376264 | tf_op jit(solution)/shard_map/ppermute | solution.py:401
  156.7 10.5 %all-to-all-start.4 = ((bf16[8,16,2048]{2,1,0:T(8,128)(2,1)}), bf16[8,16,2048]{2,1,0:T(8,128)(2,1)S(1)}, u32[]{:S(2)}, u32[]{:S(2)}) async-start(bf16[8,16,2048]{2,1,0:T(8,128)(2,1)} %sum_pieces.3), calls=%async_computation.4 | async-start | bytes 1048576 | tf_op jit(solution)/shard_map/all_to_all | solution.py:458
  167.3 5.3 %collective-permute-start.12 = (bf16[128,2048]{1,0:T(8,128)(2,1)S(1)}, bf16[128,2048]{1,0:T(8,128)(2,1)S(1)}, u32[]{:S(2)}, u32[]{:S(2)}) collective-permute-start(bf16[128,2048]{1,0:T(8,128)(2,1)S(1)} %bitcast.9), channel_id=1, source_target_pairs={{0,1},{1,0},{2,3},{3,2},{4,5},{5,4},{6,7},{7,6},{8,9},{9,8},{10,11... | collective-permute-start | bytes 1572872 | tf_op jit(solution)/shard_map/ppermute | solution.py:395
  (11 other events, 20.0 us)
